TPU v7x, 32 devices: a whole 2x2x4 slice. The times are simulated.
32 devices in a mesh: section: 2 (over core), seg: 4 (over z), tensor: 4 (over y, x).
Axes of the slice: x: 2, y: 2, z: 4, core: 2. Of those that a mesh axis runs over, the one named last changes fastest.
Arguments:
- inputs: bfloat16 [2, 1024, 768], P(None, 'seg'), may hold values from -6 to 6
- out_grad: bfloat16 [2, 1024, 768], P(None, 'seg'), may hold values from -6 to 6
- item_lengths: int32 [2, 4], replicated, may hold values from 0 to 4, as said below
- norm_gains: float32 [2, 2, 768], P('section'), may hold values from 0.1 to 1.9
- norm_biases: float32 [2, 2, 768], P('section'), may hold values from -4 to 4
- w_attn: bfloat16 [2, 3, 768, 768], P('section', None, None, 'tensor'), may hold values from -0.21875 to 0.21875
- attn_bias: float32 [2, 2, 768], P('section', None, 'tensor'), may hold values from -4 to 4
- w_out: bfloat16 [2, 768, 768], P('section', 'tensor'), may hold values from -2 to 2
- out_biases: float32 [2, 2, 768], P('section'), may hold values from -4 to 4
- w_fc: bfloat16 [2, 768, 3072], P('section', None, 'tensor'), may hold values from -0.21875 to 0.21875
- fc_bias: float32 [2, 3072], P('section', 'tensor'), may hold values from -4 to 4
- w_proj: bfloat16 [2, 3072, 768], P('section', 'tensor'), may hold values from -0.109375 to 0.109375
- w_mem_keys: bfloat16 [2, 2, 768, 384], P('section', None, None, 'tensor'), may hold values from -0.21875 to 0.21875
- w_mem_value: bfloat16 [2, 768, 768], P('section', None, 'tensor'), may hold values from -0.21875 to 0.21875
Outputs:
- input_grad: bfloat16 [2, 1024, 768], P('section', 'seg')
- norm_gains_grad: float32 [2, 2, 768], P('section')
- norm_biases_grad: float32 [2, 2, 768], P('section')
- w_attn_grad: float32 [2, 3, 768, 768], P('section', None, 'seg', 'tensor')
- attn_bias_grad: float32 [2, 2, 768], P('section', None, 'tensor')
- w_out_grad: float32 [2, 768, 768], P('section', 'tensor', 'seg')
- out_biases_grad: float32 [2, 2, 768], P('section')
- w_fc_grad: float32 [2, 768, 3072], P('section', 'seg', 'tensor')
- fc_bias_grad: float32 [2, 3072], P('section', 'tensor')
- w_proj_grad: float32 [2, 3072, 768], P('section', 'tensor', 'seg')
- w_mem_keys_grad: float32 [2, 2, 768, 384], P('section', None, 'seg', 'tensor')
- w_mem_value_grad: float32 [2, 768, 768], P('section', 'seg', 'tensor')
Inputs may be any that keep to these rules, and one draw needn't show every extreme that they name: `item_lengths`: each row lists item lengths in segments, nonzero ones first and zeros after them, summing to 4; in one row, drawn from the seed, a single item holds all 4 segments; in the other rows each item has 1 to 4 segments.
All inputs are finite; a program needn't handle non-finite values.
Results may differ from a plain program's by a relative error of at most 0.018.
Values may be sent and summed in bfloat16 or wider, within the bound.
A program may use at most 192 MiB of HBM per device.

v0:
```python
import jax
import jax.numpy as jnp
from jax import lax
from jax.sharding import PartitionSpec as P

HEAD_DIM = 64
NU = 3
MEM = 16


PRECISE = lax.Precision.HIGHEST
EPSILON = 1e-05


def shifted(shard, axis, by):
    peers = lax.axis_size(axis)
    return lax.ppermute(shard, axis, [(i, (i + by) % peers) for i in range(peers)])


def passed_along(shard, axis, by):
    peers = lax.axis_size(axis)
    pairs = [(i, i + by) for i in range(peers) if 0 <= i + by < peers]
    return lax.ppermute(shard, axis, pairs)


def matmul(left, right):
    return jnp.dot(left, right, precision=PRECISE)


def dot_plain(left, right):
    return jnp.dot(left, right, preferred_element_type=jnp.float32)


def dot_rows(left, right):
    return lax.dot_general(
        left, right, (((0,), (0,)), ((), ())), preferred_element_type=jnp.float32
    )


def dot_trans(left, right):
    return lax.dot_general(
        left, right, (((1,), (1,)), ((), ())), preferred_element_type=jnp.float32
    )


def layer_norm(hidden, scale_row, shift_row):
    row_mean = jnp.mean(hidden, axis=-1, keepdims=True)
    centered = hidden - row_mean
    variance = jnp.mean(centered * centered, axis=-1, keepdims=True)
    return centered * lax.rsqrt(variance + EPSILON) * scale_row + shift_row


def feature_map(projected):
    doubled = jnp.concatenate([jax.nn.softplus(projected), jax.nn.softplus(-projected)], axis=-1)
    return jnp.concatenate(
        [doubled * jnp.roll(doubled, shift_by, axis=-1) for shift_by in range(1, NU + 1)], axis=-1
    )


def item_starts(lengths):
    item_ends = jnp.cumsum(lengths, axis=-1)
    item_begins = item_ends - lengths
    places = jnp.arange(lengths.shape[-1], dtype=jnp.int32)
    matches = (item_begins[:, :, None] == places[None, None, :]) & (lengths[:, :, None] > 0)
    return jnp.sum(matches.astype(jnp.int32), axis=1)


def memory_read(memory, totals, phi_query):
    return matmul(phi_query, memory.T) / (matmul(phi_query, totals) + 1.0)[:, None]


def memory_update(memory, totals, phi_key, value_mem):
    recalled = memory_read(memory, totals, phi_key)
    return (memory + matmul((value_mem - recalled).T, phi_key), totals + jnp.sum(phi_key, axis=0))


def gelu_tanh(pre_activation):
    return jax.nn.gelu(pre_activation, approximate=True)


def other_section(payload):
    return shifted(payload, "section", 1)


def head_view(matrix):
    return matrix.reshape(matrix.shape[0], -1, HEAD_DIM)


def attention_scores(queries, key_heads):
    scores = jnp.einsum(
        "qhd,khd->hqk", head_view(queries), head_view(key_heads), preferred_element_type=jnp.float32
    ) * HEAD_DIM ** (-0.5)
    positions = jnp.arange(queries.shape[0])
    causal = positions[:, None] >= positions[None, :]
    return jnp.where(causal[None], scores, -jnp.inf)


def attend(queries, key_heads, values):
    scores = attention_scores(queries, key_heads)
    row_top = jnp.max(scores, axis=-1, keepdims=True)
    log_total = row_top + jnp.log(jnp.sum(jnp.exp(scores - row_top), axis=-1, keepdims=True))
    attention_probs = jnp.exp(scores - log_total).astype(jnp.bfloat16)
    mixed_heads = jnp.einsum(
        "hqk,khd->qhd", attention_probs, head_view(values), preferred_element_type=jnp.float32
    )
    return (mixed_heads.reshape(queries.shape[0], -1).astype(jnp.bfloat16), log_total)


def attend_back(queries, key_heads, values, log_total, mixed_grad):
    row_count = queries.shape[0]
    scores = attention_scores(queries, key_heads)
    probs_full = jnp.exp(scores - log_total)
    attention_probs = probs_full.astype(jnp.bfloat16)
    mixed_view = head_view(mixed_grad)
    probs_grad = jnp.einsum(
        "qhd,khd->hqk", mixed_view, head_view(values), preferred_element_type=jnp.float32
    )
    row_delta = jnp.sum(probs_grad * probs_full, axis=-1, keepdims=True)
    score_grad = (probs_full * (probs_grad - row_delta)).astype(jnp.bfloat16)
    query_grad = jnp.einsum(
        "hqk,khd->qhd", score_grad, head_view(key_heads), preferred_element_type=jnp.float32
    ) * HEAD_DIM ** (-0.5)
    key_grad = jnp.einsum(
        "hqk,qhd->khd", score_grad, head_view(queries), preferred_element_type=jnp.float32
    ) * HEAD_DIM ** (-0.5)
    value_grad = jnp.einsum(
        "hqk,qhd->khd", attention_probs, mixed_view, preferred_element_type=jnp.float32
    )
    return (
        query_grad.reshape(row_count, -1).astype(jnp.bfloat16),
        key_grad.reshape(row_count, -1).astype(jnp.bfloat16),
        value_grad.reshape(row_count, -1).astype(jnp.bfloat16),
    )


def chain_forward(phi_key, value_mem, flags_here):
    seg_index = lax.axis_index("seg")
    seg_count = lax.axis_size("seg")
    own_first = flags_here[seg_index] > 0
    empty_memory = jnp.zeros((value_mem.shape[1], phi_key.shape[1]), jnp.float32)
    empty_totals = jnp.zeros((phi_key.shape[1],), jnp.float32)

    def pass_state(step_index, carried):
        got_memory, got_totals = passed_along((carried[2], carried[3]), "seg", 1)
        got_memory = jnp.where(own_first, 0.0, got_memory)
        got_totals = jnp.where(own_first, 0.0, got_totals)
        sent_memory, sent_totals = memory_update(got_memory, got_totals, phi_key, value_mem)
        return (got_memory, got_totals, sent_memory, sent_totals)

    start_memory, start_totals = memory_update(empty_memory, empty_totals, phi_key, value_mem)
    carried = lax.fori_loop(
        0, seg_count - 1, pass_state, (empty_memory, empty_totals, start_memory, start_totals)
    )
    return (carried[0], carried[1])


def chain_backward(
    read_memory_grad, read_totals_grad, phi_key, value_mem, memory_in, totals_in, flags_here
):
    seg_index = lax.axis_index("seg")
    seg_count = lax.axis_size("seg")
    _, update_pull = jax.vjp(memory_update, memory_in, totals_in, phi_key, value_mem)
    next_first = flags_here[jnp.minimum(seg_index + 1, seg_count - 1)] > 0

    def pass_back(step_index, carried):
        got_memory, got_totals = passed_along((carried[0], carried[1]), "seg", -1)
        got_memory = jnp.where(next_first, 0.0, got_memory)
        got_totals = jnp.where(next_first, 0.0, got_totals)
        pulled = update_pull((got_memory, got_totals))
        return (read_memory_grad + pulled[0], read_totals_grad + pulled[1], got_memory, got_totals)

    start = (
        read_memory_grad,
        read_totals_grad,
        jnp.zeros_like(read_memory_grad),
        jnp.zeros_like(read_totals_grad),
    )
    carried = lax.fori_loop(0, seg_count - 1, pass_back, start)
    pulled = update_pull((carried[2], carried[3]))
    return (pulled[2], pulled[3])


def layer_forward(seg_rows, flags_here, params):
    (
        gains,
        shifts,
        w_attn,
        attn_bias,
        w_out,
        out_biases,
        w_fc,
        fc_bias,
        w_proj,
        w_mem_keys,
        w_mem_value,
    ) = params
    mem_rows = seg_rows[-MEM:]
    query_part = dot_plain(seg_rows, w_mem_keys[0]).astype(jnp.bfloat16)
    key_part = dot_plain(mem_rows, w_mem_keys[1]).astype(jnp.bfloat16)
    query_mem, key_mem = (
        lax.all_gather(query_part, "tensor", axis=1, tiled=True),
        lax.all_gather(key_part, "tensor", axis=1, tiled=True),
    )
    value_mem = dot_plain(mem_rows, w_mem_value)
    phi_key = feature_map(key_mem.astype(jnp.float32))
    memory_in, totals_in = chain_forward(phi_key, value_mem, flags_here)
    recall_part = memory_read(
        memory_in, totals_in, feature_map(query_mem.astype(jnp.float32))
    ).astype(jnp.bfloat16)
    recall_all = lax.all_gather(recall_part, "tensor", axis=1, tiled=True)
    hidden = seg_rows.astype(jnp.float32) + recall_all.astype(jnp.float32)
    normed = layer_norm(hidden, gains[0], shifts[0]).astype(jnp.bfloat16)
    queries = (dot_plain(normed, w_attn[0]) + attn_bias[0]).astype(jnp.bfloat16)
    key_heads = dot_plain(normed, w_attn[1]).astype(jnp.bfloat16)
    values = (dot_plain(normed, w_attn[2]) + attn_bias[1]).astype(jnp.bfloat16)
    mixed_heads, log_total = attend(queries, key_heads, values)
    after_attention = hidden + lax.psum(dot_plain(mixed_heads, w_out), "tensor") + out_biases[0]
    normed_mlp = layer_norm(after_attention, gains[1], shifts[1]).astype(jnp.bfloat16)
    pre_activation = dot_plain(normed_mlp, w_fc) + fc_bias
    activation = gelu_tanh(pre_activation).astype(jnp.bfloat16)
    output = after_attention + lax.psum(dot_plain(activation, w_proj), "tensor") + out_biases[1]
    kept = (
        seg_rows,
        query_mem,
        key_mem,
        value_mem,
        memory_in,
        totals_in,
        hidden,
        normed,
        queries,
        key_heads,
        values,
        mixed_heads,
        log_total,
        after_attention,
        normed_mlp,
        pre_activation,
        activation,
    )
    return (output, kept)


def layer_backward(grad_rows, kept, flags_here, params):
    (
        gains,
        shifts,
        w_attn,
        attn_bias,
        w_out,
        out_biases,
        w_fc,
        fc_bias,
        w_proj,
        w_mem_keys,
        w_mem_value,
    ) = params
    (
        seg_rows,
        query_mem,
        key_mem,
        value_mem,
        memory_in,
        totals_in,
        hidden,
        normed,
        queries,
        key_heads,
        values,
        mixed_heads,
        log_total,
        after_attention,
        normed_mlp,
        pre_activation,
        activation,
    ) = kept
    grad_low = grad_rows.astype(jnp.bfloat16)
    proj_grad = dot_rows(activation, grad_low)
    _, gelu_pull = jax.vjp(gelu_tanh, pre_activation)
    pre_grad = gelu_pull(dot_trans(grad_low, w_proj))[0].astype(jnp.bfloat16)
    fc_bias_grad = jnp.sum(pre_grad, axis=0, dtype=jnp.float32)
    fc_grad = dot_rows(normed_mlp, pre_grad)
    normed_mlp_grad = lax.psum(dot_trans(pre_grad, w_fc), "tensor")
    _, mlp_norm_pull = jax.vjp(layer_norm, after_attention, gains[1], shifts[1])
    after_part, gain_mlp, shift_mlp = mlp_norm_pull(normed_mlp_grad)
    after_grad = grad_rows + after_part
    after_low = after_grad.astype(jnp.bfloat16)
    out_weight_grad = dot_rows(mixed_heads, after_low)
    mixed_grad = dot_trans(after_low, w_out).astype(jnp.bfloat16)
    query_grad, key_grad, value_grad = attend_back(
        queries, key_heads, values, log_total, mixed_grad
    )
    attention_bias_grad = jnp.stack(
        [
            jnp.sum(query_grad, axis=0, dtype=jnp.float32),
            jnp.sum(value_grad, axis=0, dtype=jnp.float32),
        ]
    )
    attention_weight_grad = jnp.stack(
        [dot_rows(normed, query_grad), dot_rows(normed, key_grad), dot_rows(normed, value_grad)]
    )
    normed_part = (
        dot_trans(query_grad, w_attn[0])
        + dot_trans(key_grad, w_attn[1])
        + dot_trans(value_grad, w_attn[2])
    )
    normed_grad = lax.psum(normed_part, "tensor")
    _, attention_norm_pull = jax.vjp(layer_norm, hidden, gains[0], shifts[0])
    hidden_part, gain_attention, shift_attention = attention_norm_pull(normed_grad)
    hidden_grad = after_grad + hidden_part
    value_width = value_mem.shape[1]
    recall_grad = lax.dynamic_slice_in_dim(
        hidden_grad, lax.axis_index("tensor") * value_width, value_width, 1
    )
    phi_query, query_pull = jax.vjp(feature_map, query_mem.astype(jnp.float32))
    _, read_pull = jax.vjp(memory_read, memory_in, totals_in, phi_query)
    memory_grad, totals_grad, phi_query_grad = read_pull(recall_grad)
    phi_key, key_pull = jax.vjp(feature_map, key_mem.astype(jnp.float32))
    phi_key_grad, value_mem_grad = chain_backward(
        memory_grad, totals_grad, phi_key, value_mem, memory_in, totals_in, flags_here
    )
    query_full = query_pull(phi_query_grad)[0]
    key_full = key_pull(phi_key_grad)[0]
    query_own, key_own = (
        lax.psum_scatter(query_full, "tensor", scatter_dimension=1, tiled=True),
        lax.psum_scatter(key_full, "tensor", scatter_dimension=1, tiled=True),
    )
    query_own = query_own.astype(jnp.bfloat16)
    key_own = key_own.astype(jnp.bfloat16)
    value_low = value_mem_grad.astype(jnp.bfloat16)
    mem_rows = seg_rows[-MEM:]
    mem_keys_grad = jnp.stack([dot_rows(seg_rows, query_own), dot_rows(mem_rows, key_own)])
    mem_value_grad = dot_rows(mem_rows, value_low)
    tail_part = dot_trans(key_own, w_mem_keys[1]) + dot_trans(value_low, w_mem_value)
    input_part = dot_trans(query_own, w_mem_keys[0])
    input_part = jnp.concatenate([input_part[:-MEM], input_part[-MEM:] + tail_part], axis=0)
    rows_grad = hidden_grad + lax.psum(input_part, "tensor")
    gain_grads = jnp.stack([gain_attention, gain_mlp])
    shift_grads = jnp.stack([shift_attention, shift_mlp])
    out_bias_grads = jnp.stack([jnp.sum(after_grad, axis=0), jnp.sum(grad_rows, axis=0)])
    grads = (
        gain_grads,
        shift_grads,
        attention_weight_grad,
        attention_bias_grad,
        out_weight_grad,
        out_bias_grads,
        fc_grad,
        fc_bias_grad,
        proj_grad,
        mem_keys_grad,
        mem_value_grad,
    )
    return (rows_grad, grads)


def per_device(
    inputs,
    out_grad,
    item_lengths,
    norm_gains,
    norm_biases,
    w_attn,
    attn_bias,
    w_out,
    out_biases,
    w_fc,
    fc_bias,
    w_proj,
    w_mem_keys,
    w_mem_value,
):
    params = tuple(
        (
            weight[0]
            for weight in (
                norm_gains,
                norm_biases,
                w_attn,
                attn_bias,
                w_out,
                out_biases,
                w_fc,
                fc_bias,
                w_proj,
                w_mem_keys,
                w_mem_value,
            )
        )
    )
    first_flags = item_starts(item_lengths)
    section_index = lax.axis_index("section")
    micro_count = inputs.shape[0]
    tick_count = micro_count + 1
    arriving = jnp.zeros(inputs.shape[1:], jnp.bfloat16)
    saved = []
    for tick_index in range(tick_count):
        micro_index = jnp.clip(tick_index - section_index, 0, micro_count - 1)
        seg_rows = jnp.where(section_index == 0, inputs[min(tick_index, micro_count - 1)], arriving)
        output, kept = layer_forward(seg_rows, first_flags[micro_index], params)
        saved.append(kept)
        if tick_index + 1 < tick_count:
            arriving = other_section(output.astype(jnp.bfloat16))
    arriving = jnp.zeros(inputs.shape[1:], jnp.bfloat16)
    own_input = arriving
    summed = None
    for tick_index in range(tick_count):
        micro_place = tick_index - 1 + section_index
        micro_index = jnp.clip(micro_place, 0, micro_count - 1)
        active = (micro_place >= 0) & (micro_place < micro_count)
        kept = jax.tree.map(
            lambda early, late: jnp.where(section_index == 0, early, late),
            saved[max(tick_index - 1, 0)],
            saved[min(tick_index + 1, tick_count - 1)],
        )
        grad_rows = jnp.where(
            section_index == 0,
            arriving.astype(jnp.float32),
            out_grad[min(tick_index, micro_count - 1)].astype(jnp.float32),
        )
        rows_grad, grads = layer_backward(grad_rows, kept, first_flags[micro_index], params)
        grads = tuple((jnp.where(active, part_grad, 0.0) for part_grad in grads))
        summed = (
            grads if summed is None else tuple((left + right for left, right in zip(summed, grads)))
        )
        sending = rows_grad.astype(jnp.bfloat16)
        if tick_index == 1:
            own_input = sending
        arriving = other_section(sending)
    input_grad = jnp.where(section_index == 0, own_input, arriving)[None]
    (
        gain_grads,
        shift_grads,
        attention_grads,
        abias_grads,
        out_grads,
        obias_grads,
        fc_grads,
        fcb_grads,
        proj_grads,
        mkey_grads,
        mvalue_grads,
    ) = summed
    attention_grads, out_grads, fc_grads, proj_grads, mkey_grads, mvalue_grads = (
        lax.psum_scatter(attention_grads[None], "seg", scatter_dimension=2, tiled=True),
        lax.psum_scatter(out_grads[None], "seg", scatter_dimension=2, tiled=True),
        lax.psum_scatter(fc_grads[None], "seg", scatter_dimension=1, tiled=True),
        lax.psum_scatter(proj_grads[None], "seg", scatter_dimension=2, tiled=True),
        lax.psum_scatter(mkey_grads[None], "seg", scatter_dimension=2, tiled=True),
        lax.psum_scatter(mvalue_grads[None], "seg", scatter_dimension=1, tiled=True),
    )
    gain_grads, shift_grads, abias_grads, obias_grads, fcb_grads = lax.psum(
        (
            gain_grads[None],
            shift_grads[None],
            abias_grads[None],
            obias_grads[None],
            fcb_grads[None],
        ),
        "seg",
    )
    return (
        input_grad,
        gain_grads,
        shift_grads,
        attention_grads,
        abias_grads,
        out_grads,
        obias_grads,
        fc_grads,
        fcb_grads,
        proj_grads,
        mkey_grads,
        mvalue_grads,
    )


def solution(mesh):
    return jax.shard_map(
        per_device,
        mesh=mesh,
        in_specs=(
            P(None, "seg", None),
            P(None, "seg", None),
            P(),
            P("section", None, None),
            P("section", None, None),
            P("section", None, None, "tensor"),
            P("section", None, "tensor"),
            P("section", "tensor", None),
            P("section", None, None),
            P("section", None, "tensor"),
            P("section", "tensor"),
            P("section", "tensor", None),
            P("section", None, None, "tensor"),
            P("section", None, "tensor"),
        ),
        out_specs=(
            P("section", "seg", None),
            P("section", None, None),
            P("section", None, None),
            P("section", None, "seg", "tensor"),
            P("section", None, "tensor"),
            P("section", "tensor", "seg"),
            P("section", None, None),
            P("section", "seg", "tensor"),
            P("section", "tensor"),
            P("section", "tensor", "seg"),
            P("section", None, "seg", "tensor"),
            P("section", "seg", "tensor"),
        ),
        check_vma=False,
    )
```

profile of v0, /device:TPU:0, one launch (start us, length us, event | category | flops | bytes accessed | tf_op | source)
XLA Modules:
  0.0 2270.0 jit_solution(18246418338239009621)
XLA Ops:
  40.8 130.2 %while.99 = (s32[]{:T(128)}, f32[192,2304]{1,0:T(8,128)}, f32[2304]{0:T(1024)}, f32[192,2304]{1,0:T(8,128)}, f32[2304]{0:T(1024)S(1)}, /*index=5*/pred[]{:T(512)...) while((s32[]{:T(128)}, f32[192,2304]{1,0:T(8,128)}, f32[2304]{0:T(1024)}, ...), condition=%wide.region_4.5_spmd, body=%wide.region_3.4_spmd.sunk | while | flops 171207184 | bytes 23620972 | solution.py:151
  194.0 51.2 %all-reduce.54.cloned.1.call-done = f32[256,768]{1,0:T(8,128)} async-done(((f32[256,768]{1,0:T(8,128)}), f32[256,768]{1,0:T(8,128)}) %all-reduce.54.cloned.1.call-update) | async-done | bytes 786448 | tf_op jit(solution)/shard_map/psum | solution.py:217
  250.2 48.8 %all-reduce.56.cloned.1.call-done = f32[256,768]{1,0:T(8,128)} async-done(((f32[256,768]{1,0:T(8,128)}), f32[256,768]{1,0:T(8,128)}) %all-reduce.56.cloned.1.call-update) | async-done | bytes 786448 | tf_op jit(solution)/shard_map/psum | solution.py:221
  336.8 135.9 %while.100 = (s32[]{:T(128)}, f32[192,2304]{1,0:T(8,128)}, f32[2304]{0:T(1024)}, f32[192,2304]{1,0:T(8,128)}, f32[2304]{0:T(1024)}, /*index=5*/pred[]{:T(512)}, ...) while((s32[]{:T(128)}, f32[192,2304]{1,0:T(8,128)}, f32[2304]{0:T(1024)}, ...), condition=%wide.region_15.16_spmd, body=%wide.region_14.15_spmd.sunk | while | flops 171207184 | bytes 23731648 | solution.py:151
  505.6 49.0 %all-reduce.58.cloned.1.call-done = f32[256,768]{1,0:T(8,128)} async-done(((f32[256,768]{1,0:T(8,128)}), f32[256,768]{1,0:T(8,128)}) %all-reduce.58.cloned.1.call-update) | async-done | bytes 786448 | tf_op jit(solution)/shard_map/psum | solution.py:217
  570.1 44.4 %all-reduce.60.cloned.1.call-done = f32[256,768]{1,0:T(8,128)} async-done(((f32[256,768]{1,0:T(8,128)}), f32[256,768]{1,0:T(8,128)}) %all-reduce.60.cloned.1.call-update) | async-done | bytes 786448 | tf_op jit(solution)/shard_map/psum | solution.py:283
  624.3 61.2 %all-reduce.78.cloned.1.call-done = (f32[256,768]{1,0:T(8,128)}, f32[256,768]{1,0:T(8,128)}) async-done(((f32[256,768]{1,0:T(8,128)}, f32[256,768]{1,0:T(8,128)}), (f32[256,768]{1,0:T(8,128)}, f32[256,768]{1,0:T(8,128)})) %all-reduce.78.cloned.1.call-update) | async-done | bytes 1572880 | tf_op jit(solution)/shard_map/psum | solution.py:221
  725.7 134.9 %while.102 = (s32[]{:T(128)}, f32[192,2304]{1,0:T(8,128)}, f32[2304]{0:T(1024)}, f32[192,2304]{1,0:T(8,128)}, f32[2304]{0:T(1024)}, /*index=5*/pred[]{:T(512)}, ...) while((s32[]{:T(128)}, f32[192,2304]{1,0:T(8,128)}, f32[2304]{0:T(1024)}, ...), condition=%wide.region_45.48_spmd, body=%wide.region_44.47_spmd.sunk | while | flops 171207184 | bytes 23694756 | solution.py:151
  923.6 126.2 %while.101 = (s32[]{:T(128)}, f32[192,2304]{1,0:T(8,128)}, f32[2304]{0:T(1024)S(1)}, f32[192,2304]{1,0:T(8,128)}, f32[2304]{0:T(1024)}, /*index=5*/pred[]{:T(512...) while((s32[]{:T(128)}, f32[192,2304]{1,0:T(8,128)}, ...), condition=%wide.region_38.41_spmd, body=%wide.region_36.40_spmd.sunk | while | flops 171661056 | bytes 25344488 | solution.py:178
  1138.3 50.5 %all-reduce.76.cloned.1.call-done = (f32[256,768]{1,0:T(8,128)}, f32[256,768]{1,0:T(8,128)}) async-done(((f32[256,768]{1,0:T(8,128)}, f32[256,768]{1,0:T(8,128)}), (f32[256,768]{1,0:T(8,128)}, f32[256,768]{1,0:T(8,128)})) %all-reduce.76.cloned.1.call-update) | async-done | bytes 1572880 | tf_op jit(solution)/shard_map/psum | solution.py:217
  1201.7 48.1 %all-reduce.62.cloned.1.call-done = f32[256,768]{1,0:T(8,128)} async-done(((f32[256,768]{1,0:T(8,128)}), f32[256,768]{1,0:T(8,128)}) %all-reduce.62.cloned.1.call-update) | async-done | bytes 786448 | tf_op jit(solution)/shard_map/psum | solution.py:283
  1262.9 44.5 %all-reduce.64.cloned.1.call-done = f32[256,768]{1,0:T(8,128)} async-done(((f32[256,768]{1,0:T(8,128)}), f32[256,768]{1,0:T(8,128)}) %all-reduce.64.cloned.1.call-update) | async-done | bytes 786448 | tf_op jit(solution)/shard_map/psum | solution.py:307
  1327.9 146.2 %while.103 = (s32[]{:T(128)}, f32[192,2304]{1,0:T(8,128)}, f32[2304]{0:T(1024)S(1)}, f32[192,2304]{1,0:T(8,128)}, f32[2304]{0:T(1024)}, /*index=5*/pred[]{:T(512...) while((s32[]{:T(128)}, f32[192,2304]{1,0:T(8,128)}, ...), condition=%wide.region_68.71_spmd, body=%wide.region_66.70_spmd.sunk | while | flops 171661056 | bytes 25344488 | solution.py:178
  1330.7 40.0 %collective-permute-done.8 = f32[192,2304]{1,0:T(8,128)} collective-permute-done((f32[192,2304]{1,0:T(8,128)}, f32[192,2304]{1,0:T(8,128)}, u32[]{:S(2)}, u32[]{:S(2)}) %collective-permute-start.8) | collective-permute-done | bytes 1769504 | tf_op jit(solution)/shard_map/while/body/eval_jaxpr/ppermute | solution.py:23
  1380.4 39.0 %collective-permute-done.8 = f32[192,2304]{1,0:T(8,128)} collective-permute-done((f32[192,2304]{1,0:T(8,128)}, f32[192,2304]{1,0:T(8,128)}, u32[]{:S(2)}, u32[]{:S(2)}) %collective-permute-start.8) | collective-permute-done | bytes 1769504 | tf_op jit(solution)/shard_map/while/body/eval_jaxpr/ppermute | solution.py:23
  1551.4 43.1 %all-reduce.66.cloned.1.call-done = f32[256,768]{1,0:T(8,128)} async-done(((f32[256,768]{1,0:T(8,128)}), f32[256,768]{1,0:T(8,128)}) %all-reduce.66.cloned.1.call-update) | async-done | bytes 786448 | tf_op jit(solution)/shard_map/psum | solution.py:337
  1604.8 46.5 %all-reduce.68.cloned.1.call-done = f32[256,768]{1,0:T(8,128)} async-done(((f32[256,768]{1,0:T(8,128)}), f32[256,768]{1,0:T(8,128)}) %all-reduce.68.cloned.1.call-update) | async-done | bytes 786448 | tf_op jit(solution)/shard_map/psum | solution.py:283
  1664.0 46.9 %all-reduce.70.cloned.1.call-done = f32[256,768]{1,0:T(8,128)} async-done(((f32[256,768]{1,0:T(8,128)}), f32[256,768]{1,0:T(8,128)}) %all-reduce.70.cloned.1.call-update) | async-done | bytes 786448 | tf_op jit(solution)/shard_map/psum | solution.py:307
  1730.7 146.1 %while.104 = (s32[]{:T(128)}, f32[192,2304]{1,0:T(8,128)}, f32[2304]{0:T(1024)S(1)}, f32[192,2304]{1,0:T(8,128)}, f32[2304]{0:T(1024)}, /*index=5*/pred[]{:T(512...) while((s32[]{:T(128)}, f32[192,2304]{1,0:T(8,128)}, ...), condition=%wide.region_87.90_spmd, body=%wide.region_85.89_spmd.sunk | while | flops 171661056 | bytes 25344488 | solution.py:178
  1733.5 40.0 %collective-permute-done.10 = f32[192,2304]{1,0:T(8,128)} collective-permute-done((f32[192,2304]{1,0:T(8,128)}, f32[192,2304]{1,0:T(8,128)}, u32[]{:S(2)}, u32[]{:S(2)}) %collective-permute-start.10) | collective-permute-done | bytes 1769504 | tf_op jit(solution)/shard_map/while/body/eval_jaxpr/ppermute | solution.py:23
  1783.2 39.0 %collective-permute-done.10 = f32[192,2304]{1,0:T(8,128)} collective-permute-done((f32[192,2304]{1,0:T(8,128)}, f32[192,2304]{1,0:T(8,128)}, u32[]{:S(2)}, u32[]{:S(2)}) %collective-permute-start.10) | collective-permute-done | bytes 1769504 | tf_op jit(solution)/shard_map/while/body/eval_jaxpr/ppermute | solution.py:23
  2024.9 95.3 %all-reduce.74.cloned.1.call-done = f32[1,768,768]{1,0,2:T(1,128)} async-done(((f32[1,768,768]{1,0,2:T(1,128)}), f32[1,768,768]{1,0,2:T(1,128)}) %all-reduce.74.cloned.1.call-update) | async-done | bytes 2359312
  2172.4 40.5 %reduce-scatter.40.cloned.1.call-done = f32[192,576]{1,0:T(8,128)} async-done(((f32[768,576]{1,0:T(8,128)}), f32[192,576]{1,0:T(8,128)}) %reduce-scatter.40.cloned.1.call-update) | async-done | bytes 442384
  2215.2 47.8 %reduce-scatter.32.cloned.1.call-done = f32[1,192,768]{2,1,0:T(8,128)} async-done(((f32[1,768,768]{2,1,0:T(8,128)}), f32[1,192,768]{2,1,0:T(8,128)}) %reduce-scatter.32.cloned.1.call-update) | async-done | bytes 589840 | tf_op jit(solution)/shard_map/reduce_scatter | solution.py:447
  (1766 shorter events, 1367.6 us)
Async XLA Ops:
  7.2 238.0 %all-reduce.54.cloned.1.call-start = ((), (), s32[]{:S(2)}) async-start(), calls=%async_computation.11 | async-start | bytes 1572864 | tf_op jit(solution)/shard_map/psum | solution.py:217
  193.9 105.1 %all-reduce.56.cloned.1.call-start = ((), (), s32[]{:S(2)}) async-start(), calls=%async_computation.12 | async-start | bytes 1572864 | tf_op jit(solution)/shard_map/psum | solution.py:221
  250.1 304.5 %all-reduce.58.cloned.1.call-start = ((), (), s32[]{:S(2)}) async-start(), calls=%async_computation.13 | async-start | bytes 1572864 | tf_op jit(solution)/shard_map/psum | solution.py:217
  503.1 111.4 %all-reduce.60.cloned.1.call-start = ((), (), s32[]{:S(2)}) async-start(), calls=%async_computation.14 | async-start | bytes 1572864 | tf_op jit(solution)/shard_map/psum | solution.py:283
  565.7 119.8 %all-reduce.78.cloned.1.call-start = ((), (), s32[]{:S(2)}) async-start(), calls=%async_computation.34 | async-start | bytes 3145728 | tf_op jit(solution)/shard_map/psum | solution.py:221
  624.3 471.9 %reduce-scatter.34.cloned.1.call-start = ((), (), s32[]{:S(2)}) async-start(), calls=%async_computation.25 | async-start | bytes 245760
  1073.3 50.9 %reduce-scatter.26.cloned.1.call-start = ((), (), s32[]{:S(2)}) async-start(), calls=%async_computation.15 | async-start | bytes 491520 | tf_op jit(solution)/shard_map/reduce_scatter | solution.py:325
  1081.5 107.2 %all-reduce.76.cloned.1.call-start = ((), (), s32[]{:S(2)}) async-start(), calls=%async_computation.33 | async-start | bytes 3145728 | tf_op jit(solution)/shard_map/psum | solution.py:217
  1126.7 123.2 %all-reduce.62.cloned.1.call-start = ((), (), s32[]{:S(2)}) async-start(), calls=%async_computation.16 | async-start | bytes 1572864 | tf_op jit(solution)/shard_map/psum | solution.py:283
  1200.9 106.6 %all-reduce.64.cloned.1.call-start = ((), (), s32[]{:S(2)}) async-start(), calls=%async_computation.17 | async-start | bytes 1572864 | tf_op jit(solution)/shard_map/psum | solution.py:307
  1258.6 256.4 %reduce-scatter.36.cloned.1.call-start = ((), (), s32[]{:S(2)}) async-start(), calls=%async_computation.26 | async-start | bytes 245760
  1497.3 97.2 %all-reduce.66.cloned.1.call-start = ((), (), s32[]{:S(2)}) async-start(), calls=%async_computation.19 | async-start | bytes 1572864 | tf_op jit(solution)/shard_map/psum | solution.py:337
  1545.1 106.2 %all-reduce.68.cloned.1.call-start = ((), (), s32[]{:S(2)}) async-start(), calls=%async_computation.20 | async-start | bytes 1572864 | tf_op jit(solution)/shard_map/psum | solution.py:283
  1602.4 108.4 %all-reduce.70.cloned.1.call-start = ((), (), s32[]{:S(2)}) async-start(), calls=%async_computation.21 | async-start | bytes 1572864 | tf_op jit(solution)/shard_map/psum | solution.py:307
  1662.0 255.1 %reduce-scatter.38.cloned.1.call-start = ((), (), s32[]{:S(2)}) async-start(), calls=%async_computation.27 | async-start | bytes 245760
  1894.6 50.4 %reduce-scatter.30.cloned.1.call-start = ((), (), s32[]{:S(2)}) async-start(), calls=%async_computation.22 | async-start | bytes 491520 | tf_op jit(solution)/shard_map/reduce_scatter | solution.py:325
  1899.4 100.8 %all-reduce.72.cloned.1.call-start = ((), (), s32[]{:S(2)}) async-start(), calls=%async_computation.23 | async-start | bytes 1572864 | tf_op jit(solution)/shard_map/psum | solution.py:337
  1947.4 75.7 %reduce-scatter.42.cloned.1.call-start = ((), (), s32[]{:S(2)}) async-start(), calls=%async_computation.29 | async-start | bytes 983040
  1953.8 166.5 %all-reduce.74.cloned.1.call-start = ((), (), s32[]{:S(2)}) async-start(), calls=%async_computation.32 | async-start | bytes 4718592
  1966.8 178.1 %reduce-scatter.46.cloned.1.call-start = ((), (), s32[]{:S(2)}) async-start(), calls=%async_computation.31 | async-start | bytes 983040
  1972.2 197.6 %reduce-scatter.44.cloned.1.call-start = ((), (), s32[]{:S(2)}) async-start(), calls=%async_computation.30 | async-start | bytes 983040
  1980.0 232.9 %reduce-scatter.40.cloned.1.call-start = ((), (), s32[]{:S(2)}) async-start(), calls=%async_computation.28 | async-start | bytes 2457600
  1990.5 272.5 %reduce-scatter.32.cloned.1.call-start = ((), (), s32[]{:S(2)}) async-start(), calls=%async_computation.24 | async-start | bytes 2949120 | tf_op jit(solution)/shard_map/reduce_scatter | solution.py:447
  2001.4 170.2 %collective-permute-start.16 = (bf16[256,768]{1,0:T(8,128)(2,1)S(1)}, bf16[256,768]{1,0:T(8,128)(2,1)S(1)}, u32[]{:S(2)}, u32[]{:S(2)}) collective-permute-start(bf16[256,768]{1,0:T(8,128)(2,1)S(1)} %add_convert_fusion), channel_id=1, source_target_pairs={{0,16},{16,0},{1,17},{17,1},{2,18},{18,2},{3,19},{19,3},{4,20},{20... | collective-permute-start | bytes 1179656 | tf_op jit(solution)/shard_map/ppermute | solution.py:17
  (536 other events, 7960.8 us)
Sparse Core Ops, SparseCore 0:
  194.0 51.2 all-reduce.53
  250.2 48.7 all-reduce.55
  503.2 51.2 all-reduce.57
  565.8 48.7 all-reduce.59
  624.4 61.0 all-reduce.77
  1073.4 22.7 reduce-scatter.33
  1099.8 24.3 reduce-scatter.25
  1127.6 61.0 all-reduce.75
  1201.0 48.8 all-reduce.61
  1258.7 48.7 all-reduce.63
  1492.6 22.2 reduce-scatter.35
  1518.2 24.3 reduce-scatter.27
  1545.7 48.8 all-reduce.65
  1602.5 48.7 all-reduce.67
  1662.1 48.7 all-reduce.69
  1894.7 22.2 reduce-scatter.37
  1920.5 24.4 reduce-scatter.29
  1948.2 48.7 all-reduce.71
  1999.2 23.7 reduce-scatter.41
  2025.3 94.9 all-reduce.73
  2122.6 22.3 reduce-scatter.45
  2147.2 22.5 reduce-scatter.43
  2172.2 40.6 reduce-scatter.39
  2215.6 47.2 reduce-scatter.31
where the time goes:
time: 2280 us; the launch traced here: 2270 us
  waiting for transfers between devices  1480 us (65%)
  matrix products  263 us (12%)
  other arithmetic  166 us (7%)
  local copies, waits for them, and re-layouts  120 us (5%)
  starting transfers between devices  107 us (5%)
  blocking collectives  105 us (5%)
  between operations  25.2 us (1%)
    ppermute x36, waiting for transfers between devices, passed_along(): return lax.ppermute(shard, axis, pairs)  602 us
    unnamed x32, waiting for transfers between devices  219 us
    dot_general x99, matrix products, matmul(): return jnp.dot(left, right, precision=PRECISE)  181 us
    psum x3, waiting for transfers between devices, layer_forward(): lax.psum(dot_plain(mixed_heads, w_out), 'tensor')  151 us
    psum x3, waiting for transfers between devices, layer_backward(): normed_mlp_grad = lax.psum(dot_trans(pre_grad, w_fc), 'tensor')  139 us
    psum x2, waiting for transfers between devices, layer_forward(): lax.psum(dot_plain(activation, w_proj), 'tensor')  110 us
    ppermute x36, starting transfers between devices, passed_along(): return lax.ppermute(shard, axis, pairs)  103 us
    psum x2, waiting for transfers between devices, layer_backward(): normed_grad = lax.psum(normed_part, 'tensor')  91.4 us
  transfers between devices with their start and end apart: 65, of which 42 were waited for; matrix products, arithmetic and copies ran while one was open for 8% of the time, Pallas kernels for 0%

commit v1 on v0

v1 whole, which is shorter than its diff:
```python
import jax
import jax.numpy as jnp
from jax import lax
from jax.sharding import PartitionSpec as P

HEAD_DIM = 64
NU = 3
MEM = 16
EPSILON = 1e-05
F32 = jnp.float32
BF16 = jnp.bfloat16
GELU_A = 0.7978845608028654
GELU_B = 0.044715


def dot_nn(left, right):
    return lax.dot_general(left, right, (((1,), (0,)), ((), ())), preferred_element_type=F32)


def dot_nt(left, right):
    return lax.dot_general(left, right, (((1,), (1,)), ((), ())), preferred_element_type=F32)


def dot_tn(left, right):
    return lax.dot_general(left, right, (((0,), (0,)), ((), ())), preferred_element_type=F32)


def roll_lanes(values, by):
    return jnp.roll(values, by, axis=1)


def doubled_softplus(projected):
    tail = jnp.log1p(jnp.exp(-jnp.abs(projected)))
    return jnp.concatenate(
        [jnp.maximum(projected, 0.0) + tail, jnp.maximum(-projected, 0.0) + tail], axis=1
    )


def feature_map(projected):
    doubled = doubled_softplus(projected)
    return jnp.concatenate([doubled * roll_lanes(doubled, j) for j in range(1, NU + 1)], axis=1)


def feature_map_back(projected, phi_grad):
    doubled = doubled_softplus(projected)
    width = doubled.shape[1]
    total = jnp.zeros_like(doubled)
    for j in range(1, NU + 1):
        part = phi_grad[:, (j - 1) * width : j * width]
        total = total + part * roll_lanes(doubled, j) + roll_lanes(part * doubled, width - j)
    half = width // 2
    gate = 1.0 / (1.0 + jnp.exp(-projected))
    return total[:, :half] * gate - total[:, half:] * (1.0 - gate)


def norm_rows(hidden):
    centered = hidden - jnp.mean(hidden, axis=1, keepdims=True)
    scale = lax.rsqrt(jnp.mean(centered * centered, axis=1, keepdims=True) + EPSILON)
    return centered * scale, scale


def norm_back(hidden, gain_row, grad):
    unit, scale = norm_rows(hidden)
    unit_grad = grad * gain_row
    mean_grad = jnp.mean(unit_grad, axis=1, keepdims=True)
    mean_both = jnp.mean(unit_grad * unit, axis=1, keepdims=True)
    return (
        scale * (unit_grad - mean_grad - unit * mean_both),
        jnp.sum(grad * unit, axis=0, keepdims=True),
        jnp.sum(grad, axis=0, keepdims=True),
    )


def gelu_and_slope(pre):
    square = pre * pre
    bent = jnp.tanh(GELU_A * (pre + GELU_B * square * pre))
    value = 0.5 * pre * (1.0 + bent)
    slope = 0.5 * (1.0 + bent) + 0.5 * pre * (1.0 - bent * bent) * (
        GELU_A * (1.0 + 3.0 * GELU_B * square)
    )
    return value, slope


def item_ids(lengths):
    item_ends = jnp.cumsum(lengths, axis=-1)
    item_begins = item_ends - lengths
    places = jnp.arange(lengths.shape[-1], dtype=jnp.int32)
    matches = (item_begins[:, :, None] == places[None, None, :]) & (lengths[:, :, None] > 0)
    return jnp.cumsum(jnp.sum(matches.astype(jnp.int32), axis=1), axis=-1)


def reach_mask(lengths):
    ids = item_ids(lengths)
    places = jnp.arange(lengths.shape[-1])
    earlier = places[:, None] > places[None, :]
    same = (ids[:, :, None] == ids[:, None, :]) & earlier[None]
    return jnp.repeat(jnp.repeat(same.astype(F32), MEM, axis=1), MEM, axis=2)


def gather_rows(values, axis):
    return lax.all_gather(values, axis, axis=0, tiled=True)


def scatter_rows(values, axis):
    peers = lax.axis_size(axis)
    pieces = values.astype(BF16).reshape(peers, values.shape[0] // peers, values.shape[1])
    got = lax.all_to_all(pieces, axis, 0, 0, tiled=True)
    return jnp.sum(got.astype(F32), axis=0)


def scatter_columns(values, axis):
    peers = lax.axis_size(axis)
    rows = values.shape[0]
    pieces = values.reshape(rows, peers, -1).transpose(1, 0, 2)
    got = lax.all_to_all(pieces.astype(BF16), axis, 0, 0, tiled=True)
    return jnp.sum(got.astype(F32), axis=0)


def solve_forward(key_dots, key_den, value_mem):
    segments = key_dots.shape[0] // MEM
    solved = value_mem
    for s in range(1, segments):
        rows = slice(s * MEM, (s + 1) * MEM)
        read = dot_nn(key_dots[rows].astype(BF16), solved.astype(BF16)) / key_den[rows]
        solved = solved.at[rows].add(-read)
    return solved


def solve_backward(key_dots, key_den, direct):
    segments = key_dots.shape[0] // MEM
    total = direct
    for s in range(segments - 1, 0, -1):
        rows = slice(s * MEM, (s + 1) * MEM)
        back = -total[rows] / key_den[rows]
        total = total + dot_tn(key_dots[rows].astype(BF16), back.astype(BF16))
    return total


def layer_forward(own_rows, mem_rows, mask, place, params):
    gains, shifts, w_attn, attn_bias, w_out, out_biases, w_fc, fc_bias, w_proj, w_q, w_k, w_v = params
    seg, _ = place
    own_mask = lax.dynamic_slice_in_dim(mask, seg * MEM, 1, 0)
    key_mem = dot_nn(mem_rows, w_k).astype(BF16)
    phi_key = feature_map(key_mem.astype(F32)).astype(BF16)
    key_dots = dot_nt(phi_key, phi_key) * mask
    key_den = 1.0 + jnp.sum(key_dots, axis=1, keepdims=True)
    value_part = dot_nn(mem_rows, w_v)
    solved_part = solve_forward(key_dots, key_den, value_part)
    solved = lax.all_gather(solved_part.astype(BF16), "tensor", axis=1, tiled=True)
    query_mem = dot_nn(own_rows, w_q).astype(BF16)
    phi_query = feature_map(query_mem.astype(F32)).astype(BF16)
    query_dots = dot_nt(phi_query, phi_key) * own_mask
    query_den = 1.0 + jnp.sum(query_dots, axis=1, keepdims=True)
    recall = dot_nn(query_dots.astype(BF16), solved) / query_den
    hidden = own_rows.astype(F32) + recall.astype(BF16).astype(F32)
    unit, _ = norm_rows(hidden)
    normed = gather_rows((unit * gains[0] + shifts[0]).astype(BF16), "tensor")
    queries = (dot_nn(normed, w_attn[0]) + attn_bias[0]).astype(BF16)
    key_heads = dot_nn(normed, w_attn[1]).astype(BF16)
    values = (dot_nn(normed, w_attn[2]) + attn_bias[1]).astype(BF16)
    rows = normed.shape[0]
    causal = jnp.arange(rows)[:, None] >= jnp.arange(rows)[None, :]
    probs, mixed = [], []
    for h in range(queries.shape[1] // HEAD_DIM):
        cols = slice(h * HEAD_DIM, (h + 1) * HEAD_DIM)
        scores = dot_nt(queries[:, cols], key_heads[:, cols]) * HEAD_DIM ** (-0.5)
        scores = jnp.where(causal, scores, -jnp.inf)
        heights = jnp.exp(scores - jnp.max(scores, axis=1, keepdims=True))
        probs.append(heights / jnp.sum(heights, axis=1, keepdims=True))
        mixed.append(dot_nn(probs[-1].astype(BF16), values[:, cols]).astype(BF16))
    mixed = jnp.concatenate(mixed, axis=1)
    after = hidden + scatter_rows(dot_nn(mixed, w_out), "tensor") + out_biases[0]
    unit, _ = norm_rows(after)
    normed_mlp = gather_rows((unit * gains[1] + shifts[1]).astype(BF16), "tensor")
    pre = dot_nn(normed_mlp, w_fc) + fc_bias
    activation, slope = gelu_and_slope(pre)
    activation = activation.astype(BF16)
    output = after + scatter_rows(dot_nn(activation, w_proj), "tensor") + out_biases[1]
    kept = (
        own_rows, mem_rows, key_mem, phi_key, key_dots, key_den, value_part, solved_part, solved, query_mem,
        phi_query, query_dots, query_den, recall, hidden, normed, queries, key_heads, values, probs, mixed,
        after, normed_mlp, slope, activation,
    )
    return output, kept


def layer_backward(own_grad, kept, mask, place, params):
    gains, shifts, w_attn, attn_bias, w_out, out_biases, w_fc, fc_bias, w_proj, w_q, w_k, w_v = params
    (
        own_rows, mem_rows, key_mem, phi_key, key_dots, key_den, value_part, solved_part, solved, query_mem,
        phi_query, query_dots, query_den, recall, hidden, normed, queries, key_heads, values, probs, mixed,
        after, normed_mlp, slope, activation,
    ) = kept
    seg, part = place
    own_mask = lax.dynamic_slice_in_dim(mask, seg * MEM, 1, 0)
    grad_low = gather_rows(own_grad.astype(BF16), "tensor")
    pre_grad = (slope * dot_nt(grad_low, w_proj)).astype(BF16)
    proj_grad = dot_tn(activation, grad_low)
    fc_bias_grad = jnp.sum(pre_grad.astype(F32), axis=0)
    fc_grad = dot_tn(normed_mlp, pre_grad)
    after_part, gain_mlp, shift_mlp = norm_back(
        after, gains[1:2], scatter_rows(dot_nt(pre_grad, w_fc), "tensor")
    )
    after_grad = own_grad + after_part
    after_low = gather_rows(after_grad.astype(BF16), "tensor")
    out_grad = dot_tn(mixed, after_low)
    mixed_grad = dot_nt(after_low, w_out).astype(BF16)
    q_grads, k_grads, v_grads = [], [], []
    for h in range(queries.shape[1] // HEAD_DIM):
        cols = slice(h * HEAD_DIM, (h + 1) * HEAD_DIM)
        probs_grad = dot_nt(mixed_grad[:, cols], values[:, cols])
        delta = jnp.sum(probs_grad * probs[h], axis=1, keepdims=True)
        score_grad = (probs[h] * (probs_grad - delta)).astype(BF16)
        q_grads.append((dot_nn(score_grad, key_heads[:, cols]) * HEAD_DIM ** (-0.5)).astype(BF16))
        k_grads.append((dot_tn(score_grad, queries[:, cols]) * HEAD_DIM ** (-0.5)).astype(BF16))
        v_grads.append(dot_tn(probs[h].astype(BF16), mixed_grad[:, cols]).astype(BF16))
    three = [jnp.concatenate(g, axis=1) for g in (q_grads, k_grads, v_grads)]
    attn_bias_grad = jnp.stack([jnp.sum(three[i].astype(F32), axis=0) for i in (0, 2)])
    attn_grad = jnp.stack([dot_tn(normed, g) for g in three])
    normed_part = sum(dot_nt(g, w_attn[i]) for i, g in enumerate(three))
    hidden_part, gain_attn, shift_attn = norm_back(
        hidden, gains[0:1], scatter_rows(normed_part, "tensor")
    )
    hidden_grad = after_grad + hidden_part
    num_grad = (hidden_grad / query_den).astype(BF16)
    den_grad = -jnp.sum(hidden_grad * recall, axis=1, keepdims=True) / query_den
    dots_grad = ((dot_nt(num_grad, solved) + den_grad) * own_mask).astype(BF16)
    query_grad = feature_map_back(query_mem.astype(F32), dot_nn(dots_grad, phi_key)).astype(BF16)
    solved_direct = dot_tn(query_dots.astype(BF16), num_grad)
    key_direct = feature_map_back(key_mem.astype(F32), dot_tn(dots_grad, phi_query))
    solved_direct = scatter_columns(solved_direct, "tensor")
    solved_direct = jnp.sum(lax.all_gather(solved_direct.astype(BF16), "seg").astype(F32), axis=0)
    value_grad = solve_backward(key_dots, key_den, solved_direct)
    read = value_part - solved_part
    key_den_grad = jnp.sum(value_grad * read, axis=1, keepdims=True) / key_den
    back = (-value_grad / key_den).astype(BF16)
    key_dots_grad = (dot_nt(back, solved_part.astype(BF16)) + key_den_grad) * mask
    both = (key_dots_grad + key_dots_grad.T).astype(BF16)
    key_solve = feature_map_back(key_mem.astype(F32), dot_nn(both, phi_key))
    mine = (jnp.arange(key_solve.shape[0]) // MEM == seg)[:, None]
    key_direct = key_direct + jnp.where(mine, key_solve, 0.0)
    key_direct = scatter_columns(key_direct, "tensor")
    key_grad = jnp.sum(lax.all_gather(key_direct.astype(BF16), "seg").astype(F32), axis=0).astype(BF16)
    value_low = value_grad.astype(BF16)
    mem_width = mem_rows.shape[1] // lax.axis_size("seg")
    mem_cols = lax.dynamic_slice_in_dim(mem_rows, seg * mem_width, mem_width, 1)
    mem_key_grad = dot_tn(mem_cols, key_grad)
    mem_value_grad = dot_tn(mem_cols, value_low)
    return (
        hidden_grad, query_grad, key_grad, value_low,
        (gain_attn, gain_mlp, shift_attn, shift_mlp, jnp.sum(after_grad, axis=0, keepdims=True), jnp.sum(own_grad, axis=0, keepdims=True)),
        (attn_grad, attn_bias_grad, out_grad, fc_grad, fc_bias_grad, proj_grad, mem_key_grad, mem_value_grad),
    )


def per_device(
    inputs, out_grad, item_lengths, norm_gains, norm_biases, w_attn, attn_bias, w_out, out_biases, w_fc, fc_bias,
    w_proj, w_mem_keys, w_mem_value,
):
    section, seg, part = (lax.axis_index(name) for name in ("section", "seg", "tensor"))
    segments, parts = lax.axis_size("seg"), lax.axis_size("tensor")
    layers = lax.axis_size("section")
    mask = reach_mask(item_lengths)[section]
    weights = (norm_gains, norm_biases, w_attn, attn_bias, w_out, out_biases, w_fc, fc_bias, w_proj, w_mem_keys, w_mem_value)
    weights = [lax.all_gather(w, "section", axis=0, tiled=True) for w in weights]
    full_keys = lax.all_gather(weights[9], "tensor", axis=3, tiled=True)
    rows_all, grad_all = inputs[section], out_grad[section]
    chunk = rows_all.shape[0] // parts
    own_rows = lax.dynamic_slice_in_dim(rows_all, part * chunk, chunk, 0)
    place = (seg, part)
    saved, layer_params = [], []
    for layer in range(layers):
        mems = lax.all_gather(own_rows[-MEM:], ("seg", "tensor"), axis=0)
        mem_rows = mems[parts - 1 :: parts].reshape(segments * MEM, -1)
        params = tuple(w[layer] for w in weights[:9]) + (full_keys[layer, 0], full_keys[layer, 1], weights[10][layer])
        output, kept = layer_forward(own_rows, mem_rows, mask, place, params)
        saved.append(kept)
        layer_params.append(params)
        own_rows = output.astype(BF16)
    own_grad = lax.dynamic_slice_in_dim(grad_all, part * chunk, chunk, 0).astype(F32)
    rows_grads, matrix_grads = [None] * layers, [None] * layers
    for layer in reversed(range(layers)):
        params, kept = layer_params[layer], saved[layer]
        hidden_grad, query_grad, key_grad, value_low, rows_grads[layer], grads = layer_backward(own_grad, kept, mask, place, params)
        w_q = params[9]
        keys_here = lax.dynamic_slice_in_dim(key_grad, seg * MEM, MEM, 0)
        values_here = lax.dynamic_slice_in_dim(value_low, seg * MEM, MEM, 0)
        tail = dot_nt(keys_here, weights[9][layer, 1]) + dot_nt(values_here, params[11])
        tail = jnp.sum(lax.all_gather(tail.astype(BF16), "tensor").astype(F32), axis=0)
        tail = jnp.concatenate([jnp.zeros((chunk - MEM, tail.shape[1]), F32), tail], axis=0)
        rows_grad = hidden_grad + dot_nt(query_grad, w_q) + jnp.where(part == parts - 1, tail, 0.0)
        own_grad = rows_grad.astype(BF16).astype(F32)
        rows_full = gather_rows(kept[0], "tensor")
        query_cols = lax.all_to_all(query_grad.reshape(chunk, parts, -1).transpose(1, 0, 2), "tensor", 0, 0, tiled=True)
        query_cols = query_cols.reshape(chunk * parts, -1)
        matrix_grads[layer] = grads + (dot_tn(rows_full, query_cols),)
    input_grad = gather_rows(own_grad.astype(BF16), "tensor")[None]

    def over_layers(values):
        return lax.psum_scatter(jnp.stack(values), "section", scatter_dimension=0, tiled=True)

    rows_sums = lax.psum(over_layers([jnp.concatenate(r, axis=0) for r in rows_grads]), ("seg", "tensor"))

    def spread(index, axis):
        stacked = jnp.stack([g[index] for g in matrix_grads]).astype(BF16)
        pair = lax.all_to_all(stacked, "section", 0, 0, tiled=True)
        both = jnp.sum(pair.astype(F32), axis=0)
        cut = both.astype(BF16).reshape(both.shape[:axis] + (segments, -1) + both.shape[axis + 1 :])
        got = lax.all_to_all(cut, "seg", axis, axis, tiled=True)
        return jnp.sum(got.astype(F32), axis=axis)[None]

    biases = lax.psum(
        (over_layers([g[1] for g in matrix_grads]), over_layers([g[4] for g in matrix_grads])), "seg"
    )
    query_w = spread(8, 0)
    key_w = over_layers([g[6] for g in matrix_grads])
    return (
        input_grad,
        rows_sums[:, 0:2],
        rows_sums[:, 2:4],
        spread(0, 1),
        biases[0],
        spread(2, 1),
        rows_sums[:, 4:6],
        spread(3, 0),
        biases[1],
        spread(5, 1),
        jnp.stack([query_w, key_w], axis=1),
        over_layers([g[7] for g in matrix_grads]),
    )


def solution(mesh):
    return jax.shard_map(
        per_device,
        mesh=mesh,
        in_specs=(
            P(None, "seg", None),
            P(None, "seg", None),
            P(),
            P("section", None, None),
            P("section", None, None),
            P("section", None, None, "tensor"),
            P("section", None, "tensor"),
            P("section", "tensor", None),
            P("section", None, None),
            P("section", None, "tensor"),
            P("section", "tensor"),
            P("section", "tensor", None),
            P("section", None, None, "tensor"),
            P("section", None, "tensor"),
        ),
        out_specs=(
            P("section", "seg", None),
            P("section", None, None),
            P("section", None, None),
            P("section", None, "seg", "tensor"),
            P("section", None, "tensor"),
            P("section", "tensor", "seg"),
            P("section", None, None),
            P("section", "seg", "tensor"),
            P("section", "tensor"),
            P("section", "tensor", "seg"),
            P("section", None, "seg", "tensor"),
            P("section", "seg", "tensor"),
        ),
        check_vma=False,
    )
```

time: 2280 us -> 807 us (0.35)
  waiting for transfers between devices: 1480 us -> 60.2 us
  blocking collectives: 105 us -> 406 us
  matrix products: 263 us -> 86.9 us
  other arithmetic: 166 us -> 74.6 us
  local copies, waits for them, and re-layouts: 120 us -> 72.7 us
  starting transfers between devices: 107 us -> 73.5 us
    ppermute x41 -> x0, waiting for transfers between devices: 603 us -> none  [the longest x36 602 us: passed_along(): return lax.ppermute(shard, axis, pairs)]
    psum x12 -> x0, waiting for transfers between devices: 534 us -> none  [the longest x3 151 us: layer_forward(): lax.psum(dot_plain(mixed_heads, w_out), 'tensor')]
    unnamed x32 -> x7, waiting for transfers between devices: 219 us -> 1.96 us
    all_gather x9 -> x29, blocking collectives: 84.6 us -> 297 us  [the longest x11 111 us: gather_rows(): return lax.all_gather(values, axis, axis=0, tiled=True)]
    dot_general x200 -> x119, matrix products: 263 us -> 86.9 us  [the longest x40 33.6 us: dot_tn(): lax.dot_general(left, right, (((0,), (0,)), ((), ())), preferred_element_...]
    reduce_scatter x4 -> x3, waiting for transfers between devices: 127 us -> 0.04 us  [over_layers(): lax.psum_scatter(jnp.stack(values), 'section', scatter_dimension=0, tiled...]
    ppermute x41 -> x0, starting transfers between devices: 104 us -> none  [the longest x36 103 us: passed_along(): return lax.ppermute(shard, axis, pairs)]
    all_to_all x0 -> x19, starting transfers between devices: none -> 73.2 us  [the longest x7 27.2 us: scatter_rows(): got = lax.all_to_all(pieces, axis, 0, 0, tiled=True)]
  transfers between devices with their start and end apart: 65 -> 26, of which waited for: 42 -> 13; matrix products, arithmetic and copies ran while one was open for 8% -> 17% of each run, Pallas kernels for 0% -> 0%
where the time goes in v1:
time: 807 us; the launch traced here: 792 us
  blocking collectives  406 us (50%)
  matrix products  86.9 us (11%)
  other arithmetic  74.6 us (9%)
  starting transfers between devices  73.5 us (9%)
  local copies, waits for them, and re-layouts  72.7 us (9%)
  waiting for transfers between devices  60.2 us (7%)
  between operations  18.7 us (2%)
    all_gather x11, blocking collectives, gather_rows(): return lax.all_gather(values, axis, axis=0, tiled=True)  111 us
    all_gather x2, blocking collectives, per_device(): mems = lax.all_gather(own_rows[-MEM:], ('seg', 'tensor'), axis=0)  84 us
    psum x1, blocking collectives, per_device(): lax.psum(over_layers([jnp.concatenate(r, axis=0) for r in rows_grads]), (...  72.6 us
    all_to_all x5, waiting for transfers between devices, spread(): got = lax.all_to_all(cut, 'seg', axis, axis, tiled=True)  33.8 us
    dot_general x40, matrix products, dot_tn(): lax.dot_general(left, right, (((0,), (0,)), ((), ())), preferred_element_...  33.6 us
    dot_general x41, matrix products, dot_nn(): lax.dot_general(left, right, (((1,), (0,)), ((), ())), preferred_element_...  28 us
    all_gather x2, blocking collectives, layer_backward(): lax.all_gather(key_direct.astype(BF16), 'seg').astype(F32)  27.5 us
    all_to_all x7, starting transfers between devices, scatter_rows(): got = lax.all_to_all(pieces, axis, 0, 0, tiled=True)  27.2 us
  transfers between devices with their start and end apart: 26, of which 13 were waited for; matrix products, arithmetic and copies ran while one was open for 17% of the time, Pallas kernels for 0%

profile of v1, /device:TPU:0, one launch (start us, length us, event | category | flops | bytes accessed | tf_op | source)
XLA Modules:
  0.0 792.2 jit_solution(9589946103953370662)
XLA Ops:
  17.0 44.9 %all_gather.123 = bf16[16,16,768]{2,1,0:T(8,128)(2,1)S(1)} all-gather(bf16[1,16,768]{2,1,0:T(8,128)(2,1)S(1)} %constant_dynamic-slice_fusion), channel_id=1, replica_groups=mesh['section'=2,'seg'=4,'tensor'=4] {'seg','tensor'}, dimensions={0}, use_global_device_ids=true | all-gather | bytes 417792 | tf_op jit(solution)/shard_map/all_gather | solution.py:273
  83.6 6.9 all-gather.9
  98.5 10.0 %all_gather.128 = bf16[256,768]{1,0:T(8,128)(2,1)S(1)} all-gather(bf16[64,768]{1,0:T(8,128)(2,1)S(1)} %add_convert_fusion.4), channel_id=1, replica_groups=mesh['section'=2,'seg'=4,'tensor'=4] {'tensor'}, dimensions={0}, use_global_device_ids=true | all-gather | bytes 491520 | tf_op jit(solution)/shard_map/all_gather | solution.py:101
  126.3 9.5 %all_gather.133 = bf16[256,768]{1,0:T(8,128)(2,1)S(1)} all-gather(bf16[64,768]{1,0:T(8,128)(2,1)S(1)} %add_convert_fusion.3), channel_id=1, replica_groups=mesh['section'=2,'seg'=4,'tensor'=4] {'tensor'}, dimensions={0}, use_global_device_ids=true | all-gather | bytes 491520 | tf_op jit(solution)/shard_map/all_gather | solution.py:101
  151.0 39.1 %all-gather = bf16[256,768]{1,0:T(8,128)(2,1)S(1)} all-gather(bf16[16,768]{1,0:T(8,128)(2,1)S(1)} %slice.1058), channel_id=2, replica_groups=mesh['section'=2,'seg'=4,'tensor'=4] {'seg','tensor'}, dimensions={0}, use_global_device_ids=true | all-gather | bytes 417792 | tf_op jit(solution)/shard_map/all_gather | solution.py:273
  198.5 7.5 all-gather.11
  213.2 10.2 %all_gather.140 = bf16[256,768]{1,0:T(8,128)(2,1)S(1)} all-gather(bf16[64,768]{1,0:T(8,128)(2,1)S(1)} %add_convert_fusion.1), channel_id=1, replica_groups=mesh['section'=2,'seg'=4,'tensor'=4] {'tensor'}, dimensions={0}, use_global_device_ids=true | all-gather | bytes 491520 | tf_op jit(solution)/shard_map/all_gather | solution.py:101
  232.4 12.3 %all-gather.8 = bf16[1,256,768]{2,1,0:T(8,128)(2,1)} all-gather(bf16[1,64,768]{2,1,0:T(8,128)(2,1)} %copy-done.94), channel_id=10, replica_groups=mesh['section'=2,'seg'=4,'tensor'=4] {'tensor'}, dimensions={1}, use_global_device_ids=true | all-gather | bytes 491520 | tf_op jit(solution)/shard_map/all_gather | solution.py:101
  244.7 10.6 %all-gather.1 = bf16[1,256,768]{2,1,0:T(8,128)(2,1)} all-gather(bf16[1,64,768]{2,1,0:T(8,128)(2,1)} %get-tuple-element.124), channel_id=3, replica_groups=mesh['section'=2,'seg'=4,'tensor'=4] {'tensor'}, dimensions={1}, use_global_device_ids=true | all-gather | bytes 491520 | tf_op jit(solution)/shard_map/all_gather | solution.py:101
  255.8 9.6 %all_gather.160 = bf16[256,768]{1,0:T(8,128)(2,1)} all-gather(bf16[64,768]{1,0:T(8,128)(2,1)S(1)} %add_convert_fusion.2), channel_id=1, replica_groups=mesh['section'=2,'seg'=4,'tensor'=4] {'tensor'}, dimensions={0}, use_global_device_ids=true | all-gather | bytes 491520 | tf_op jit(solution)/shard_map/all_gather | solution.py:101
  267.4 9.2 %all_gather.141 = bf16[256,768]{1,0:T(8,128)(2,1)S(1)} all-gather(bf16[64,768]{1,0:T(8,128)(2,1)S(1)} %add_convert_fusion), channel_id=1, replica_groups=mesh['section'=2,'seg'=4,'tensor'=4] {'tensor'}, dimensions={0}, use_global_device_ids=true | all-gather | bytes 491520 | tf_op jit(solution)/shard_map/all_gather | solution.py:101
  298.5 9.7 %all_gather.143 = bf16[256,768]{1,0:T(8,128)(2,1)S(1)} all-gather(bf16[64,768]{1,0:T(8,128)(2,1)S(1)} %convert_element_type.561), channel_id=1, replica_groups=mesh['section'=2,'seg'=4,'tensor'=4] {'tensor'}, dimensions={0}, use_global_device_ids=true | all-gather | bytes 491520 | tf_op jit(solution)/shard_map/all_gather | solution.py:101
  358.8 13.6 %all-gather.2 = bf16[256,192]{1,0:T(8,128)(2,1)S(1)} all-gather(bf16[64,192]{1,0:T(8,128)(2,1)} %reduce_sum.835), channel_id=4, replica_groups=mesh['section'=2,'seg'=4,'tensor'=4] {'seg'}, dimensions={0}, use_global_device_ids=true | all-gather | bytes 122880 | tf_op jit(solution)/shard_map/all_gather | solution.py:232
  397.6 13.9 %all-gather.3 = bf16[256,96]{1,0:T(8,128)(2,1)} all-gather(bf16[64,96]{1,0:T(8,128)(2,1)S(1)} %reduce_sum.838), channel_id=5, replica_groups=mesh['section'=2,'seg'=4,'tensor'=4] {'seg'}, dimensions={0}, use_global_device_ids=true | all-gather | bytes 61440 | tf_op jit(solution)/shard_map/all_gather | solution.py:243
  414.3 7.6 all-gather.4
  423.8 9.6 %all_gather.150 = bf16[256,768]{1,0:T(8,128)(2,1)S(1)} all-gather(bf16[64,768]{1,0:T(8,128)(2,1)S(1)} %fusion.30), channel_id=1, replica_groups=mesh['section'=2,'seg'=4,'tensor'=4] {'tensor'}, dimensions={0}, use_global_device_ids=true | all-gather | bytes 491520 | tf_op jit(solution)/shard_map/all_gather | solution.py:101
  450.0 10.0 %all_gather.151 = bf16[256,768]{1,0:T(8,128)(2,1)S(1)} all-gather(bf16[64,768]{1,0:T(8,128)(2,1)S(1)} %convert_element_type.600), channel_id=1, replica_groups=mesh['section'=2,'seg'=4,'tensor'=4] {'tensor'}, dimensions={0}, use_global_device_ids=true | all-gather | bytes 491520 | tf_op jit(solution)/shard_map/all_gather | solution.py:101
  509.9 13.5 %all-gather.5 = bf16[256,192]{1,0:T(8,128)(2,1)S(1)} all-gather(bf16[64,192]{1,0:T(8,128)(2,1)S(1)} %reduce_sum.851), channel_id=7, replica_groups=mesh['section'=2,'seg'=4,'tensor'=4] {'seg'}, dimensions={0}, use_global_device_ids=true | all-gather | bytes 122880 | tf_op jit(solution)/shard_map/all_gather | solution.py:232
  565.4 10.2 %all-to-all-done.14 = bf16[192,4,192]{2,0,1:T(8,128)(2,1)S(1)} async-done(((bf16[192,4,192]{2,0,1:T(8,128)(2,1)}), bf16[192,4,192]{2,0,1:T(8,128)(2,1)S(1)}, u32[]{:S(2)}, u32[]{:S(2)}) %all-to-all-start.14) | async-done | bytes 294944 | tf_op jit(solution)/shard_map/all_to_all | solution.py:309
  594.5 21.3 %all-to-all-done.12 = bf16[3,4,192,192]{3,2,0,1:T(8,128)(2,1)S(1)} async-done(((bf16[3,4,192,192]{3,2,0,1:T(8,128)(2,1)}), bf16[3,4,192,192]{3,2,0,1:T(8,128)(2,1)S(1)}, u32[]{:S(2)}, u32[]{:S(2)}) %all-to-all-start.12) | async-done | bytes 884768 | tf_op jit(solution)/shard_map/all_to_all | solution.py:309
  649.2 13.6 %all-gather.6 = bf16[256,96]{1,0:T(8,128)(2,1)S(1)} all-gather(bf16[64,96]{1,0:T(8,128)(2,1)S(1)} %reduce_sum.854), channel_id=8, replica_groups=mesh['section'=2,'seg'=4,'tensor'=4] {'seg'}, dimensions={0}, use_global_device_ids=true | all-gather | bytes 61440 | tf_op jit(solution)/shard_map/all_gather | solution.py:243
  665.4 12.3 %all-reduce.4 = (f32[1,2,192]{2,1,0:T(2,128)}, f32[1,768]{1,0:T(1,128)}) all-reduce(f32[1,2,192]{2,1,0:T(2,128)S(1)} %constant_dynamic-slice_fusion.9, f32[1,768]{1,0:T(1,128)S(1)} %constant_dynamic-slice_fusion.8), channel_id=1, replica_groups=mesh['section'=2,'seg'=4,'tensor'=4] {'seg'}, use_global_device_ids=true, to_apply=%region_83.84 | all-reduce | flops 1152 | bytes 9216 | tf_op jit(solution)/shard_map/psum | solution.py:312
  679.6 72.6 %psum.21 = f32[1,6,768]{2,1,0:T(8,128)} all-reduce(f32[1,6,768]{2,1,0:T(8,128)} %reduce-scatter.4.cloned.1.call-done), channel_id=1, replica_groups=mesh['section'=2,'seg'=4,'tensor'=4] {'seg','tensor'}, use_global_device_ids=true, to_apply=%region_75.76 | all-reduce | flops 4608 | bytes 36864 | tf_op jit(solution)/shard_map/psum | solution.py:302
  767.3 10.0 %all_gather.158 = bf16[256,768]{1,0:T(8,128)(2,1)S(1)} all-gather(bf16[64,768]{1,0:T(8,128)(2,1)S(1)} %fusion.31), channel_id=1, replica_groups=mesh['section'=2,'seg'=4,'tensor'=4] {'tensor'}, dimensions={0}, use_global_device_ids=true | all-gather | bytes 491520 | tf_op jit(solution)/shard_map/all_gather | solution.py:101
  (1018 shorter events, 385.6 us)
Async XLA Ops:
  7.2 69.5 %all-gather.17.cloned.1.call-start = ((), (), s32[]{:S(2)}) async-start(), calls=%async_computation.26 | async-start | bytes 2949120 | tf_op jit(solution)/shard_map/all_gather | solution.py:266
  12.9 95.7 %all-gather.19.cloned.1.call-start = ((), (), s32[]{:S(2)}) async-start(), calls=%async_computation.27 | async-start | bytes 2654208 | tf_op jit(solution)/shard_map/all_gather | solution.py:265
  13.6 122.2 %all-gather.21.cloned.1.call-start = ((), (), s32[]{:S(2)}) async-start(), calls=%async_computation.28 | async-start | bytes 3538944 | tf_op jit(solution)/shard_map/all_gather | solution.py:265
  14.4 124.3 %all-gather.23.cloned.1.call-start = ((), (), s32[]{:S(2)}) async-start(), calls=%async_computation.29 | async-start | bytes 3538944 | tf_op jit(solution)/shard_map/all_gather | solution.py:265
  115.5 9.3 %all-to-all-start = ((bf16[4,64,768]{2,1,0:T(8,128)(2,1)}), bf16[4,64,768]{2,1,0:T(8,128)(2,1)S(1)}, u32[]{:S(2)}, u32[]{:S(2)}) async-start(bf16[4,64,768]{2,1,0:T(8,128)(2,1)} %bitcast.359), calls=%async_computation | async-start | bytes 786432 | tf_op jit(solution)/shard_map/all_to_all | solution.py:107
  141.6 9.3 %all-to-all-start.1 = ((bf16[4,64,768]{2,1,0:T(8,128)(2,1)}), bf16[4,64,768]{2,1,0:T(8,128)(2,1)S(1)}, u32[]{:S(2)}, u32[]{:S(2)}) async-start(bf16[4,64,768]{2,1,0:T(8,128)(2,1)} %bitcast.363), calls=%async_computation.1 | async-start | bytes 786432 | tf_op jit(solution)/shard_map/all_to_all | solution.py:107
  228.1 37.2 %all-to-all-start.2 = ((bf16[4,64,768]{2,1,0:T(8,128)(2,1)}), bf16[4,64,768]{2,1,0:T(8,128)(2,1)}, u32[]{:S(2)}, u32[]{:S(2)}) async-start(bf16[4,64,768]{2,1,0:T(8,128)(2,1)} %bitcast.361), calls=%async_computation.2 | async-start | bytes 786432 | tf_op jit(solution)/shard_map/all_to_all | solution.py:107
  282.5 10.1 %all-to-all-start.3 = ((bf16[4,64,768]{2,1,0:T(8,128)(2,1)}), bf16[4,64,768]{2,1,0:T(8,128)(2,1)}, u32[]{:S(2)}, u32[]{:S(2)}) async-start(bf16[4,64,768]{2,1,0:T(8,128)(2,1)} %bitcast.362), calls=%async_computation.3 | async-start | bytes 786432 | tf_op jit(solution)/shard_map/all_to_all | solution.py:107
  315.4 10.8 %all-to-all-start.4 = ((bf16[4,64,768]{2,1,0:T(8,128)(2,1)}), bf16[4,64,768]{2,1,0:T(8,128)(2,1)}, u32[]{:S(2)}, u32[]{:S(2)}) async-start(bf16[4,64,768]{2,1,0:T(8,128)(2,1)} %bitcast.341), calls=%async_computation.4 | async-start | bytes 786432 | tf_op jit(solution)/shard_map/all_to_all | solution.py:107
  343.6 9.5 %all-to-all-start.5 = ((bf16[4,64,192]{2,1,0:T(8,128)(2,1)}), bf16[4,64,192]{2,1,0:T(8,128)(2,1)}, u32[]{:S(2)}, u32[]{:S(2)}) async-start(bf16[4,64,192]{2,1,0:T(8,128)(2,1)} %bitcast.357), calls=%async_computation.5 | async-start | bytes 262144 | tf_op jit(solution)/shard_map/all_to_all | solution.py:115
  353.1 34.5 %all-to-all-start.20 = ((bf16[4,64,96]{2,1,0:T(8,128)(2,1)}), bf16[4,64,96]{2,1,0:T(8,128)(2,1)}, u32[]{:S(2)}, u32[]{:S(2)}) async-start(bf16[4,64,96]{2,1,0:T(8,128)(2,1)} %bitcast.370), calls=%async_computation.21 | async-start | bytes 131072 | tf_op jit(solution)/shard_map/all_to_all | solution.py:294
  387.6 9.1 %all-to-all-start.6 = ((bf16[4,64,96]{2,1,0:T(8,128)(2,1)}), bf16[4,64,96]{2,1,0:T(8,128)(2,1)}, u32[]{:S(2)}, u32[]{:S(2)}) async-start(bf16[4,64,96]{2,1,0:T(8,128)(2,1)} %bitcast.373), calls=%async_computation.6 | async-start | bytes 131072 | tf_op jit(solution)/shard_map/all_to_all | solution.py:115
  437.5 9.3 %all-to-all-start.7 = ((bf16[4,64,768]{2,1,0:T(8,128)(2,1)}), bf16[4,64,768]{2,1,0:T(8,128)(2,1)S(1)}, u32[]{:S(2)}, u32[]{:S(2)}) async-start(bf16[4,64,768]{2,1,0:T(8,128)(2,1)} %bitcast.360), calls=%async_computation.7 | async-start | bytes 786432 | tf_op jit(solution)/shard_map/all_to_all | solution.py:107
  469.1 10.2 %all-to-all-start.8 = ((bf16[4,64,768]{2,1,0:T(8,128)(2,1)}), bf16[4,64,768]{2,1,0:T(8,128)(2,1)}, u32[]{:S(2)}, u32[]{:S(2)}) async-start(bf16[4,64,768]{2,1,0:T(8,128)(2,1)} %bitcast.342), calls=%async_computation.8 | async-start | bytes 786432 | tf_op jit(solution)/shard_map/all_to_all | solution.py:107
  495.0 9.0 %all-to-all-start.9 = ((bf16[4,64,192]{2,1,0:T(8,128)(2,1)}), bf16[4,64,192]{2,1,0:T(8,128)(2,1)}, u32[]{:S(2)}, u32[]{:S(2)}) async-start(bf16[4,64,192]{2,1,0:T(8,128)(2,1)} %bitcast.358), calls=%async_computation.9 | async-start | bytes 262144 | tf_op jit(solution)/shard_map/all_to_all | solution.py:115
  504.0 28.7 %all-to-all-start.17 = ((bf16[2,768,768]{2,1,0:T(8,128)(2,1)}), bf16[2,768,768]{2,1,0:T(8,128)(2,1)}, u32[]{:S(2)}, u32[]{:S(2)}) async-start(bf16[2,768,768]{2,1,0:T(8,128)(2,1)} %pad_maximum_fusion.1), calls=%async_computation.18 | async-start | bytes 4718592 | tf_op jit(solution)/shard_map/all_to_all | solution.py:306
  560.8 14.9 %all-to-all-start.14 = ((bf16[192,4,192]{2,0,1:T(8,128)(2,1)}), bf16[192,4,192]{2,0,1:T(8,128)(2,1)S(1)}, u32[]{:S(2)}, u32[]{:S(2)}) async-start(bf16[192,4,192]{2,0,1:T(8,128)(2,1)} %copy.110), calls=%async_computation.15 | async-start | bytes 786432 | tf_op jit(solution)/shard_map/all_to_all | solution.py:309
  576.4 9.6 %all-to-all-start.22 = ((bf16[4,192,96]{1,2,0:T(8,128)(2,1)}), bf16[4,192,96]{1,2,0:T(8,128)(2,1)S(1)}, u32[]{:S(2)}, u32[]{:S(2)}) async-start(bf16[4,192,96]{1,2,0:T(8,128)(2,1)} %copy.114), calls=%async_computation.23 | async-start | bytes 393216 | tf_op jit(solution)/shard_map/all_to_all | solution.py:309
  586.7 29.2 %all-to-all-start.12 = ((bf16[3,4,192,192]{3,2,0,1:T(8,128)(2,1)}), bf16[3,4,192,192]{3,2,0,1:T(8,128)(2,1)S(1)}, u32[]{:S(2)}, u32[]{:S(2)}) async-start(bf16[3,4,192,192]{3,2,0,1:T(8,128)(2,1)} %copy.109), calls=%async_computation.13 | async-start | bytes 2359296 | tf_op jit(solution)/shard_map/all_to_all | solution.py:309
  615.8 136.4 %all-to-all-start.18 = ((bf16[768,4,192]{0,2,1:T(8,128)(2,1)}), bf16[768,4,192]{0,2,1:T(8,128)(2,1)}, u32[]{:S(2)}, u32[]{:S(2)}) async-start(bf16[768,4,192]{0,2,1:T(8,128)(2,1)} %bitcast.338), calls=%async_computation.19 | async-start | bytes 2359296 | tf_op jit(solution)/shard_map/all_to_all | solution.py:309
  620.1 59.5 %reduce-scatter.4.cloned.1.call-start = ((), (), s32[]{:S(2)}) async-start(), calls=%async_computation.30 | async-start | bytes 73728 | tf_op jit(solution)/shard_map/reduce_scatter | solution.py:300
  648.3 130.0 %reduce-scatter.6.cloned.1.call-start = ((), (), s32[]{:S(2)}) async-start(), calls=%async_computation.31 | async-start | bytes 294912 | tf_op jit(solution)/shard_map/reduce_scatter | solution.py:300
  664.6 119.6 %reduce-scatter.8.cloned.1.call-start = ((), (), s32[]{:S(2)}) async-start(), calls=%async_computation.32 | async-start | bytes 589824 | tf_op jit(solution)/shard_map/reduce_scatter | solution.py:300
  752.2 31.0 %all-to-all-start.16 = ((bf16[4,192,768]{2,1,0:T(8,128)(2,1)}), bf16[4,192,768]{2,1,0:T(8,128)(2,1)S(1)}, u32[]{:S(2)}, u32[]{:S(2)}) async-start(bf16[4,192,768]{2,1,0:T(8,128)(2,1)} %bitcast.339), calls=%async_computation.17 | async-start | bytes 2359296 | tf_op jit(solution)/shard_map/all_to_all | solution.py:309
  (284 other events, 2649.9 us)
Sparse Core Ops, SparseCore 0:
  13.0 44.3 all-gather.16
  58.9 10.3 all-gather.18
  70.9 12.1 all-gather.20
  84.4 12.1 all-gather.22
  648.4 7.1 reduce-scatter.3
  664.7 6.8 reduce-scatter.5
  679.7 4.3 reduce-scatter.7

commit v2 on v1

--- a/solution.py
+++ b/solution.py
@@ -1,6 +1,12 @@
+import functools
+from types import SimpleNamespace
+from typing import Any, NamedTuple
+
 import jax
 import jax.numpy as jnp
 from jax import lax
+from jax.experimental import pallas as pl
+from jax.experimental.pallas import tpu as pltpu
 from jax.sharding import PartitionSpec as P
 
 HEAD_DIM = 64
@@ -11,6 +17,8 @@
 BF16 = jnp.bfloat16
 GELU_A = 0.7978845608028654
 GELU_B = 0.044715
+LAYERS = 2
+MESH = pl.DeviceIdType.MESH
 
 
 def dot_nn(left, right):
@@ -25,29 +33,26 @@
     return lax.dot_general(left, right, (((0,), (0,)), ((), ())), preferred_element_type=F32)
 
 
-def roll_lanes(values, by):
-    return jnp.roll(values, by, axis=1)
-
-
 def doubled_softplus(projected):
-    tail = jnp.log1p(jnp.exp(-jnp.abs(projected)))
+    small = jnp.exp(-jnp.abs(projected))
+    tail = jnp.where(small < 1e-3, small - 0.5 * small * small, jnp.log1p(small))
     return jnp.concatenate(
         [jnp.maximum(projected, 0.0) + tail, jnp.maximum(-projected, 0.0) + tail], axis=1
     )
 
 
-def feature_map(projected):
+def feature_map(projected, roll=pltpu.roll):
     doubled = doubled_softplus(projected)
-    return jnp.concatenate([doubled * roll_lanes(doubled, j) for j in range(1, NU + 1)], axis=1)
-
-
-def feature_map_back(projected, phi_grad):
+    return jnp.concatenate([doubled * roll(doubled, j, 1) for j in range(1, NU + 1)], axis=1)
+
+
+def feature_map_back(projected, phi_grad, roll=pltpu.roll):
     doubled = doubled_softplus(projected)
     width = doubled.shape[1]
     total = jnp.zeros_like(doubled)
     for j in range(1, NU + 1):
         part = phi_grad[:, (j - 1) * width : j * width]
-        total = total + part * roll_lanes(doubled, j) + roll_lanes(part * doubled, width - j)
+        total = total + part * roll(doubled, j, 1) + roll(part * doubled, width - j, 1)
     half = width // 2
     gate = 1.0 / (1.0 + jnp.exp(-projected))
     return total[:, :half] * gate - total[:, half:] * (1.0 - gate)
@@ -81,6 +86,811 @@
     return value, slope
 
 
+def xor_peer(place, other, count):
+    total, bit = 0, 1
+    while bit < count:
+        mine = lax.rem(lax.div(place, bit), 2)
+        total = total + bit * (1 - mine if other & bit else mine)
+        bit *= 2
+    return total
+
+
+def split(values):
+    high = values.astype(BF16)
+    return high, (values - high.astype(F32)).astype(BF16)
+
+
+class Sizes:
+    def __init__(self, mesh, shapes):
+        self.segs, self.parts = mesh.shape["seg"], mesh.shape["tensor"]
+        inputs, w_attn, w_fc, w_keys = shapes
+        self.rows, self.width = inputs[1] // self.segs, inputs[2]
+        self.chunk = self.rows // self.parts
+        self.mems = self.segs * MEM
+        self.heads_w = w_attn[3] // self.parts
+        self.heads = self.heads_w // HEAD_DIM
+        self.units = w_fc[2] // self.parts
+        self.keys = w_keys[3]
+        self.keys_w = self.keys // self.parts
+        self.phi = 2 * self.keys * NU
+        self.val_w = self.width // self.parts
+        self.cut = self.width // self.segs
+        self.cut_pad = -(-self.cut // 16) * 16
+        self.sems = 120 + 48 * self.parts + 2 * self.segs * (self.parts + 16)
+
+
+def scratch_of(z):
+    S, T, R, D, C, M = z.segs, z.parts, z.rows, z.width, z.chunk, z.mems
+    bf = lambda *d: pltpu.VMEM(d, BF16)
+    fl = lambda *d: pltpu.VMEM(d, F32)
+    return dict(
+        gains=fl(2, 2, D), shifts=fl(2, 2, D), w_attn=bf(2, 3, z.heads_w, D), attn_bias=fl(2, 2, z.heads_w),
+        w_out=bf(2, z.heads_w, D), out_biases=fl(2, 2, D), w_fc=bf(2, D, z.units), fc_bias=fl(2, 1, z.units),
+        w_proj=bf(2, z.units, D), w_keys=bf(2, 2, z.keys, D), w_value=bf(2, z.val_w, D),
+        xfull=bf(2, R, D), gfull=bf(2, R, D), mem_rows=bf(2, M, D),
+        keyb=bf(2, M, z.keys), phik=bf(2, M, z.phi), kdots=fl(2, M, M), vpart=fl(2, M, z.val_w),
+        upart=fl(2, M, z.val_w), uall=bf(2, T, M, z.val_w), qmem=bf(2, C, z.keys), phiq=bf(2, C, z.phi),
+        qdots=fl(2, C, M), recall=fl(2, C, D), hidden=fl(2, C, D), normed=bf(2, R, D), qkv=bf(2, 3, R, z.heads_w),
+        probs=fl(2, z.heads, R, R), mixed=bf(2, R, z.heads_w), after=fl(2, C, D), normed_mlp=bf(2, R, D),
+        slope=fl(2, R, z.units), act=bf(2, R, z.units), rs_src=bf(7, R, D), rs_own=fl(R, D), q_src=bf(R, z.keys_w), q_parts=bf(T, C, z.keys_w), k_parts=bf(T, M, z.keys_w), rs_dst=bf(7, T - 1, C, D),
+        low2=bf(2, R, D), dpre=bf(R, z.units), dqkv=bf(3, R, z.heads_w),
+        x1_src=fl(2, T, M, z.val_w), x1_dst=fl(2, T - 1, M, z.val_w), x1_mid=fl(2, M, z.val_w), x1_far=fl(2, max(S - 1, 1), M, z.val_w),
+        x2_src=fl(2, T, M, z.keys_w), x2_dst=fl(2, T - 1, M, z.keys_w), x2_mid=fl(2, M, z.keys_w), x2_far=fl(2, max(S - 1, 1), M, z.keys_w), x4_src=fl(2, T, M, z.keys_w), x4_dst=fl(2, T - 1, M, z.keys_w), ksolve=fl(M, z.keys), dk_direct=fl(M, z.keys_w),
+        dq_src=bf(2, T, C, z.keys_w), dq_all=bf(2, R, z.keys_w), dv=bf(M, z.val_w), vgrad=fl(M, z.val_w),
+        x3_src=bf(2, MEM, D), x3_dst=bf(2, T - 1, MEM, D), final=bf(R, D), tmp=fl(C, D),
+        grad_f=bf(2, S, 2, z.cut_pad, D), grad_a=bf(2, S, 4, z.cut_pad, z.heads_w), grad_q=bf(2, S, z.cut_pad, z.keys_w),
+        pair_f=bf(S, 2, z.cut_pad, D), pair_a=bf(S, 4, z.cut_pad, z.heads_w), pair_q=bf(S, z.cut_pad, z.keys_w),
+        far_f=bf(max(S - 1, 1), 2, z.cut_pad, D), far_a=bf(max(S - 1, 1), 4, z.cut_pad, z.heads_w), far_q=bf(max(S - 1, 1), z.cut_pad, z.keys_w),
+        mem_k=fl(2, D, z.keys_w), mem_v=fl(2, D, z.val_w), pair_k=fl(z.cut, z.keys_w), pair_v=fl(z.cut, z.val_w),
+        small=fl(2, 16, D), pair_small=fl(16, D), part_small=fl(T, 8, D), seg_small=fl(S, 16, D),
+        send=pltpu.SemaphoreType.DMA((z.sems,)), recv=pltpu.SemaphoreType.DMA((z.sems,)), load=pltpu.SemaphoreType.DMA((14, 2)),
+        shard=pltpu.SemaphoreType.DMA((2, 2, T)),
+    )
+
+
+class Outer(NamedTuple):
+    inputs: Any
+    out_grad: Any
+    item_lengths: Any
+    norm_gains: Any
+    norm_biases: Any
+    w_attn_in: Any
+    attn_bias_in: Any
+    w_out_in: Any
+    out_biases_in: Any
+    w_fc_in: Any
+    fc_bias_in: Any
+    w_proj_in: Any
+    w_keys_in: Any
+    w_value_in: Any
+    input_grad: Any
+    gain_grads: Any
+    shift_grads: Any
+    attn_grads: Any
+    abias_grads: Any
+    out_grads: Any
+    obias_grads: Any
+    fc_grads: Any
+    fcb_grads: Any
+    proj_grads: Any
+    mkey_grads: Any
+    mvalue_grads: Any
+
+
+def kernel(z, held_names, *refs):
+    outer = len(Outer._fields)
+    r = SimpleNamespace(**Outer(*refs[:outer])._asdict(), **dict(zip(held_names, refs[outer:])))
+    S, T, R, D, C, M = z.segs, z.parts, z.rows, z.width, z.chunk, z.mems
+    c, s, t = (lax.axis_index(a) for a in ("section", "seg", "tensor"))
+    other = 1 - c
+    tpeers = [xor_peer(t, i, T) for i in range(T)]
+    to_seg = [lax.rem(s + i, S) for i in range(S)]
+    own = pl.ds(pl.multiple_of(t * C, C), C)
+    seg_rows = pl.ds(pl.multiple_of(s * MEM, MEM), MEM)
+    used = [0]
+    sent = []
+    owed = {}
+
+    def alloc(count):
+        used[0] += count
+        assert used[0] <= z.sems
+        return used[0] - count
+
+    def owe(copies):
+        def wait():
+            for copy in copies:
+                copy.wait_recv()
+
+        owed[id(copies)] = wait
+        return id(copies)
+
+    def wait_bytes(ref, semaphore):
+        pltpu.make_async_copy(ref, ref, semaphore).wait()
+
+    def remote(src, dst, index, device, recv=None):
+        copy = pltpu.make_async_remote_copy(
+            src_ref=src, dst_ref=dst, send_sem=r.send.at[index],
+            recv_sem=r.recv.at[index] if recv is None else recv, device_id=device, device_id_type=MESH,
+        )
+        return copy
+
+    def to_parts(src_of, dst):
+        base = alloc(T - 1)
+        copies = []
+        for i in range(T - 1, 0, -1):
+            copy = remote(src_of(tpeers[i]), dst(i), base + i - 1, (c, s, tpeers[i]))
+            copy.start()
+            copies.append(copy)
+        sent.extend((copy, None) for copy in copies)
+        return owe(copies)
+
+    def to_segs(src_of, dst):
+        base = alloc(S - 1)
+        copies = [
+            remote(src_of(to_seg[i]), dst(i), base + i - 1, (c, to_seg[i], t)) for i in range(1, S)
+        ]
+        for copy in copies:
+            copy.start()
+        sent.extend((copy, None) for copy in copies)
+        return owe(copies)
+
+    def arrive(key):
+        owed.pop(key)()
+
+    def wait_load(ref, layer):
+        arrive((id(ref), layer))
+
+    barrier = pltpu.get_barrier_semaphore()
+    greeted = [(other, s, t)] + [(c, to_seg[i], tpeers[j]) for i in range(S) for j in range(T) if i or j]
+    for device in greeted:
+        pl.semaphore_signal(barrier, inc=1, device_id=device, device_id_type=MESH)
+
+    loads = [
+        (r.w_value, r.w_value_in.at[0]), (r.gains, r.norm_gains.at[0]), (r.shifts, r.norm_biases.at[0]),
+        (r.attn_bias, r.attn_bias_in.at[0]), (r.out_biases, r.out_biases_in.at[0]), (r.w_attn, r.w_attn_in.at[0]), (r.w_out, r.w_out_in.at[0]), (r.w_fc, r.w_fc_in.at[0]),
+        (r.w_proj, r.w_proj_in.at[0]), (r.fc_bias, r.fc_bias_in),
+    ]
+    input_copy = pltpu.make_async_copy(r.inputs.at[c], r.xfull.at[0], r.load.at[10, 0])
+    input_copy.start()
+    owed[0] = input_copy.wait
+    def shard_rows(part):
+        return pl.ds(pl.multiple_of(part * z.keys_w, 16), z.keys_w)
+
+    for which in (0, 1):
+        pltpu.make_async_copy(
+            r.w_keys_in.at[0, which], r.w_keys.at[c, which, shard_rows(t)], r.shard.at[c, which, 0]
+        ).start()
+    for kind, (held, source) in enumerate(loads):
+        pltpu.make_async_copy(source, held.at[c], r.load.at[kind, c]).start()
+        for layer in range(LAYERS):
+            owed[id(held), layer] = functools.partial(wait_bytes, held.at[layer], r.load.at[kind, layer])
+    grad_copy = pltpu.make_async_copy(r.out_grad.at[c], r.gfull.at[1], r.load.at[11, 0])
+    grad_copy.start()
+    owed[1] = grad_copy.wait
+
+    pl.semaphore_wait(barrier, len(greeted))
+
+    first_rows = to_segs(
+        lambda _: r.inputs.at[c, pl.ds(R - MEM, MEM)], lambda i: r.mem_rows.at[0, seg_rows]
+    )
+
+    def shard_wait(layer, which, i):
+        wait_bytes(r.w_keys.at[layer, which, pl.ds(0, z.keys_w)], r.shard.at[layer, which, i])
+
+    def peer_shards(core, layer, which):
+        @pl.when(c == core)
+        def _():
+            for i in range(1, T):
+                shard_wait(layer, which, i)
+
+    def spread_shard(layer, which):
+        base = alloc(T - 1)
+        place = r.w_keys.at[layer, which, shard_rows(t)]
+        copies = [
+            remote(r.w_keys_in.at[0, which], place, base + i - 1, (c, s, tpeers[i]), r.shard.at[layer, which, i])
+            for i in range(T - 1, 0, -1)
+        ]
+
+        @pl.when(c == layer)
+        def _():
+            for copy in copies:
+                copy.start()
+
+        sent.extend((copy, c == layer) for copy in copies)
+        owed[11, layer, which] = functools.partial(peer_shards, layer, layer, which)
+
+    def forward_shard(layer, which):
+        arrive((11, layer, which))
+        base = alloc(T - 1)
+        copies = []
+        for i in range(1, T):
+            place = r.w_keys.at[layer, which, shard_rows(tpeers[i])]
+            copies.append(remote(place, place, base + i - 1, (other, s, t), r.shard.at[layer, which, i]))
+
+        @pl.when(c == layer)
+        def _():
+            for copy in copies:
+                copy.start()
+
+        sent.extend((copy, c == layer) for copy in copies)
+        owed[12, layer, which] = functools.partial(peer_shards, 1 - layer, layer, which)
+
+    base = alloc(2)
+    for which in (0, 1):
+        copy = remote(
+            r.w_keys_in.at[0, which], r.w_keys.at[c, which, shard_rows(t)], base + which, (other, s, t), r.shard.at[c, which, 0]
+        )
+        copy.start()
+        sent.append((copy, None))
+        for layer in range(LAYERS):
+            owed[10, layer, which] = functools.partial(shard_wait, layer, which, 0)
+    pair_base = alloc(len(loads))
+    for kind, (held, source) in enumerate(loads):
+        copy = remote(source, held.at[c], pair_base + kind, (other, s, t), r.load.at[kind, c])
+        copy.start()
+        sent.append((copy, None))
+
+    row_seg = lax.broadcasted_iota(jnp.int32, (M, 1), 0) // MEM
+    col_seg = lax.broadcasted_iota(jnp.int32, (1, M), 1) // MEM
+    row_item, col_item, own_item = jnp.zeros((M, 1), jnp.int32), jnp.zeros((1, M), jnp.int32), 0
+    begin = 0
+    for i in range(r.item_lengths.shape[1]):
+        length = r.item_lengths[c, i]
+        there = jnp.where(length > 0, begin, S)
+        row_item = row_item + (row_seg >= there).astype(jnp.int32)
+        col_item = col_item + (col_seg >= there).astype(jnp.int32)
+        own_item = own_item + jnp.where(s >= there, 1, 0)
+        begin = begin + length
+    key_mask = jnp.where((row_item == col_item) & (row_seg > col_seg), 1.0, 0.0)
+    row_mask = jnp.where((col_item == own_item) & (col_seg < s), 1.0, 0.0)
+    lane_head = lax.broadcasted_iota(jnp.int32, (1, z.heads_w), 1) // HEAD_DIM
+    head_rows = [(lane_head == h).astype(F32).astype(BF16) for h in range(z.heads)]
+    rs_count = [0]
+
+    def reduce_rows(partial):
+        k = rs_count[0]
+        rs_count[0] += 1
+        r.rs_own[...] = partial
+        r.rs_src[k] = partial.astype(BF16)
+        copies = to_parts(
+            lambda peer: r.rs_src.at[k, pl.ds(pl.multiple_of(peer * C, C), C)], lambda i: r.rs_dst.at[k, i - 1]
+        )
+
+        def finish():
+            arrive(copies)
+            total = r.rs_own[own, :]
+            for i in range(T - 1):
+                total = total + r.rs_dst[k, i].astype(F32)
+            return total
+
+        return finish
+
+    def share_rows(ref, layer):
+        return to_parts(lambda _: ref.at[layer, own], lambda i: ref.at[layer, own])
+
+    def forward(l):
+        own_shard = shard_rows(t)
+        if l == 0:
+            arrive(0)
+            arrive((10, 0, 0))
+            r.q_src[...] = dot_nt(r.xfull[0], r.w_keys[0, 0, own_shard, :]).astype(BF16)
+            r.q_parts[t] = r.q_src[own, :]
+            query_step = to_parts(
+                lambda peer: r.q_src.at[pl.ds(pl.multiple_of(peer * C, C), C)], lambda i: r.q_parts.at[t]
+            )
+            r.mem_rows[0, seg_rows, :] = r.xfull[0, R - MEM :, :]
+            arrive((10, 0, 1))
+            arrive(first_rows)
+            mems = r.mem_rows[0]
+            r.k_parts[t] = dot_nt(mems, r.w_keys[0, 1, own_shard, :]).astype(BF16)
+            key_step = to_parts(lambda _: r.k_parts.at[t], lambda i: r.k_parts.at[t])
+            arrive(query_step)
+            queries_mem = jnp.concatenate([r.q_parts[u] for u in range(T)], axis=1)
+        else:
+            for which in (0, 1):
+                arrive((10, 1, which))
+                arrive((12, 1, which))
+            queries_mem = dot_nt(r.xfull[1, own, :], r.w_keys[1, 0]).astype(BF16)
+        x = r.xfull[l, own, :]
+        r.qmem[l] = queries_mem
+        phi_query = feature_map(queries_mem.astype(F32)).astype(BF16)
+        r.phiq[l] = phi_query
+        wait_load(r.w_value, l)
+        if l == 1:
+            arrive(4)
+            mems = r.mem_rows[1]
+        value_part = dot_nt(mems, r.w_value[l])
+        r.vpart[l] = value_part
+        r.upart[l] = value_part
+        if l == 0:
+            arrive(key_step)
+            keys = jnp.concatenate([r.k_parts[u] for u in range(T)], axis=1)
+        else:
+            keys = dot_nt(mems, r.w_keys[1, 1]).astype(BF16)
+        r.keyb[l] = keys
+        phi_key = feature_map(keys.astype(F32)).astype(BF16)
+        r.phik[l] = phi_key
+        key_dots = dot_nt(phi_key, phi_key) * key_mask
+        r.kdots[l] = key_dots
+        key_den = 1.0 + jnp.sum(key_dots, axis=1, keepdims=True)
+        for k in range(1, S):
+            rows = slice(k * MEM, (k + 1) * MEM)
+            read = dot_nn(key_dots[rows].astype(BF16), r.upart[l].astype(BF16)) / key_den[rows]
+            r.upart[l, rows, :] = value_part[rows] - read
+        r.uall[l, t] = r.upart[l].astype(BF16)
+        solved = to_parts(lambda _: r.uall.at[l, t], lambda i: r.uall.at[l, t])
+        if l == 0:
+            spread_shard(1, 1)
+        else:
+            spread_shard(0, 0)
+        query_dots = dot_nt(phi_query, phi_key) * row_mask
+        r.qdots[l] = query_dots
+        query_den = 1.0 + jnp.sum(query_dots, axis=1, keepdims=True)
+        for ref in (r.gains, r.shifts, r.attn_bias, r.out_biases):
+            wait_load(ref, l)
+        arrive(solved)
+        high, low = split(query_dots)
+        recall = [dot_nn(high, r.uall[l, u]) + dot_nn(low, r.uall[l, u]) for u in range(T)]
+        recall = jnp.concatenate(recall, axis=1) / query_den
+        r.recall[l] = recall
+        hidden = x.astype(F32) + recall.astype(BF16).astype(F32)
+        r.hidden[l] = hidden
+        unit, _ = norm_rows(hidden)
+        r.normed[l, own, :] = (unit * r.gains[l, 0:1] + r.shifts[l, 0:1]).astype(BF16)
+        shared = share_rows(r.normed, l)
+        wait_load(r.w_attn, l)
+        wait_load(r.w_out, l)
+        arrive(shared)
+        if l == 0:
+            spread_shard(1, 0)
+            row_step = None
+        else:
+            spread_shard(0, 1)
+            row_step = share_rows(r.xfull, 1)
+        normed = r.normed[l]
+        queries = (dot_nt(normed, r.w_attn[l, 0]) + r.attn_bias[l, 0:1]).astype(BF16)
+        key_heads = dot_nt(normed, r.w_attn[l, 1]).astype(BF16)
+        values = (dot_nt(normed, r.w_attn[l, 2]) + r.attn_bias[l, 1:2]).astype(BF16)
+        r.qkv[l, 0] = queries
+        r.qkv[l, 1] = key_heads
+        r.qkv[l, 2] = values
+        causal = lax.broadcasted_iota(jnp.int32, (R, R), 0) >= lax.broadcasted_iota(jnp.int32, (R, R), 1)
+        mixed = jnp.zeros((R, z.heads_w), F32)
+        for h in range(z.heads):
+            scores = dot_nt(queries, key_heads * head_rows[h]) * HEAD_DIM ** (-0.5)
+            scores = jnp.where(causal, scores, -jnp.inf)
+            heights = jnp.exp(scores - jnp.max(scores, axis=1, keepdims=True))
+            probs = heights * (1.0 / jnp.sum(heights, axis=1, keepdims=True))
+            r.probs[l, h] = probs
+            mixed = mixed + dot_nn(probs.astype(BF16), values * head_rows[h])
+        mixed = mixed.astype(BF16)
+        r.mixed[l] = mixed
+        finish = reduce_rows(dot_nn(mixed, r.w_out[l]))
+        after = r.hidden[l] + finish() + r.out_biases[l, 0:1]
+        r.after[l] = after
+        unit, _ = norm_rows(after)
+        r.normed_mlp[l, own, :] = (unit * r.gains[l, 1:2] + r.shifts[l, 1:2]).astype(BF16)
+        shared = share_rows(r.normed_mlp, l)
+        wait_load(r.w_fc, l)
+        wait_load(r.fc_bias, l)
+        wait_load(r.w_proj, l)
+        if l == 0:
+            forward_shard(1, 1)
+            forward_shard(1, 0)
+        arrive(shared)
+        pre = dot_nn(r.normed_mlp[l], r.w_fc[l]) + r.fc_bias[l]
+        activation, slope = gelu_and_slope(pre)
+        activation = activation.astype(BF16)
+        r.act[l] = activation
+        r.slope[l] = slope
+        if l == 0:
+            finish = reduce_rows(dot_nn(activation, r.w_proj[l]))
+            output = r.after[l] + finish() + r.out_biases[l, 1:2]
+            r.xfull[1, own, :] = output.astype(BF16)
+            base, places = alloc(S), alloc(S * T)
+            last = r.xfull.at[1, pl.ds(R - MEM, MEM)]
+
+            @pl.when(t == T - 1)
+            def _():
+                r.mem_rows[1, seg_rows, :] = r.xfull[1, R - MEM :, :]
+                for i in range(S - 1, -1, -1):
+                    for j in range(1 if i == 0 else 0, T):
+                        copy = pltpu.make_async_remote_copy(
+                            src_ref=last, dst_ref=r.mem_rows.at[1, seg_rows], send_sem=r.send.at[places + i * T + j],
+                            recv_sem=r.recv.at[base + i], device_id=(c, to_seg[i], tpeers[j]), device_id_type=MESH,
+                        )
+                        copy.start()
+
+            def wait_rows(i):
+                wait_bytes(r.mem_rows.at[1, pl.ds(0, MEM)], r.recv.at[base + i])
+
+            def wait_all():
+                pl.when(t != T - 1)(functools.partial(wait_rows, 0))
+                for i in range(1, S):
+                    wait_rows(i)
+
+            owed[4] = wait_all
+
+            def drain():
+                @pl.when(t == T - 1)
+                def _():
+                    for i in range(S):
+                        for j in range(1 if i == 0 else 0, T):
+                            wait_bytes(last, r.send.at[places + i * T + j])
+
+            sent.append((drain, drain))
+        return row_step
+
+    fam_f, fam_a, fam_q = (r.grad_f, r.pair_f, r.far_f), (r.grad_a, r.pair_a, r.far_a), (r.grad_q, r.pair_q, r.far_q)
+
+    def blocks_of(first_row, count):
+        row, pieces = first_row, []
+        while row < first_row + count:
+            block, inside = row // z.cut, row % z.cut
+            size = min(z.cut - inside, first_row + count - row)
+            pieces.append((block, inside, row - first_row, size))
+            row += size
+        return pieces
+
+    def weight_grad(left, right, store):
+        stripe = min(256, D)
+        for k in range(0, D, stripe):
+            grad = dot_tn(left[:, k : k + stripe], right).astype(BF16)
+            for block, inside, row, size in blocks_of(k, stripe):
+                store(block, slice(inside, inside + size), grad[row : row + size])
+
+    def pair_send(src, dst):
+        index = alloc(1)
+        return remote(src, dst, index, (other, s, t))
+
+    def hand_over(l, names):
+        copies = [pair_send(grad.at[l], pair) for grad, pair, _ in names]
+
+        @pl.when(c != l)
+        def _():
+            for copy in copies:
+                copy.start()
+
+        sent.extend((copy, c != l) for copy in copies)
+        return owe_owner(l, copies)
+
+    def owe_owner(l, copies):
+        def wait():
+            @pl.when(c == l)
+            def _():
+                for copy in copies:
+                    copy.wait_recv()
+
+        owed[id(copies)] = wait
+        return id(copies)
+
+    def add_and_spread(l, names, copies):
+        bases = [alloc(S - 1) for _ in names]
+        arrive(copies)
+
+        @pl.when(c == l)
+        def _():
+            for (grad, pair, far), base in zip(names, bases):
+
+                @pl.loop(0, S)
+                def _(j):
+                    if len(grad.shape) == 4:
+                        grad[l, j] = (grad[l, j].astype(F32) + pair[j].astype(F32)).astype(BF16)
+                    else:
+                        for m in range(grad.shape[2]):
+                            grad[l, j, m] = (grad[l, j, m].astype(F32) + pair[j, m].astype(F32)).astype(BF16)
+
+                for i in range(1, S):
+                    remote(grad.at[l, to_seg[i]], far.at[i - 1], base + i - 1, (c, to_seg[i], t)).start()
+
+        for (grad, _, far), base in zip(names, bases):
+            owed[id(far), l] = functools.partial(far_wait, l, far, base)
+            sent.append((functools.partial(far_drain, l, grad, base),) * 2)
+
+    def far_wait(l, far, base):
+        @pl.when(c == l)
+        def _():
+            for i in range(1, S):
+                wait_bytes(far.at[i - 1], r.recv.at[base + i - 1])
+
+    def far_drain(l, grad, base):
+        @pl.when(c == l)
+        def _():
+            for i in range(1, S):
+                wait_bytes(grad.at[l, 0], r.send.at[base + i - 1])
+
+    def owe_small(l):
+        copy = pair_send(r.small.at[l], r.pair_small)
+        pl.when(c != l)(copy.start)
+        sent.append((copy, c != l))
+        return owe_owner(l, [copy])
+
+    def owner_copies(l, copies):
+        @pl.when(c == l)
+        def _():
+            for copy in copies:
+                copy.start()
+
+        sent.extend((copy, c == l) for copy in copies)
+        return owe_owner(l, copies)
+
+    def small_parts(l, key):
+        arrive(key)
+
+        @pl.when(c == l)
+        def _():
+            r.seg_small[0] = r.small[l] + r.pair_small[...]
+            r.part_small[0] = r.seg_small[0, 0:8, :]
+
+        base = alloc(T - 1)
+        return owner_copies(
+            l, [remote(r.part_small.at[0], r.part_small.at[i], base + i - 1, (c, s, tpeers[i])) for i in range(1, T)]
+        )
+
+    def small_segs(l, key):
+        arrive(key)
+
+        @pl.when(c == l)
+        def _():
+            total = r.part_small[0]
+            for i in range(1, T):
+                total = total + r.part_small[i]
+            r.seg_small[0, 0:8, :] = total
+
+        base = alloc(S - 1)
+        return owner_copies(
+            l, [remote(r.seg_small.at[0], r.seg_small.at[i], base + i - 1, (c, to_seg[i], t)) for i in range(1, S)]
+        )
+
+    def backward(l):
+        if l == 1:
+            arrive(1)
+        grad_low = r.gfull[l]
+        pre_grad = (r.slope[l] * dot_nt(grad_low, r.w_proj[l])).astype(BF16)
+        r.dpre[...] = pre_grad
+        finish = reduce_rows(dot_nt(pre_grad, r.w_fc[l]))
+        own_grad = r.gfull[l, own, :].astype(F32)
+
+        def store_f(m):
+            def store(block, rows, value):
+                r.grad_f[l, block, m, rows, :] = value
+
+            return store
+
+        weight_grad(r.normed_mlp.at[l], r.dpre[...], store_f(0))
+        weight_grad(r.gfull.at[l], r.act[l], store_f(1))
+        r.small[l, 8:9, :] = jnp.sum(r.dpre[...].astype(F32), axis=0, keepdims=True)
+        pair_f = hand_over(l, (fam_f,))
+        if l == 1:
+            forward_shard(0, 0)
+            forward_shard(0, 1)
+        after_part, gain_mlp, shift_mlp = norm_back(r.after[l], r.gains[l, 1:2], finish())
+        after_grad = own_grad + after_part
+        r.tmp[...] = after_grad
+        r.low2[l, own, :] = after_grad.astype(BF16)
+        shared = share_rows(r.low2, l)
+        r.small[l, 1:2, :] = gain_mlp
+        r.small[l, 3:4, :] = shift_mlp
+        r.small[l, 4:5, :] = jnp.sum(after_grad, axis=0, keepdims=True)
+        r.small[l, 5:6, :] = jnp.sum(own_grad, axis=0, keepdims=True)
+        add_and_spread(l, (fam_f,), pair_f)
+        arrive(shared)
+        after_low = r.low2[l]
+        mixed_grad = dot_nt(after_low, r.w_out[l]).astype(BF16)
+        queries, key_heads, values = r.qkv[l, 0], r.qkv[l, 1], r.qkv[l, 2]
+        q_grad = k_grad = v_grad = jnp.zeros((R, z.heads_w), F32)
+        for h in range(z.heads):
+            probs = r.probs[l, h]
+            mixed_here = mixed_grad * head_rows[h]
+            probs_grad = dot_nt(mixed_here, values)
+            delta = jnp.sum(probs_grad * probs, axis=1, keepdims=True)
+            score_grad = (probs * (probs_grad - delta)).astype(BF16)
+            q_grad = q_grad + dot_nn(score_grad, key_heads * head_rows[h])
+            k_grad = k_grad + dot_tn(score_grad, queries * head_rows[h])
+            v_grad = v_grad + dot_tn(probs.astype(BF16), mixed_here)
+        scale = HEAD_DIM ** (-0.5)
+        r.dqkv[0] = (q_grad * scale).astype(BF16)
+        r.dqkv[1] = (k_grad * scale).astype(BF16)
+        r.dqkv[2] = v_grad.astype(BF16)
+        finish = reduce_rows(sum(dot_nn(r.dqkv[i], r.w_attn[l, i]) for i in range(3)))
+
+        def store_a(m):
+            def store(block, rows, value):
+                r.grad_a[l, block, m, rows, :] = value
+
+            return store
+
+        for i in range(3):
+            weight_grad(r.normed.at[l], r.dqkv[i], store_a(i))
+        weight_grad(r.low2.at[l], r.mixed[l], store_a(3))
+        pair_a = hand_over(l, (fam_a,))
+        for row, i in ((9, 0), (10, 2)):
+            r.small[l, row : row + 1, : z.heads_w] = jnp.sum(r.dqkv[i].astype(F32), axis=0, keepdims=True)
+        hidden_part, gain_attn, shift_attn = norm_back(r.hidden[l], r.gains[l, 0:1], finish())
+        hidden_grad = r.tmp[...] + hidden_part
+        r.tmp[...] = hidden_grad
+        r.small[l, 0:1, :] = gain_attn
+        r.small[l, 2:3, :] = shift_attn
+        small_key = owe_small(l)
+        query_den = 1.0 + jnp.sum(r.qdots[l], axis=1, keepdims=True)
+        high, low = split(hidden_grad / query_den)
+        den_grad = -jnp.sum((hidden_grad / query_den) * r.recall[l], axis=1, keepdims=True)
+        highs = [high[:, u * z.val_w : (u + 1) * z.val_w] for u in range(T)]
+        lows = [low[:, u * z.val_w : (u + 1) * z.val_w] for u in range(T)]
+        dots_high, dots_low = split(r.qdots[l])
+        for u in range(T):
+            r.x1_src[l, u] = dot_tn(dots_high, highs[u]) + dot_tn(dots_high, lows[u]) + dot_tn(dots_low, highs[u])
+        value_step = to_parts(lambda peer: r.x1_src.at[l, peer], lambda i: r.x1_dst.at[l, i - 1])
+        dots_grad = sum(dot_nt(highs[u], r.uall[l, u]) + dot_nt(lows[u], r.uall[l, u]) for u in range(T)) + den_grad
+        dots_grad = (dots_grad * row_mask).astype(BF16)
+        key_direct = feature_map_back(r.keyb[l].astype(F32), dot_tn(dots_grad, r.phiq[l]))
+        for u in range(T):
+            r.x2_src[l, u] = key_direct[:, u * z.keys_w : (u + 1) * z.keys_w]
+        key_step = to_parts(lambda peer: r.x2_src.at[l, peer], lambda i: r.x2_dst.at[l, i - 1])
+        arrive(value_step)
+        r.x1_mid[l] = r.x1_src[l, t] + sum(r.x1_dst[l, i] for i in range(T - 1))
+        value_step = to_segs(lambda _: r.x1_mid.at[l], lambda i: r.x1_far.at[l, i - 1])
+        arrive(key_step)
+        r.x2_mid[l] = r.x2_src[l, t] + sum(r.x2_dst[l, i] for i in range(T - 1))
+        key_step = to_segs(lambda _: r.x2_mid.at[l], lambda i: r.x2_far.at[l, i - 1])
+        query_grad = feature_map_back(r.qmem[l].astype(F32), dot_nn(dots_grad, r.phik[l])).astype(BF16)
+        for u in range(T):
+            r.dq_src[l, u] = query_grad[:, u * z.keys_w : (u + 1) * z.keys_w]
+        r.dq_all[l, own, :] = r.dq_src[l, t]
+        query_step = to_parts(lambda peer: r.dq_src.at[l, peer], lambda i: r.dq_all.at[l, own])
+        if l == 0:
+            arrive((12, 0, 0))
+            arrive((12, 0, 1))
+        r.tmp[...] += dot_nn(query_grad, r.w_keys[l, 0])
+        arrive(value_step)
+        direct = r.x1_mid[l] + sum(r.x1_far[l, i] for i in range(S - 1))
+        key_dots = r.kdots[l]
+        key_den = 1.0 + jnp.sum(key_dots, axis=1, keepdims=True)
+        r.vgrad[...] = direct
+        for k in range(S - 1, 0, -1):
+            rows = slice(k * MEM, (k + 1) * MEM)
+            back = -r.vgrad[rows, :] / key_den[rows]
+            r.vgrad[...] += dot_tn(key_dots[rows].astype(BF16), back.astype(BF16))
+        value_grad = r.vgrad[...]
+        read = r.vpart[l] - r.upart[l]
+        back = (-value_grad / key_den).astype(BF16)
+        key_den_grad = -jnp.sum(back.astype(F32) * read, axis=1, keepdims=True)
+        key_dots_grad = (dot_nt(back, r.upart[l].astype(BF16)) + key_den_grad) * key_mask
+        both = (key_dots_grad + key_dots_grad.T).astype(BF16)
+        key_solve = feature_map_back(r.keyb[l].astype(F32), dot_nn(both, r.phik[l]))
+        r.ksolve[...] = key_solve
+        r.dv[...] = value_grad.astype(BF16)
+        arrive(key_step)
+        r.dk_direct[...] = r.x2_mid[l] + sum(r.x2_far[l, i] for i in range(S - 1))
+        tail = dot_nn(r.dv[seg_rows, :], r.w_value[l])
+        tail = tail + dot_nn(r.dk_direct[seg_rows, :].astype(BF16), r.w_keys[l, 1, shard_rows(t), :])
+        tail = tail + dot_nn(r.ksolve[seg_rows, :].astype(BF16), r.w_keys[l, 1])
+        r.x3_src[l] = tail.astype(BF16)
+        base, place = alloc(T - 1), alloc(1)
+
+        for i in range(1, T):
+
+            @pl.when(tpeers[i] == T - 1)
+            def _():
+                copy = pltpu.make_async_remote_copy(
+                    src_ref=r.x3_src.at[l], dst_ref=r.x3_dst.at[l, i - 1], send_sem=r.send.at[place],
+                    recv_sem=r.recv.at[base + i - 1], device_id=(c, s, tpeers[i]), device_id_type=MESH,
+                )
+                copy.start()
+
+        def drain():
+            @pl.when(t != T - 1)
+            def _():
+                wait_bytes(r.x3_src.at[l], r.send.at[place])
+
+        sent.append((drain, drain))
+        for u in range(T):
+            r.x4_src[l, u] = key_solve[:, u * z.keys_w : (u + 1) * z.keys_w]
+        solve_step = to_parts(lambda peer: r.x4_src.at[l, peer], lambda i: r.x4_dst.at[l, i - 1])
+        add_and_spread(l, (fam_a,), pair_a)
+
+        @pl.when(t == T - 1)
+        def _():
+            total = r.x3_src[l].astype(F32)
+            for i in range(T - 1):
+                wait_bytes(r.x3_dst.at[l, i], r.recv.at[base + i])
+                total = total + r.x3_dst[l, i].astype(F32)
+            r.tmp[C - MEM :, :] += total
+
+        target = r.gfull.at[0] if l == 1 else r.final
+        target[own, :] = r.tmp[...].astype(BF16)
+        rows_step = to_parts(lambda _: target.at[own], lambda i: target.at[own])
+        arrive(query_step)
+        if l == 1:
+            arrive(row_step)
+        weight_grad(r.xfull.at[l], r.dq_all[l], lambda block, rows, value: r.grad_q.__setitem__((l, block, rows, slice(None)), value))
+        pair_q = hand_over(l, (fam_q,))
+        r.mem_v[l] = dot_tn(r.mem_rows[l], r.dv[...])
+        arrive(solve_step)
+        key_grad = r.dk_direct[...] + r.x4_src[l, t] + sum(r.x4_dst[l, i] for i in range(T - 1))
+        r.mem_k[l] = dot_tn(r.mem_rows[l], key_grad.astype(BF16))
+        rows = pl.ds(pl.multiple_of(s * z.cut, 8), z.cut)
+        mem_copies = [pair_send(r.mem_k.at[l, rows], r.pair_k), pair_send(r.mem_v.at[l, rows], r.pair_v)]
+
+        @pl.when(c != l)
+        def _():
+            for copy in mem_copies:
+                copy.start()
+
+        sent.extend((copy, c != l) for copy in mem_copies)
+        mem_key = owe_owner(l, mem_copies)
+        small_key = small_parts(l, small_key)
+        add_and_spread(l, (fam_q,), pair_q)
+        arrive(rows_step)
+        return mem_key, small_key
+
+    forward(0)
+    row_step = forward(1)
+    for l in range(LAYERS):
+        r.small[l] = jnp.zeros((16, D), F32)
+    mem_key1, small_key1 = backward(1)
+    mem_key0, small_key0 = backward(0)
+
+    r.input_grad[0] = r.final[...]
+    l = c
+
+    small_key1, small_key0 = small_segs(1, small_key1), small_segs(0, small_key0)
+    arrive(mem_key1)
+    arrive(mem_key0)
+    rows = pl.ds(pl.multiple_of(s * z.cut, 8), z.cut)
+    r.mkey_grads[0, 1] = r.mem_k[l, rows, :] + r.pair_k[...]
+    r.mvalue_grads[0] = r.mem_v[l, rows, :] + r.pair_v[...]
+
+    families = (fam_f, fam_a, fam_q)
+
+    def far_sum(family, m=None):
+        grad, _, far = families[family]
+        pick = (slice(0, z.cut), slice(None)) if m is None else (m, slice(0, z.cut), slice(None))
+        total = grad[(l, s) + pick].astype(F32)
+        for i in range(S - 1):
+            total = total + far[(i,) + pick].astype(F32)
+        return total
+
+    for family in range(3):
+
+        for layer in range(LAYERS):
+            arrive((id(families[family][2]), layer))
+        if family == 0:
+            r.fc_grads[0] = far_sum(0, 0)
+            r.proj_grads[0] = far_sum(0, 1)
+        elif family == 1:
+            for i in range(3):
+                r.attn_grads[0, i] = far_sum(1, i)
+            r.out_grads[0] = far_sum(1, 3).T
+        else:
+            r.mkey_grads[0, 0] = far_sum(2)
+    arrive(small_key1)
+    arrive(small_key0)
+    total = r.seg_small[0]
+    for i in range(1, S):
+        total = total + r.seg_small[i]
+    r.gain_grads[0] = total[0:2]
+    r.shift_grads[0] = total[2:4]
+    r.obias_grads[0] = total[4:6]
+    r.fcb_grads[...] = total[8:9, : z.units]
+    r.abias_grads[0] = total[9:11, : z.heads_w]
+
+    assert not owed
+    for copy, when in sent:
+        if when is copy:
+            copy()
+        elif when is None:
+            copy.wait_send()
+        else:
+            pl.when(when)(copy.wait_send)
+
+
+def hand_out(*refs):
+    count = len(refs) // 2
+    for source, target in zip(refs[:count], refs[count:]):
+        target[...] = source[...]
+
+
 def item_ids(lengths):
     item_ends = jnp.cumsum(lengths, axis=-1)
     item_begins = item_ends - lengths
@@ -141,14 +951,14 @@
     seg, _ = place
     own_mask = lax.dynamic_slice_in_dim(mask, seg * MEM, 1, 0)
     key_mem = dot_nn(mem_rows, w_k).astype(BF16)
-    phi_key = feature_map(key_mem.astype(F32)).astype(BF16)
+    phi_key = feature_map(key_mem.astype(F32), jnp.roll).astype(BF16)
     key_dots = dot_nt(phi_key, phi_key) * mask
     key_den = 1.0 + jnp.sum(key_dots, axis=1, keepdims=True)
     value_part = dot_nn(mem_rows, w_v)
     solved_part = solve_forward(key_dots, key_den, value_part)
     solved = lax.all_gather(solved_part.astype(BF16), "tensor", axis=1, tiled=True)
     query_mem = dot_nn(own_rows, w_q).astype(BF16)
-    phi_query = feature_map(query_mem.astype(F32)).astype(BF16)
+    phi_query = feature_map(query_mem.astype(F32), jnp.roll).astype(BF16)
     query_dots = dot_nt(phi_query, phi_key) * own_mask
     query_den = 1.0 + jnp.sum(query_dots, axis=1, keepdims=True)
     recall = dot_nn(query_dots.astype(BF16), solved) / query_den
@@ -225,9 +1035,9 @@
     num_grad = (hidden_grad / query_den).astype(BF16)
     den_grad = -jnp.sum(hidden_grad * recall, axis=1, keepdims=True) / query_den
     dots_grad = ((dot_nt(num_grad, solved) + den_grad) * own_mask).astype(BF16)
-    query_grad = feature_map_back(query_mem.astype(F32), dot_nn(dots_grad, phi_key)).astype(BF16)
+    query_grad = feature_map_back(query_mem.astype(F32), dot_nn(dots_grad, phi_key), jnp.roll).astype(BF16)
     solved_direct = dot_tn(query_dots.astype(BF16), num_grad)
-    key_direct = feature_map_back(key_mem.astype(F32), dot_tn(dots_grad, phi_query))
+    key_direct = feature_map_back(key_mem.astype(F32), dot_tn(dots_grad, phi_query), jnp.roll)
     solved_direct = scatter_columns(solved_direct, "tensor")
     solved_direct = jnp.sum(lax.all_gather(solved_direct.astype(BF16), "seg").astype(F32), axis=0)
     value_grad = solve_backward(key_dots, key_den, solved_direct)
@@ -236,7 +1046,7 @@
     back = (-value_grad / key_den).astype(BF16)
     key_dots_grad = (dot_nt(back, solved_part.astype(BF16)) + key_den_grad) * mask
     both = (key_dots_grad + key_dots_grad.T).astype(BF16)
-    key_solve = feature_map_back(key_mem.astype(F32), dot_nn(both, phi_key))
+    key_solve = feature_map_back(key_mem.astype(F32), dot_nn(both, phi_key), jnp.roll)
     mine = (jnp.arange(key_solve.shape[0]) // MEM == seg)[:, None]
     key_direct = key_direct + jnp.where(mine, key_solve, 0.0)
     key_direct = scatter_columns(key_direct, "tensor")
@@ -253,7 +1063,7 @@
     )
 
 
-def per_device(
+def general_device(
     inputs, out_grad, item_lengths, norm_gains, norm_biases, w_attn, attn_bias, w_out, out_biases, w_fc, fc_bias,
     w_proj, w_mem_keys, w_mem_value,
 ):
@@ -331,8 +1141,49 @@
 
 
 def solution(mesh):
+    def per_device(*args):
+        inputs, out_grad, item_lengths = args[:3]
+        S, T = mesh.shape["seg"], mesh.shape["tensor"]
+        w_attn, w_fc, w_keys = args[5], args[9], args[12]
+        z = Sizes(
+            mesh,
+            (
+                (0, inputs.shape[1] * S, inputs.shape[2]), (0, 0, 0, w_attn.shape[3] * T), (0, 0, w_fc.shape[2] * T),
+                (0, 0, 0, w_keys.shape[3] * T),
+            ),
+        )
+        scratch = scratch_of(z)
+        D = z.width
+        outs = dict(
+            input_grad=((1, z.rows, D), BF16), gain_grads=((1, 2, D), F32), shift_grads=((1, 2, D), F32),
+            attn_grads=((1, 3, z.cut, z.heads_w), F32), abias_grads=((1, 2, z.heads_w), F32),
+            out_grads=((1, z.heads_w, z.cut), F32), obias_grads=((1, 2, D), F32), fc_grads=((1, z.cut, z.units), F32),
+            fcb_grads=((1, z.units), F32), proj_grads=((1, z.cut, z.units), F32),
+            mkey_grads=((1, 2, z.cut, z.keys_w), F32), mvalue_grads=((1, z.cut, z.val_w), F32),
+        )
+        names = tuple(scratch)
+        vmem, anywhere = pl.BlockSpec(memory_space=pltpu.VMEM), pl.BlockSpec(memory_space=pl.ANY)
+        shapes = [jax.ShapeDtypeStruct(*shape) for shape in outs.values()]
+        flip = lambda w: jnp.swapaxes(w, -1, -2)
+        results = pl.pallas_call(
+            functools.partial(kernel, z, names),
+            out_shape=shapes,
+            in_specs=[anywhere, anywhere, pl.BlockSpec(memory_space=pltpu.SMEM)] + [anywhere] * 11,
+            out_specs=[vmem] * len(outs),
+            scratch_shapes=list(scratch.values()),
+            compiler_params=pltpu.CompilerParams(
+                collective_id=0, has_side_effects=True, vmem_limit_bytes=63 * 2**20
+            ),
+            name="two_layers",
+        )(*args[:5], flip(w_attn), *args[6:12], flip(w_keys), flip(args[13]))
+        results = list(pl.pallas_call(
+            hand_out, out_shape=shapes, in_specs=[vmem] * len(outs), out_specs=[vmem] * len(outs), name="hand_out"
+        )(*results))
+        results[9] = flip(results[9])
+        return tuple(results)
+
     return jax.shard_map(
-        per_device,
+        per_device if mesh.shape["seg"] * MEM <= 128 else general_device,
         mesh=mesh,
         in_specs=(
             P(None, "seg", None),

time: 807 us -> 222 us (0.28); the launches traced: 792 us -> 222 us
  blocking collectives: 406 us -> 0 us
  Pallas kernels: 0 us -> 222 us
  matrix products: 86.9 us -> 0 us
  other arithmetic: 74.6 us -> 0 us
  starting transfers between devices: 73.5 us -> 0 us
  local copies, waits for them, and re-layouts: 72.7 us -> 0 us
  waiting for transfers between devices: 60.2 us -> 0 us
  between operations: 18.7 us -> 0.76 us
    all_gather x29 -> x0, blocking collectives: 297 us -> none  [the longest x11 111 us: gather_rows(): return lax.all_gather(values, axis, axis=0, tiled=True)]
    pallas_call x0 -> x2, Pallas kernels: none -> 222 us  [the longest x1 218 us: per_device(): pl.pallas_call(functools.partial(kernel, z, names), out_shape=shapes, in_...]
    dot_general x119 -> x0, matrix products: 86.9 us -> none  [the longest x40 33.6 us: dot_tn(): lax.dot_general(left, right, (((0,), (0,)), ((), ())), preferred_element_...]
    psum x2 -> x0, blocking collectives: 84.9 us -> none  [the longest x1 72.6 us: per_device(): lax.psum(over_layers([jnp.concatenate(r, axis=0) for r in rows_grads]), (...]
    all_to_all x19 -> x0, starting transfers between devices: 73.2 us -> none  [the longest x7 27.2 us: scatter_rows(): got = lax.all_to_all(pieces, axis, 0, 0, tiled=True)]
    all_to_all x19 -> x0, waiting for transfers between devices: 58.2 us -> none  [the longest x5 33.8 us: spread(): got = lax.all_to_all(cut, 'seg', axis, axis, tiled=True)]
    reduce_sum x53 -> x0, other arithmetic: 42.7 us -> none  [the longest x4 6 us: norm_back(): jnp.sum(grad, axis=0, keepdims=True)]
    unnamed x572 -> x0, local copies, waits for them, and re-layouts: 22.2 us -> none
  transfers between devices with their start and end apart: 26 -> 0, of which waited for: 13 -> 0; matrix products, arithmetic and copies ran while one was open for 17% -> 0% of each run, Pallas kernels for 0% -> 0%
where the time goes in v2:
time: 222 us
  Pallas kernels  222 us (100%)
    pallas_call x1, Pallas kernels, per_device(): pl.pallas_call(functools.partial(kernel, z, names), out_shape=shapes, in_...  218 us

profile of v2, /device:TPU:0, one launch (start us, length us, event | category | flops | bytes accessed | tf_op | source)
XLA Modules:
  0.0 222.3 jit_solution(16020164810418340597)
XLA Ops:
  0.6 218.2 %two_layers.1 = (bf16[1,256,768]{2,1,0:T(8,128)(2,1)}, f32[1,2,768]{2,1,0:T(2,128)}, f32[1,2,768]{2,1,0:T(2,128)}, f32[1,3,192,192]{3,2,1,0:T(8,128)}, f32[1,2,1...) custom-call(bf16[2,256,768]{2,1,0:T(8,128)(2,1)} %refs_0_.1, ...), custom_call_target="tpu_custom_call" | custom-call | tf_op jit(solution)/shard_map/two_layers/pallas_call | solution.py:1168
  218.9 3.3 %hand_out.1 = (bf16[1,256,768]{2,1,0:T(8,128)(2,1)}, f32[1,2,768]{2,1,0:T(2,128)}, f32[1,2,768]{2,1,0:T(2,128)}, f32[1,3,192,192]{3,2,1,0:T(8,128)}, f32[1,2,192...) custom-call(bf16[1,256,768]{2,1,0:T(8,128)(2,1)} %get-tuple-element., ...), custom_call_target="tpu_custom_call" | custom-call | tf_op jit(solution)/shard_map/hand_out/pallas_call | solution.py:1179

commit v3 on v2

--- a/solution.py
+++ b/solution.py
@@ -116,6 +116,7 @@
         self.val_w = self.width // self.parts
         self.cut = self.width // self.segs
         self.cut_pad = -(-self.cut // 16) * 16
+        self.pieces = 4 if self.cut_pad % 64 == 0 else 1
         self.sems = 120 + 48 * self.parts + 2 * self.segs * (self.parts + 16)
 
 
@@ -138,9 +139,11 @@
         x2_src=fl(2, T, M, z.keys_w), x2_dst=fl(2, T - 1, M, z.keys_w), x2_mid=fl(2, M, z.keys_w), x2_far=fl(2, max(S - 1, 1), M, z.keys_w), x4_src=fl(2, T, M, z.keys_w), x4_dst=fl(2, T - 1, M, z.keys_w), ksolve=fl(M, z.keys), dk_direct=fl(M, z.keys_w),
         dq_src=bf(2, T, C, z.keys_w), dq_all=bf(2, R, z.keys_w), dv=bf(M, z.val_w), vgrad=fl(M, z.val_w),
         x3_src=bf(2, MEM, D), x3_dst=bf(2, T - 1, MEM, D), final=bf(R, D), tmp=fl(C, D),
-        grad_f=bf(2, S, 2, z.cut_pad, D), grad_a=bf(2, S, 4, z.cut_pad, z.heads_w), grad_q=bf(2, S, z.cut_pad, z.keys_w),
-        pair_f=bf(S, 2, z.cut_pad, D), pair_a=bf(S, 4, z.cut_pad, z.heads_w), pair_q=bf(S, z.cut_pad, z.keys_w),
-        far_f=bf(max(S - 1, 1), 2, z.cut_pad, D), far_a=bf(max(S - 1, 1), 4, z.cut_pad, z.heads_w), far_q=bf(max(S - 1, 1), z.cut_pad, z.keys_w),
+        grad_p=bf(2, S, z.cut_pad, z.units), grad_c=bf(2, S, z.cut_pad, z.units), grad_qk=bf(2, S, z.cut_pad, 2 * z.heads_w),
+        grad_vo=bf(2, S, z.cut_pad, 2 * z.heads_w), grad_q=bf(2, S, z.cut_pad, z.keys_w),
+        pair_f=bf(2, S, z.cut_pad, z.units), pair_a=bf(2, S, z.cut_pad, 2 * z.heads_w), pair_q=bf(2, S, z.cut_pad, z.keys_w),
+        far_p=bf(S, z.cut_pad, z.units), far_c=bf(S, z.cut_pad, z.units), far_qk=bf(S, z.cut_pad, 2 * z.heads_w),
+        far_vo=bf(S, z.cut_pad, 2 * z.heads_w), far_q=bf(S, z.cut_pad, z.keys_w), dqk=bf(R, 2 * z.heads_w),
         mem_k=fl(2, D, z.keys_w), mem_v=fl(2, D, z.val_w), pair_k=fl(z.cut, z.keys_w), pair_v=fl(z.cut, z.val_w),
         small=fl(2, 16, D), pair_small=fl(16, D), part_small=fl(T, 8, D), seg_small=fl(S, 16, D),
         send=pltpu.SemaphoreType.DMA((z.sems,)), recv=pltpu.SemaphoreType.DMA((z.sems,)), load=pltpu.SemaphoreType.DMA((14, 2)),
@@ -234,14 +237,29 @@
         sent.extend((copy, None) for copy in copies)
         return owe(copies)
 
-    def arrive(key):
+    def arrive(key, pieces=0):
+        pump(pieces)
         owed.pop(key)()
+
+    queues = [], []
+
+    def pump(pieces):
+        for core, queue in enumerate(queues):
+            now = queue[:pieces]
+            del queue[:pieces]
+
+            def start():
+                for copy in now:
+                    copy.start()
+
+            if now:
+                pl.when(c == core)(start)
 
     def wait_load(ref, layer):
         arrive((id(ref), layer))
 
     barrier = pltpu.get_barrier_semaphore()
-    greeted = [(other, s, t)] + [(c, to_seg[i], tpeers[j]) for i in range(S) for j in range(T) if i or j]
+    greeted = [(other, to_seg[i], t) for i in range(S)] + [(c, to_seg[i], tpeers[j]) for i in range(S) for j in range(T) if i or j]
     for device in greeted:
         pl.semaphore_signal(barrier, inc=1, device_id=device, device_id_type=MESH)
 
@@ -260,10 +278,22 @@
         pltpu.make_async_copy(
             r.w_keys_in.at[0, which], r.w_keys.at[c, which, shard_rows(t)], r.shard.at[c, which, 0]
         ).start()
-    for kind, (held, source) in enumerate(loads):
-        pltpu.make_async_copy(source, held.at[c], r.load.at[kind, c]).start()
-        for layer in range(LAYERS):
-            owed[id(held), layer] = functools.partial(wait_bytes, held.at[layer], r.load.at[kind, layer])
+    def load_own(kinds):
+        for kind in kinds:
+            held, source = loads[kind]
+            pltpu.make_async_copy(source, held.at[c], r.load.at[kind, c]).start()
+
+    def load_other(kinds):
+        for kind in kinds:
+            held, source = loads[kind]
+            copy = remote(source, held.at[c], pair_base + kind, (other, s, t), r.load.at[kind, c])
+            copy.start()
+            sent.append((copy, None))
+            for layer in range(LAYERS):
+                owed[id(held), layer] = functools.partial(wait_bytes, held.at[layer], r.load.at[kind, layer])
+
+    early, middle = range(0, 5), range(5, 7)
+    load_own(range(len(loads)))
     grad_copy = pltpu.make_async_copy(r.out_grad.at[c], r.gfull.at[1], r.load.at[11, 0])
     grad_copy.start()
     owed[1] = grad_copy.wait
@@ -325,10 +355,7 @@
         for layer in range(LAYERS):
             owed[10, layer, which] = functools.partial(shard_wait, layer, which, 0)
     pair_base = alloc(len(loads))
-    for kind, (held, source) in enumerate(loads):
-        copy = remote(source, held.at[c], pair_base + kind, (other, s, t), r.load.at[kind, c])
-        copy.start()
-        sent.append((copy, None))
+    load_other(early)
 
     row_seg = lax.broadcasted_iota(jnp.int32, (M, 1), 0) // MEM
     col_seg = lax.broadcasted_iota(jnp.int32, (1, M), 1) // MEM
@@ -357,7 +384,7 @@
         )
 
         def finish():
-            arrive(copies)
+            arrive(copies, 2)
             total = r.rs_own[own, :]
             for i in range(T - 1):
                 total = total + r.rs_dst[k, i].astype(F32)
@@ -384,6 +411,7 @@
             mems = r.mem_rows[0]
             r.k_parts[t] = dot_nt(mems, r.w_keys[0, 1, own_shard, :]).astype(BF16)
             key_step = to_parts(lambda _: r.k_parts.at[t], lambda i: r.k_parts.at[t])
+            load_other(middle)
             arrive(query_step)
             queries_mem = jnp.concatenate([r.q_parts[u] for u in range(T)], axis=1)
         else:
@@ -438,15 +466,15 @@
         unit, _ = norm_rows(hidden)
         r.normed[l, own, :] = (unit * r.gains[l, 0:1] + r.shifts[l, 0:1]).astype(BF16)
         shared = share_rows(r.normed, l)
+        if l == 0:
+            load_other([9, 7])
         wait_load(r.w_attn, l)
         wait_load(r.w_out, l)
         arrive(shared)
         if l == 0:
             spread_shard(1, 0)
-            row_step = None
         else:
             spread_shard(0, 1)
-            row_step = share_rows(r.xfull, 1)
         normed = r.normed[l]
         queries = (dot_nt(normed, r.w_attn[l, 0]) + r.attn_bias[l, 0:1]).astype(BF16)
         key_heads = dot_nt(normed, r.w_attn[l, 1]).astype(BF16)
@@ -466,6 +494,8 @@
         mixed = mixed.astype(BF16)
         r.mixed[l] = mixed
         finish = reduce_rows(dot_nn(mixed, r.w_out[l]))
+        if l == 0:
+            load_other([8])
         after = r.hidden[l] + finish() + r.out_biases[l, 0:1]
         r.after[l] = after
         unit, _ = norm_rows(after)
@@ -478,6 +508,7 @@
             forward_shard(1, 1)
             forward_shard(1, 0)
         arrive(shared)
+        row_step = share_rows(r.xfull, 1) if l == 1 else None
         pre = dot_nn(r.normed_mlp[l], r.w_fc[l]) + r.fc_bias[l]
         activation, slope = gelu_and_slope(pre)
         activation = activation.astype(BF16)
@@ -521,7 +552,9 @@
             sent.append((drain, drain))
         return row_step
 
-    fam_f, fam_a, fam_q = (r.grad_f, r.pair_f, r.far_f), (r.grad_a, r.pair_a, r.far_a), (r.grad_q, r.pair_q, r.far_q)
+    fam_p, fam_c = (r.grad_p, r.pair_f, r.far_p, 0), (r.grad_c, r.pair_f, r.far_c, 1)
+    fam_qk, fam_vo = (r.grad_qk, r.pair_a, r.far_qk, 0), (r.grad_vo, r.pair_a, r.far_vo, 1)
+    fam_q = (r.grad_q, r.pair_q, r.far_q, None)
 
     def blocks_of(first_row, count):
         row, pieces = first_row, []
@@ -532,27 +565,28 @@
             row += size
         return pieces
 
-    def weight_grad(left, right, store):
+    def weight_grad(l, family, *pairs):
         stripe = min(256, D)
         for k in range(0, D, stripe):
-            grad = dot_tn(left[:, k : k + stripe], right).astype(BF16)
+            parts = [dot_tn(left[:, k : k + stripe], right).astype(BF16) for left, right in pairs]
+            grad = parts[0] if len(parts) == 1 else jnp.concatenate(parts, axis=1)
             for block, inside, row, size in blocks_of(k, stripe):
-                store(block, slice(inside, inside + size), grad[row : row + size])
+                family[0][l, block, inside : inside + size, :] = grad[row : row + size]
 
     def pair_send(src, dst):
         index = alloc(1)
         return remote(src, dst, index, (other, s, t))
 
-    def hand_over(l, names):
-        copies = [pair_send(grad.at[l], pair) for grad, pair, _ in names]
-
-        @pl.when(c != l)
-        def _():
-            for copy in copies:
-                copy.start()
-
-        sent.extend((copy, c != l) for copy in copies)
-        return owe_owner(l, copies)
+    def adder_of(l, family):
+        return l if family[3] is None else family[3]
+
+    def hand_over(l, family):
+        grad, pair, _, _ = family
+        adder = adder_of(l, family)
+        copy = pair_send(grad.at[l], pair.at[l])
+        pl.when(c != adder)(copy.start)
+        sent.append((copy, c != adder))
+        return owe_owner(adder, [copy])
 
     def owe_owner(l, copies):
         def wait():
@@ -564,40 +598,51 @@
         owed[id(copies)] = wait
         return id(copies)
 
-    def add_and_spread(l, names, copies):
-        bases = [alloc(S - 1) for _ in names]
-        arrive(copies)
-
-        @pl.when(c == l)
+    def add_pair(l, family, key):
+        grad, pair, _, _ = family
+        arrive(key)
+
+        @pl.when(c == adder_of(l, family))
         def _():
-            for (grad, pair, far), base in zip(names, bases):
-
-                @pl.loop(0, S)
-                def _(j):
-                    if len(grad.shape) == 4:
-                        grad[l, j] = (grad[l, j].astype(F32) + pair[j].astype(F32)).astype(BF16)
-                    else:
-                        for m in range(grad.shape[2]):
-                            grad[l, j, m] = (grad[l, j, m].astype(F32) + pair[j, m].astype(F32)).astype(BF16)
-
-                for i in range(1, S):
-                    remote(grad.at[l, to_seg[i]], far.at[i - 1], base + i - 1, (c, to_seg[i], t)).start()
-
-        for (grad, _, far), base in zip(names, bases):
-            owed[id(far), l] = functools.partial(far_wait, l, far, base)
-            sent.append((functools.partial(far_drain, l, grad, base),) * 2)
-
-    def far_wait(l, far, base):
-        @pl.when(c == l)
+            @pl.loop(0, S)
+            def _(j):
+                grad[l, j] = (grad[l, j].astype(F32) + pair[l, j].astype(F32)).astype(BF16)
+
+    def spread(l, family):
+        grad, _, far, _ = family
+        adder = adder_of(l, family)
+        base = alloc(S)
+        near = adder == l
+
+        @pl.when(c == adder)
         def _():
-            for i in range(1, S):
-                wait_bytes(far.at[i - 1], r.recv.at[base + i - 1])
-
-    def far_drain(l, grad, base):
-        @pl.when(c == l)
-        def _():
-            for i in range(1, S):
-                wait_bytes(grad.at[l, 0], r.send.at[base + i - 1])
+            if near:
+                far[0] = grad[l, s]
+            else:
+                remote(grad.at[l, s], far.at[0], base, (other, s, t)).start()
+
+        size = z.cut_pad if z.cut_pad * grad.shape[3] <= 20000 else z.cut_pad // z.pieces
+        for i in range(S - 1, 0, -1):
+            for first in range(0, z.cut_pad, size):
+                piece = pl.ds(first, size)
+                copy = remote(grad.at[l, to_seg[i], piece], far.at[i, piece], base + i, (l, to_seg[i], t))
+                queues[adder].append(copy)
+        pump(1000)
+
+        def wait():
+            @pl.when(c == l)
+            def _():
+                for i in range(1 if near else 0, S):
+                    wait_bytes(far.at[i], r.recv.at[base + i])
+
+        def drain():
+            @pl.when(c == adder)
+            def _():
+                for i in range(1 if near else 0, S):
+                    wait_bytes(far.at[i], r.send.at[base + i])
+
+        owed[id(far), l] = wait
+        sent.append((drain, drain))
 
     def owe_small(l):
         copy = pair_send(r.small.at[l], r.pair_small)
@@ -651,19 +696,16 @@
         finish = reduce_rows(dot_nt(pre_grad, r.w_fc[l]))
         own_grad = r.gfull[l, own, :].astype(F32)
 
-        def store_f(m):
-            def store(block, rows, value):
-                r.grad_f[l, block, m, rows, :] = value
-
-            return store
-
-        weight_grad(r.normed_mlp.at[l], r.dpre[...], store_f(0))
-        weight_grad(r.gfull.at[l], r.act[l], store_f(1))
+        weight_grad(l, fam_p, (r.gfull.at[l], r.act[l]))
+        pair_p = hand_over(l, fam_p)
+        weight_grad(l, fam_c, (r.normed_mlp.at[l], r.dpre[...]))
+        pair_c = hand_over(l, fam_c)
         r.small[l, 8:9, :] = jnp.sum(r.dpre[...].astype(F32), axis=0, keepdims=True)
-        pair_f = hand_over(l, (fam_f,))
         if l == 1:
             forward_shard(0, 0)
             forward_shard(0, 1)
+        add_pair(l, fam_p, pair_p)
+        spread(l, fam_p)
         after_part, gain_mlp, shift_mlp = norm_back(r.after[l], r.gains[l, 1:2], finish())
         after_grad = own_grad + after_part
         r.tmp[...] = after_grad
@@ -673,8 +715,11 @@
         r.small[l, 3:4, :] = shift_mlp
         r.small[l, 4:5, :] = jnp.sum(after_grad, axis=0, keepdims=True)
         r.small[l, 5:6, :] = jnp.sum(own_grad, axis=0, keepdims=True)
-        add_and_spread(l, (fam_f,), pair_f)
-        arrive(shared)
+        add_pair(l, fam_c, pair_c)
+        if l == 0:
+            spread(l, fam_c)
+        arrive(shared, 2)
+        pump(2)
         after_low = r.low2[l]
         mixed_grad = dot_nt(after_low, r.w_out[l]).astype(BF16)
         queries, key_heads, values = r.qkv[l, 0], r.qkv[l, 1], r.qkv[l, 2]
@@ -692,18 +737,13 @@
         r.dqkv[0] = (q_grad * scale).astype(BF16)
         r.dqkv[1] = (k_grad * scale).astype(BF16)
         r.dqkv[2] = v_grad.astype(BF16)
+        r.dqk[...] = jnp.concatenate([r.dqkv[0], r.dqkv[1]], axis=1)
         finish = reduce_rows(sum(dot_nn(r.dqkv[i], r.w_attn[l, i]) for i in range(3)))
 
-        def store_a(m):
-            def store(block, rows, value):
-                r.grad_a[l, block, m, rows, :] = value
-
-            return store
-
-        for i in range(3):
-            weight_grad(r.normed.at[l], r.dqkv[i], store_a(i))
-        weight_grad(r.low2.at[l], r.mixed[l], store_a(3))
-        pair_a = hand_over(l, (fam_a,))
+        weight_grad(l, fam_qk, (r.normed.at[l], r.dqk[...]))
+        pair_qk = hand_over(l, fam_qk)
+        weight_grad(l, fam_vo, (r.normed.at[l], r.dqkv[2]), (r.low2.at[l], r.mixed[l]))
+        pair_vo = hand_over(l, fam_vo)
         for row, i in ((9, 0), (10, 2)):
             r.small[l, row : row + 1, : z.heads_w] = jnp.sum(r.dqkv[i].astype(F32), axis=0, keepdims=True)
         hidden_part, gain_attn, shift_attn = norm_back(r.hidden[l], r.gains[l, 0:1], finish())
@@ -727,12 +767,15 @@
         for u in range(T):
             r.x2_src[l, u] = key_direct[:, u * z.keys_w : (u + 1) * z.keys_w]
         key_step = to_parts(lambda peer: r.x2_src.at[l, peer], lambda i: r.x2_dst.at[l, i - 1])
-        arrive(value_step)
+        add_pair(l, fam_qk, pair_qk)
+        add_pair(l, fam_vo, pair_vo)
+        arrive(value_step, 2)
         r.x1_mid[l] = r.x1_src[l, t] + sum(r.x1_dst[l, i] for i in range(T - 1))
         value_step = to_segs(lambda _: r.x1_mid.at[l], lambda i: r.x1_far.at[l, i - 1])
         arrive(key_step)
         r.x2_mid[l] = r.x2_src[l, t] + sum(r.x2_dst[l, i] for i in range(T - 1))
         key_step = to_segs(lambda _: r.x2_mid.at[l], lambda i: r.x2_far.at[l, i - 1])
+        pump(1)
         query_grad = feature_map_back(r.qmem[l].astype(F32), dot_nn(dots_grad, r.phik[l])).astype(BF16)
         for u in range(T):
             r.dq_src[l, u] = query_grad[:, u * z.keys_w : (u + 1) * z.keys_w]
@@ -742,8 +785,13 @@
             arrive((12, 0, 0))
             arrive((12, 0, 1))
         r.tmp[...] += dot_nn(query_grad, r.w_keys[l, 0])
-        arrive(value_step)
+        arrive(value_step, 1)
         direct = r.x1_mid[l] + sum(r.x1_far[l, i] for i in range(S - 1))
+        arrive(key_step)
+        small_key = small_parts(l, small_key)
+        for family in (fam_c, fam_qk, fam_vo) if l == 1 else (fam_qk, fam_vo):
+            spread(l, family)
+        pump(4)
         key_dots = r.kdots[l]
         key_den = 1.0 + jnp.sum(key_dots, axis=1, keepdims=True)
         r.vgrad[...] = direct
@@ -760,7 +808,6 @@
         key_solve = feature_map_back(r.keyb[l].astype(F32), dot_nn(both, r.phik[l]))
         r.ksolve[...] = key_solve
         r.dv[...] = value_grad.astype(BF16)
-        arrive(key_step)
         r.dk_direct[...] = r.x2_mid[l] + sum(r.x2_far[l, i] for i in range(S - 1))
         tail = dot_nn(r.dv[seg_rows, :], r.w_value[l])
         tail = tail + dot_nn(r.dk_direct[seg_rows, :].astype(BF16), r.w_keys[l, 1, shard_rows(t), :])
@@ -787,7 +834,7 @@
         for u in range(T):
             r.x4_src[l, u] = key_solve[:, u * z.keys_w : (u + 1) * z.keys_w]
         solve_step = to_parts(lambda peer: r.x4_src.at[l, peer], lambda i: r.x4_dst.at[l, i - 1])
-        add_and_spread(l, (fam_a,), pair_a)
+        pump(2)
 
         @pl.when(t == T - 1)
         def _():
@@ -800,11 +847,13 @@
         target = r.gfull.at[0] if l == 1 else r.final
         target[own, :] = r.tmp[...].astype(BF16)
         rows_step = to_parts(lambda _: target.at[own], lambda i: target.at[own])
+        small_key = small_segs(l, small_key)
+        pump(4)
         arrive(query_step)
         if l == 1:
             arrive(row_step)
-        weight_grad(r.xfull.at[l], r.dq_all[l], lambda block, rows, value: r.grad_q.__setitem__((l, block, rows, slice(None)), value))
-        pair_q = hand_over(l, (fam_q,))
+        weight_grad(l, fam_q, (r.xfull.at[l], r.dq_all[l]))
+        pair_q = hand_over(l, fam_q)
         r.mem_v[l] = dot_tn(r.mem_rows[l], r.dv[...])
         arrive(solve_step)
         key_grad = r.dk_direct[...] + r.x4_src[l, t] + sum(r.x4_dst[l, i] for i in range(T - 1))
@@ -819,8 +868,10 @@
 
         sent.extend((copy, c != l) for copy in mem_copies)
         mem_key = owe_owner(l, mem_copies)
-        small_key = small_parts(l, small_key)
-        add_and_spread(l, (fam_q,), pair_q)
+        add_pair(l, fam_q, pair_q)
+        spread(l, fam_q)
+        if l == 0:
+            pump(100)
         arrive(rows_step)
         return mem_key, small_key
 
@@ -834,36 +885,26 @@
     r.input_grad[0] = r.final[...]
     l = c
 
-    small_key1, small_key0 = small_segs(1, small_key1), small_segs(0, small_key0)
     arrive(mem_key1)
     arrive(mem_key0)
     rows = pl.ds(pl.multiple_of(s * z.cut, 8), z.cut)
     r.mkey_grads[0, 1] = r.mem_k[l, rows, :] + r.pair_k[...]
     r.mvalue_grads[0] = r.mem_v[l, rows, :] + r.pair_v[...]
 
-    families = (fam_f, fam_a, fam_q)
-
-    def far_sum(family, m=None):
-        grad, _, far = families[family]
-        pick = (slice(0, z.cut), slice(None)) if m is None else (m, slice(0, z.cut), slice(None))
-        total = grad[(l, s) + pick].astype(F32)
-        for i in range(S - 1):
-            total = total + far[(i,) + pick].astype(F32)
-        return total
-
-    for family in range(3):
-
-        for layer in range(LAYERS):
-            arrive((id(families[family][2]), layer))
-        if family == 0:
-            r.fc_grads[0] = far_sum(0, 0)
-            r.proj_grads[0] = far_sum(0, 1)
-        elif family == 1:
-            for i in range(3):
-                r.attn_grads[0, i] = far_sum(1, i)
-            r.out_grads[0] = far_sum(1, 3).T
-        else:
-            r.mkey_grads[0, 0] = far_sum(2)
+    def far_sum(far):
+        arrive((id(far), 1))
+        arrive((id(far), 0))
+        return sum(far[i, : z.cut, :].astype(F32) for i in range(S))
+
+    r.proj_grads[0] = far_sum(r.far_p)
+    r.fc_grads[0] = far_sum(r.far_c)
+    both = far_sum(r.far_qk)
+    r.attn_grads[0, 0] = both[:, : z.heads_w]
+    r.attn_grads[0, 1] = both[:, z.heads_w :]
+    both = far_sum(r.far_vo)
+    r.attn_grads[0, 2] = both[:, : z.heads_w]
+    r.out_grads[0] = both[:, z.heads_w :].T
+    r.mkey_grads[0, 0] = far_sum(r.far_q)
     arrive(small_key1)
     arrive(small_key0)
     total = r.seg_small[0]

time: 222 us -> 208 us (0.937)
  Pallas kernels: 222 us -> 207 us
    pallas_call x1, Pallas kernels: 218 us -> 203 us  [per_device(): pl.pallas_call(functools.partial(kernel, z, names), out_shape=shapes, in_...]
where the time goes in v3:
time: 208 us; the launch traced here: 207 us
  Pallas kernels  207 us (100%)
    pallas_call x1, Pallas kernels, per_device(): pl.pallas_call(functools.partial(kernel, z, names), out_shape=shapes, in_...  203 us

profile of v3, /device:TPU:0, one launch (start us, length us, event | category | flops | bytes accessed | tf_op | source)
XLA Modules:
  0.0 207.5 jit_solution(11451276021728140792)
XLA Ops:
  0.6 203.4 %two_layers.1 = (bf16[1,256,768]{2,1,0:T(8,128)(2,1)}, f32[1,2,768]{2,1,0:T(2,128)}, f32[1,2,768]{2,1,0:T(2,128)}, f32[1,3,192,192]{3,2,1,0:T(8,128)}, f32[1,2,1...) custom-call(bf16[2,256,768]{2,1,0:T(8,128)(2,1)} %refs_0_.1, ...), custom_call_target="tpu_custom_call" | custom-call | tf_op jit(solution)/shard_map/two_layers/pallas_call | solution.py:1209
  204.0 3.3 %hand_out.1 = (bf16[1,256,768]{2,1,0:T(8,128)(2,1)}, f32[1,2,768]{2,1,0:T(2,128)}, f32[1,2,768]{2,1,0:T(2,128)}, f32[1,3,192,192]{3,2,1,0:T(8,128)}, f32[1,2,192...) custom-call(bf16[1,256,768]{2,1,0:T(8,128)(2,1)} %get-tuple-element., ...), custom_call_target="tpu_custom_call" | custom-call | tf_op jit(solution)/shard_map/hand_out/pallas_call | solution.py:1220

commit v4 on v3

--- a/solution.py
+++ b/solution.py
@@ -116,7 +116,6 @@
         self.val_w = self.width // self.parts
         self.cut = self.width // self.segs
         self.cut_pad = -(-self.cut // 16) * 16
-        self.pieces = 4 if self.cut_pad % 64 == 0 else 1
         self.sems = 120 + 48 * self.parts + 2 * self.segs * (self.parts + 16)
 
 
@@ -141,7 +140,7 @@
         x3_src=bf(2, MEM, D), x3_dst=bf(2, T - 1, MEM, D), final=bf(R, D), tmp=fl(C, D),
         grad_p=bf(2, S, z.cut_pad, z.units), grad_c=bf(2, S, z.cut_pad, z.units), grad_qk=bf(2, S, z.cut_pad, 2 * z.heads_w),
         grad_vo=bf(2, S, z.cut_pad, 2 * z.heads_w), grad_q=bf(2, S, z.cut_pad, z.keys_w),
-        pair_f=bf(2, S, z.cut_pad, z.units), pair_a=bf(2, S, z.cut_pad, 2 * z.heads_w), pair_q=bf(2, S, z.cut_pad, z.keys_w),
+        pair_f=bf(2, S, z.cut_pad, z.units), pair_a=bf(2, S, z.cut_pad, 2 * z.heads_w), pair_q=bf(2, S, z.cut_pad, z.keys_w), relay_f=bf(2, 2, z.cut_pad, z.units), relay_a=bf(2, 2, z.cut_pad, 2 * z.heads_w), relay_q=bf(2, 2, z.cut_pad, z.keys_w),
         far_p=bf(S, z.cut_pad, z.units), far_c=bf(S, z.cut_pad, z.units), far_qk=bf(S, z.cut_pad, 2 * z.heads_w),
         far_vo=bf(S, z.cut_pad, 2 * z.heads_w), far_q=bf(S, z.cut_pad, z.keys_w), dqk=bf(R, 2 * z.heads_w),
         mem_k=fl(2, D, z.keys_w), mem_v=fl(2, D, z.val_w), pair_k=fl(z.cut, z.keys_w), pair_v=fl(z.cut, z.val_w),
@@ -237,23 +236,8 @@
         sent.extend((copy, None) for copy in copies)
         return owe(copies)
 
-    def arrive(key, pieces=0):
-        pump(pieces)
+    def arrive(key):
         owed.pop(key)()
-
-    queues = [], []
-
-    def pump(pieces):
-        for core, queue in enumerate(queues):
-            now = queue[:pieces]
-            del queue[:pieces]
-
-            def start():
-                for copy in now:
-                    copy.start()
-
-            if now:
-                pl.when(c == core)(start)
 
     def wait_load(ref, layer):
         arrive((id(ref), layer))
@@ -384,7 +368,7 @@
         )
 
         def finish():
-            arrive(copies, 2)
+            arrive(copies)
             total = r.rs_own[own, :]
             for i in range(T - 1):
                 total = total + r.rs_dst[k, i].astype(F32)
@@ -552,9 +536,14 @@
             sent.append((drain, drain))
         return row_step
 
-    fam_p, fam_c = (r.grad_p, r.pair_f, r.far_p, 0), (r.grad_c, r.pair_f, r.far_c, 1)
-    fam_qk, fam_vo = (r.grad_qk, r.pair_a, r.far_qk, 0), (r.grad_vo, r.pair_a, r.far_vo, 1)
-    fam_q = (r.grad_q, r.pair_q, r.far_q, None)
+    fam_p, fam_c = (r.grad_p, r.pair_f, r.far_p, 0, r.relay_f), (r.grad_c, r.pair_f, r.far_c, 1, r.relay_f)
+    fam_qk, fam_vo = (r.grad_qk, r.pair_a, r.far_qk, 0, r.relay_a), (r.grad_vo, r.pair_a, r.far_vo, 1, r.relay_a)
+    fam_q = (r.grad_q, r.pair_q, r.far_q, None, r.relay_q)
+    on_line = S == 4
+    partner = s + 1 - 2 * lax.rem(s, 2)
+    across = 2 - 2 * lax.div(s, 2)
+    outer = jnp.logical_or(s == 0, s == 3)
+    relays = {}
 
     def blocks_of(first_row, count):
         row, pieces = first_row, []
@@ -581,7 +570,7 @@
         return l if family[3] is None else family[3]
 
     def hand_over(l, family):
-        grad, pair, _, _ = family
+        grad, pair, _, _, _ = family
         adder = adder_of(l, family)
         copy = pair_send(grad.at[l], pair.at[l])
         pl.when(c != adder)(copy.start)
@@ -599,7 +588,7 @@
         return id(copies)
 
     def add_pair(l, family, key):
-        grad, pair, _, _ = family
+        grad, pair, _, _, _ = family
         arrive(key)
 
         @pl.when(c == adder_of(l, family))
@@ -608,41 +597,69 @@
             def _(j):
                 grad[l, j] = (grad[l, j].astype(F32) + pair[l, j].astype(F32)).astype(BF16)
 
-    def spread(l, family):
-        grad, _, far, _ = family
+    def spread(l, family, direct):
+        grad, _, far, _, relay = family
         adder = adder_of(l, family)
-        base = alloc(S)
         near = adder == l
+        direct = direct or not on_line
+        base = alloc(S if direct else 5)
+        steps = range(1, S) if direct else (1, 2)
 
         @pl.when(c == adder)
         def _():
+            if direct:
+                for i in range(S - 1, 0, -1):
+                    remote(grad.at[l, to_seg[i]], far.at[i], base + i, (l, to_seg[i], t)).start()
+            else:
+
+                @pl.when(outer)
+                def _():
+                    for k in range(2):
+                        remote(grad.at[l, across + k], relay.at[l, k], base + 3 + k, (c, partner, t)).start()
+
+                remote(grad.at[l, partner], far.at[1], base + 1, (l, partner, t)).start()
             if near:
                 far[0] = grad[l, s]
             else:
                 remote(grad.at[l, s], far.at[0], base, (other, s, t)).start()
 
-        size = z.cut_pad if z.cut_pad * grad.shape[3] <= 20000 else z.cut_pad // z.pieces
-        for i in range(S - 1, 0, -1):
-            for first in range(0, z.cut_pad, size):
-                piece = pl.ds(first, size)
-                copy = remote(grad.at[l, to_seg[i], piece], far.at[i, piece], base + i, (l, to_seg[i], t))
-                queues[adder].append(copy)
-        pump(1000)
+        if not direct:
+
+            @pl.when(c == l)
+            def _():
+                for i in range(3, S):
+                    far[i] = jnp.zeros(far.shape[1:], BF16)
+
+            def pass_on():
+                @pl.when(jnp.logical_and(c == adder, jnp.logical_not(outer)))
+                def _():
+                    for k in range(2):
+                        wait_bytes(relay.at[l, k], r.recv.at[base + 3 + k])
+                        place = across + k
+                        grad[l, place] = (grad[l, place].astype(F32) + relay[l, k].astype(F32)).astype(BF16)
+                        remote(grad.at[l, place], far.at[2], base + 3 + k, (l, place, t), r.recv.at[base + 2]).start()
+
+            relays[id(far), l] = pass_on
 
         def wait():
             @pl.when(c == l)
             def _():
-                for i in range(1 if near else 0, S):
+                for i in steps if near else (0, *steps):
                     wait_bytes(far.at[i], r.recv.at[base + i])
 
         def drain():
             @pl.when(c == adder)
             def _():
-                for i in range(1 if near else 0, S):
-                    wait_bytes(far.at[i], r.send.at[base + i])
+                ends = tuple(steps) if direct else (1, 3, 4)
+                for i in ends if near else (0, *ends):
+                    wait_bytes(far.at[0], r.send.at[base + i])
 
         owed[id(far), l] = wait
         sent.append((drain, drain))
+
+    def pass_on(l, family):
+        if (id(family[2]), l) in relays:
+            relays.pop((id(family[2]), l))()
 
     def owe_small(l):
         copy = pair_send(r.small.at[l], r.pair_small)
@@ -704,8 +721,11 @@
         if l == 1:
             forward_shard(0, 0)
             forward_shard(0, 1)
+        if l == 0:
+            pass_on(1, fam_c)
+            pass_on(1, fam_qk)
         add_pair(l, fam_p, pair_p)
-        spread(l, fam_p)
+        spread(l, fam_p, False)
         after_part, gain_mlp, shift_mlp = norm_back(r.after[l], r.gains[l, 1:2], finish())
         after_grad = own_grad + after_part
         r.tmp[...] = after_grad
@@ -717,9 +737,10 @@
         r.small[l, 5:6, :] = jnp.sum(own_grad, axis=0, keepdims=True)
         add_pair(l, fam_c, pair_c)
         if l == 0:
-            spread(l, fam_c)
-        arrive(shared, 2)
-        pump(2)
+            spread(l, fam_c, False)
+            pass_on(1, fam_vo)
+            pass_on(1, fam_q)
+        arrive(shared)
         after_low = r.low2[l]
         mixed_grad = dot_nt(after_low, r.w_out[l]).astype(BF16)
         queries, key_heads, values = r.qkv[l, 0], r.qkv[l, 1], r.qkv[l, 2]
@@ -769,13 +790,13 @@
         key_step = to_parts(lambda peer: r.x2_src.at[l, peer], lambda i: r.x2_dst.at[l, i - 1])
         add_pair(l, fam_qk, pair_qk)
         add_pair(l, fam_vo, pair_vo)
-        arrive(value_step, 2)
+        pass_on(l, fam_p)
+        arrive(value_step)
         r.x1_mid[l] = r.x1_src[l, t] + sum(r.x1_dst[l, i] for i in range(T - 1))
         value_step = to_segs(lambda _: r.x1_mid.at[l], lambda i: r.x1_far.at[l, i - 1])
         arrive(key_step)
         r.x2_mid[l] = r.x2_src[l, t] + sum(r.x2_dst[l, i] for i in range(T - 1))
         key_step = to_segs(lambda _: r.x2_mid.at[l], lambda i: r.x2_far.at[l, i - 1])
-        pump(1)
         query_grad = feature_map_back(r.qmem[l].astype(F32), dot_nn(dots_grad, r.phik[l])).astype(BF16)
         for u in range(T):
             r.dq_src[l, u] = query_grad[:, u * z.keys_w : (u + 1) * z.keys_w]
@@ -785,13 +806,12 @@
             arrive((12, 0, 0))
             arrive((12, 0, 1))
         r.tmp[...] += dot_nn(query_grad, r.w_keys[l, 0])
-        arrive(value_step, 1)
+        arrive(value_step)
         direct = r.x1_mid[l] + sum(r.x1_far[l, i] for i in range(S - 1))
         arrive(key_step)
         small_key = small_parts(l, small_key)
         for family in (fam_c, fam_qk, fam_vo) if l == 1 else (fam_qk, fam_vo):
-            spread(l, family)
-        pump(4)
+            spread(l, family, False)
         key_dots = r.kdots[l]
         key_den = 1.0 + jnp.sum(key_dots, axis=1, keepdims=True)
         r.vgrad[...] = direct
@@ -834,7 +854,6 @@
         for u in range(T):
             r.x4_src[l, u] = key_solve[:, u * z.keys_w : (u + 1) * z.keys_w]
         solve_step = to_parts(lambda peer: r.x4_src.at[l, peer], lambda i: r.x4_dst.at[l, i - 1])
-        pump(2)
 
         @pl.when(t == T - 1)
         def _():
@@ -848,7 +867,6 @@
         target[own, :] = r.tmp[...].astype(BF16)
         rows_step = to_parts(lambda _: target.at[own], lambda i: target.at[own])
         small_key = small_segs(l, small_key)
-        pump(4)
         arrive(query_step)
         if l == 1:
             arrive(row_step)
@@ -869,9 +887,12 @@
         sent.extend((copy, c != l) for copy in mem_copies)
         mem_key = owe_owner(l, mem_copies)
         add_pair(l, fam_q, pair_q)
-        spread(l, fam_q)
+        spread(l, fam_q, False)
         if l == 0:
-            pump(100)
+            pass_on(l, fam_c)
+            pass_on(l, fam_qk)
+            pass_on(l, fam_vo)
+            pass_on(l, fam_q)
         arrive(rows_step)
         return mem_key, small_key
 
@@ -916,7 +937,7 @@
     r.fcb_grads[...] = total[8:9, : z.units]
     r.abias_grads[0] = total[9:11, : z.heads_w]
 
-    assert not owed
+    assert not owed and not relays
     for copy, when in sent:
         if when is copy:
             copy()

time: 208 us -> 197 us (0.947)
  Pallas kernels: 207 us -> 196 us
    pallas_call x1, Pallas kernels: 203 us -> 193 us  [per_device(): pl.pallas_call(functools.partial(kernel, z, names), out_shape=shapes, in_...]
where the time goes in v4:
time: 197 us
  Pallas kernels  196 us (99%)
    pallas_call x1, Pallas kernels, per_device(): pl.pallas_call(functools.partial(kernel, z, names), out_shape=shapes, in_...  193 us

profile of v4, /device:TPU:0, one launch (start us, length us, event | category | flops | bytes accessed | tf_op | source)
XLA Modules:
  0.0 196.9 jit_solution(7628677546922024745)
XLA Ops:
  0.6 192.8 %two_layers.1 = (bf16[1,256,768]{2,1,0:T(8,128)(2,1)}, f32[1,2,768]{2,1,0:T(2,128)}, f32[1,2,768]{2,1,0:T(2,128)}, f32[1,3,192,192]{3,2,1,0:T(8,128)}, f32[1,2,1...) custom-call(bf16[2,256,768]{2,1,0:T(8,128)(2,1)} %refs_0_.1, ...), custom_call_target="tpu_custom_call" | custom-call | tf_op jit(solution)/shard_map/two_layers/pallas_call | solution.py:1230
  193.4 3.3 %hand_out.1 = (bf16[1,256,768]{2,1,0:T(8,128)(2,1)}, f32[1,2,768]{2,1,0:T(2,128)}, f32[1,2,768]{2,1,0:T(2,128)}, f32[1,3,192,192]{3,2,1,0:T(8,128)}, f32[1,2,192...) custom-call(bf16[1,256,768]{2,1,0:T(8,128)(2,1)} %get-tuple-element., ...), custom_call_target="tpu_custom_call" | custom-call | tf_op jit(solution)/shard_map/hand_out/pallas_call | solution.py:1241

commit v5 on v4

--- a/solution.py
+++ b/solution.py
@@ -98,6 +98,13 @@
 def split(values):
     high = values.astype(BF16)
     return high, (values - high.astype(F32)).astype(BF16)
+
+
+def plus(first, others, count):
+    total = first.astype(F32)
+    for i in range(count):
+        total = total + others[i].astype(F32)
+    return total
 
 
 class Sizes:
@@ -134,8 +141,8 @@
         probs=fl(2, z.heads, R, R), mixed=bf(2, R, z.heads_w), after=fl(2, C, D), normed_mlp=bf(2, R, D),
         slope=fl(2, R, z.units), act=bf(2, R, z.units), rs_src=bf(7, R, D), rs_own=fl(R, D), q_src=bf(R, z.keys_w), q_parts=bf(T, C, z.keys_w), k_parts=bf(T, M, z.keys_w), rs_dst=bf(7, T - 1, C, D),
         low2=bf(2, R, D), dpre=bf(R, z.units), dqkv=bf(3, R, z.heads_w),
-        x1_src=fl(2, T, M, z.val_w), x1_dst=fl(2, T - 1, M, z.val_w), x1_mid=fl(2, M, z.val_w), x1_far=fl(2, max(S - 1, 1), M, z.val_w),
-        x2_src=fl(2, T, M, z.keys_w), x2_dst=fl(2, T - 1, M, z.keys_w), x2_mid=fl(2, M, z.keys_w), x2_far=fl(2, max(S - 1, 1), M, z.keys_w), x4_src=fl(2, T, M, z.keys_w), x4_dst=fl(2, T - 1, M, z.keys_w), ksolve=fl(M, z.keys), dk_direct=fl(M, z.keys_w),
+        x1_src=bf(2, T, M, z.val_w), x1_dst=bf(2, T - 1, M, z.val_w), x1_mid=bf(2, M, z.val_w), x1_far=bf(2, max(S - 1, 1), M, z.val_w),
+        x2_src=bf(2, T, M, z.keys_w), x2_dst=bf(2, T - 1, M, z.keys_w), x2_mid=bf(2, M, z.keys_w), x2_far=bf(2, max(S - 1, 1), M, z.keys_w), x4_src=bf(2, T, M, z.keys_w), x4_dst=bf(2, T - 1, M, z.keys_w), ksolve=fl(M, z.keys), dk_direct=fl(M, z.keys_w),
         dq_src=bf(2, T, C, z.keys_w), dq_all=bf(2, R, z.keys_w), dv=bf(M, z.val_w), vgrad=fl(M, z.val_w),
         x3_src=bf(2, MEM, D), x3_dst=bf(2, T - 1, MEM, D), final=bf(R, D), tmp=fl(C, D),
         grad_p=bf(2, S, z.cut_pad, z.units), grad_c=bf(2, S, z.cut_pad, z.units), grad_qk=bf(2, S, z.cut_pad, 2 * z.heads_w),
@@ -144,7 +151,7 @@
         far_p=bf(S, z.cut_pad, z.units), far_c=bf(S, z.cut_pad, z.units), far_qk=bf(S, z.cut_pad, 2 * z.heads_w),
         far_vo=bf(S, z.cut_pad, 2 * z.heads_w), far_q=bf(S, z.cut_pad, z.keys_w), dqk=bf(R, 2 * z.heads_w),
         mem_k=fl(2, D, z.keys_w), mem_v=fl(2, D, z.val_w), pair_k=fl(z.cut, z.keys_w), pair_v=fl(z.cut, z.val_w),
-        small=fl(2, 16, D), pair_small=fl(16, D), part_small=fl(T, 8, D), seg_small=fl(S, 16, D),
+        small=fl(2, 16, D), pair_small=fl(16, D), part_small=fl(T, 8, D), sum_small=fl(16, D), seg_small=bf(S, 16, D),
         send=pltpu.SemaphoreType.DMA((z.sems,)), recv=pltpu.SemaphoreType.DMA((z.sems,)), load=pltpu.SemaphoreType.DMA((14, 2)),
         shard=pltpu.SemaphoreType.DMA((2, 2, T)),
     )
@@ -681,8 +688,8 @@
 
         @pl.when(c == l)
         def _():
-            r.seg_small[0] = r.small[l] + r.pair_small[...]
-            r.part_small[0] = r.seg_small[0, 0:8, :]
+            r.sum_small[...] = r.small[l] + r.pair_small[...]
+            r.part_small[0] = r.sum_small[0:8, :]
 
         base = alloc(T - 1)
         return owner_copies(
@@ -697,7 +704,8 @@
             total = r.part_small[0]
             for i in range(1, T):
                 total = total + r.part_small[i]
-            r.seg_small[0, 0:8, :] = total
+            r.sum_small[0:8, :] = total
+            r.seg_small[0] = r.sum_small[...].astype(BF16)
 
         base = alloc(S - 1)
         return owner_copies(
@@ -780,22 +788,25 @@
         lows = [low[:, u * z.val_w : (u + 1) * z.val_w] for u in range(T)]
         dots_high, dots_low = split(r.qdots[l])
         for u in range(T):
-            r.x1_src[l, u] = dot_tn(dots_high, highs[u]) + dot_tn(dots_high, lows[u]) + dot_tn(dots_low, highs[u])
+            grad = dot_tn(dots_high, highs[u]) + dot_tn(dots_high, lows[u]) + dot_tn(dots_low, highs[u])
+            r.x1_src[l, u] = grad.astype(BF16)
         value_step = to_parts(lambda peer: r.x1_src.at[l, peer], lambda i: r.x1_dst.at[l, i - 1])
         dots_grad = sum(dot_nt(highs[u], r.uall[l, u]) + dot_nt(lows[u], r.uall[l, u]) for u in range(T)) + den_grad
         dots_grad = (dots_grad * row_mask).astype(BF16)
         key_direct = feature_map_back(r.keyb[l].astype(F32), dot_tn(dots_grad, r.phiq[l]))
         for u in range(T):
-            r.x2_src[l, u] = key_direct[:, u * z.keys_w : (u + 1) * z.keys_w]
+            r.x2_src[l, u] = key_direct[:, u * z.keys_w : (u + 1) * z.keys_w].astype(BF16)
         key_step = to_parts(lambda peer: r.x2_src.at[l, peer], lambda i: r.x2_dst.at[l, i - 1])
         add_pair(l, fam_qk, pair_qk)
         add_pair(l, fam_vo, pair_vo)
         pass_on(l, fam_p)
         arrive(value_step)
-        r.x1_mid[l] = r.x1_src[l, t] + sum(r.x1_dst[l, i] for i in range(T - 1))
+        value_part = plus(r.x1_src[l, t], r.x1_dst.at[l], T - 1)
+        r.x1_mid[l] = value_part.astype(BF16)
         value_step = to_segs(lambda _: r.x1_mid.at[l], lambda i: r.x1_far.at[l, i - 1])
         arrive(key_step)
-        r.x2_mid[l] = r.x2_src[l, t] + sum(r.x2_dst[l, i] for i in range(T - 1))
+        key_part = plus(r.x2_src[l, t], r.x2_dst.at[l], T - 1)
+        r.x2_mid[l] = key_part.astype(BF16)
         key_step = to_segs(lambda _: r.x2_mid.at[l], lambda i: r.x2_far.at[l, i - 1])
         query_grad = feature_map_back(r.qmem[l].astype(F32), dot_nn(dots_grad, r.phik[l])).astype(BF16)
         for u in range(T):
@@ -807,7 +818,7 @@
             arrive((12, 0, 1))
         r.tmp[...] += dot_nn(query_grad, r.w_keys[l, 0])
         arrive(value_step)
-        direct = r.x1_mid[l] + sum(r.x1_far[l, i] for i in range(S - 1))
+        direct = plus(value_part, r.x1_far.at[l], S - 1)
         arrive(key_step)
         small_key = small_parts(l, small_key)
         for family in (fam_c, fam_qk, fam_vo) if l == 1 else (fam_qk, fam_vo):
@@ -828,7 +839,7 @@
         key_solve = feature_map_back(r.keyb[l].astype(F32), dot_nn(both, r.phik[l]))
         r.ksolve[...] = key_solve
         r.dv[...] = value_grad.astype(BF16)
-        r.dk_direct[...] = r.x2_mid[l] + sum(r.x2_far[l, i] for i in range(S - 1))
+        r.dk_direct[...] = plus(key_part, r.x2_far.at[l], S - 1)
         tail = dot_nn(r.dv[seg_rows, :], r.w_value[l])
         tail = tail + dot_nn(r.dk_direct[seg_rows, :].astype(BF16), r.w_keys[l, 1, shard_rows(t), :])
         tail = tail + dot_nn(r.ksolve[seg_rows, :].astype(BF16), r.w_keys[l, 1])
@@ -852,7 +863,7 @@
 
         sent.append((drain, drain))
         for u in range(T):
-            r.x4_src[l, u] = key_solve[:, u * z.keys_w : (u + 1) * z.keys_w]
+            r.x4_src[l, u] = key_solve[:, u * z.keys_w : (u + 1) * z.keys_w].astype(BF16)
         solve_step = to_parts(lambda peer: r.x4_src.at[l, peer], lambda i: r.x4_dst.at[l, i - 1])
 
         @pl.when(t == T - 1)
@@ -874,7 +885,7 @@
         pair_q = hand_over(l, fam_q)
         r.mem_v[l] = dot_tn(r.mem_rows[l], r.dv[...])
         arrive(solve_step)
-        key_grad = r.dk_direct[...] + r.x4_src[l, t] + sum(r.x4_dst[l, i] for i in range(T - 1))
+        key_grad = plus(r.dk_direct[...] + r.x4_src[l, t].astype(F32), r.x4_dst.at[l], T - 1)
         r.mem_k[l] = dot_tn(r.mem_rows[l], key_grad.astype(BF16))
         rows = pl.ds(pl.multiple_of(s * z.cut, 8), z.cut)
         mem_copies = [pair_send(r.mem_k.at[l, rows], r.pair_k), pair_send(r.mem_v.at[l, rows], r.pair_v)]
@@ -928,9 +939,9 @@
     r.mkey_grads[0, 0] = far_sum(r.far_q)
     arrive(small_key1)
     arrive(small_key0)
-    total = r.seg_small[0]
+    total = r.sum_small[...]
     for i in range(1, S):
-        total = total + r.seg_small[i]
+        total = total + r.seg_small[i].astype(F32)
     r.gain_grads[0] = total[0:2]
     r.shift_grads[0] = total[2:4]
     r.obias_grads[0] = total[4:6]

time: 197 us -> 188 us (0.954)
  Pallas kernels: 196 us -> 187 us
    pallas_call x1, Pallas kernels: 193 us -> 184 us  [per_device(): pl.pallas_call(functools.partial(kernel, z, names), out_shape=shapes, in_...]
where the time goes in v5:
time: 188 us
  Pallas kernels  187 us (99%)
    pallas_call x1, Pallas kernels, per_device(): pl.pallas_call(functools.partial(kernel, z, names), out_shape=shapes, in_...  184 us

profile of v5, /device:TPU:0, one launch (start us, length us, event | category | flops | bytes accessed | tf_op | source)
XLA Modules:
  0.0 188.1 jit_solution(5965025793106412363)
XLA Ops:
  0.6 184.0 %two_layers.1 = (bf16[1,256,768]{2,1,0:T(8,128)(2,1)}, f32[1,2,768]{2,1,0:T(2,128)}, f32[1,2,768]{2,1,0:T(2,128)}, f32[1,3,192,192]{3,2,1,0:T(8,128)}, f32[1,2,1...) custom-call(bf16[2,256,768]{2,1,0:T(8,128)(2,1)} %refs_0_.1, ...), custom_call_target="tpu_custom_call" | custom-call | tf_op jit(solution)/shard_map/two_layers/pallas_call | solution.py:1241
  184.6 3.3 %hand_out.1 = (bf16[1,256,768]{2,1,0:T(8,128)(2,1)}, f32[1,2,768]{2,1,0:T(2,128)}, f32[1,2,768]{2,1,0:T(2,128)}, f32[1,3,192,192]{3,2,1,0:T(8,128)}, f32[1,2,192...) custom-call(bf16[1,256,768]{2,1,0:T(8,128)(2,1)} %get-tuple-element., ...), custom_call_target="tpu_custom_call" | custom-call | tf_op jit(solution)/shard_map/hand_out/pallas_call | solution.py:1252

commit v6 on v5

--- a/solution.py
+++ b/solution.py
@@ -348,6 +348,7 @@
     pair_base = alloc(len(loads))
     load_other(early)
 
+    spread_shard(1, 1)
     row_seg = lax.broadcasted_iota(jnp.int32, (M, 1), 0) // MEM
     col_seg = lax.broadcasted_iota(jnp.int32, (1, M), 1) // MEM
     row_item, col_item, own_item = jnp.zeros((M, 1), jnp.int32), jnp.zeros((1, M), jnp.int32), 0
@@ -439,9 +440,7 @@
         r.uall[l, t] = r.upart[l].astype(BF16)
         solved = to_parts(lambda _: r.uall.at[l, t], lambda i: r.uall.at[l, t])
         if l == 0:
-            spread_shard(1, 1)
-        else:
-            spread_shard(0, 0)
+            spread_shard(1, 0)
         query_dots = dot_nt(phi_query, phi_key) * row_mask
         r.qdots[l] = query_dots
         query_den = 1.0 + jnp.sum(query_dots, axis=1, keepdims=True)
@@ -462,10 +461,6 @@
         wait_load(r.w_attn, l)
         wait_load(r.w_out, l)
         arrive(shared)
-        if l == 0:
-            spread_shard(1, 0)
-        else:
-            spread_shard(0, 1)
         normed = r.normed[l]
         queries = (dot_nt(normed, r.w_attn[l, 0]) + r.attn_bias[l, 0:1]).astype(BF16)
         key_heads = dot_nt(normed, r.w_attn[l, 1]).astype(BF16)
@@ -499,7 +494,6 @@
             forward_shard(1, 1)
             forward_shard(1, 0)
         arrive(shared)
-        row_step = share_rows(r.xfull, 1) if l == 1 else None
         pre = dot_nn(r.normed_mlp[l], r.w_fc[l]) + r.fc_bias[l]
         activation, slope = gelu_and_slope(pre)
         activation = activation.astype(BF16)
@@ -541,7 +535,6 @@
                             wait_bytes(last, r.send.at[places + i * T + j])
 
             sent.append((drain, drain))
-        return row_step
 
     fam_p, fam_c = (r.grad_p, r.pair_f, r.far_p, 0, r.relay_f), (r.grad_c, r.pair_f, r.far_c, 1, r.relay_f)
     fam_qk, fam_vo = (r.grad_qk, r.pair_a, r.far_qk, 0, r.relay_a), (r.grad_vo, r.pair_a, r.far_vo, 1, r.relay_a)
@@ -726,9 +719,6 @@
         weight_grad(l, fam_c, (r.normed_mlp.at[l], r.dpre[...]))
         pair_c = hand_over(l, fam_c)
         r.small[l, 8:9, :] = jnp.sum(r.dpre[...].astype(F32), axis=0, keepdims=True)
-        if l == 1:
-            forward_shard(0, 0)
-            forward_shard(0, 1)
         if l == 0:
             pass_on(1, fam_c)
             pass_on(1, fam_qk)
@@ -749,6 +739,9 @@
             pass_on(1, fam_vo)
             pass_on(1, fam_q)
         arrive(shared)
+        if l == 0:
+            forward_shard(0, 0)
+            forward_shard(0, 1)
         after_low = r.low2[l]
         mixed_grad = dot_nt(after_low, r.w_out[l]).astype(BF16)
         queries, key_heads, values = r.qkv[l, 0], r.qkv[l, 1], r.qkv[l, 2]
@@ -797,6 +790,8 @@
         for u in range(T):
             r.x2_src[l, u] = key_direct[:, u * z.keys_w : (u + 1) * z.keys_w].astype(BF16)
         key_step = to_parts(lambda peer: r.x2_src.at[l, peer], lambda i: r.x2_dst.at[l, i - 1])
+        if l == 1:
+            row_step = share_rows(r.xfull, 1)
         add_pair(l, fam_qk, pair_qk)
         add_pair(l, fam_vo, pair_vo)
         pass_on(l, fam_p)
@@ -808,6 +803,8 @@
         key_part = plus(r.x2_src[l, t], r.x2_dst.at[l], T - 1)
         r.x2_mid[l] = key_part.astype(BF16)
         key_step = to_segs(lambda _: r.x2_mid.at[l], lambda i: r.x2_far.at[l, i - 1])
+        for family in (fam_c, fam_qk, fam_vo) if l == 1 else (fam_qk, fam_vo):
+            spread(l, family, False)
         query_grad = feature_map_back(r.qmem[l].astype(F32), dot_nn(dots_grad, r.phik[l])).astype(BF16)
         for u in range(T):
             r.dq_src[l, u] = query_grad[:, u * z.keys_w : (u + 1) * z.keys_w]
@@ -817,12 +814,17 @@
             arrive((12, 0, 0))
             arrive((12, 0, 1))
         r.tmp[...] += dot_nn(query_grad, r.w_keys[l, 0])
+        target = r.gfull.at[0] if l == 1 else r.final
+        first = pl.ds(pl.multiple_of(t * C, 16), C - MEM)
+        rest = pl.ds(pl.multiple_of(t * C + C - MEM, 16), MEM)
+        target[first, :] = r.tmp[: C - MEM, :].astype(BF16)
+        first_step = to_parts(lambda _: target.at[first], lambda i: target.at[first])
+        if l == 1:
+            spread_shard(0, 0)
         arrive(value_step)
         direct = plus(value_part, r.x1_far.at[l], S - 1)
         arrive(key_step)
         small_key = small_parts(l, small_key)
-        for family in (fam_c, fam_qk, fam_vo) if l == 1 else (fam_qk, fam_vo):
-            spread(l, family, False)
         key_dots = r.kdots[l]
         key_den = 1.0 + jnp.sum(key_dots, axis=1, keepdims=True)
         r.vgrad[...] = direct
@@ -874,10 +876,11 @@
                 total = total + r.x3_dst[l, i].astype(F32)
             r.tmp[C - MEM :, :] += total
 
-        target = r.gfull.at[0] if l == 1 else r.final
-        target[own, :] = r.tmp[...].astype(BF16)
-        rows_step = to_parts(lambda _: target.at[own], lambda i: target.at[own])
+        target[rest, :] = r.tmp[C - MEM :, :].astype(BF16)
+        rest_step = to_parts(lambda _: target.at[rest], lambda i: target.at[rest])
         small_key = small_segs(l, small_key)
+        if l == 1:
+            spread_shard(0, 1)
         arrive(query_step)
         if l == 1:
             arrive(row_step)
@@ -904,11 +907,12 @@
             pass_on(l, fam_qk)
             pass_on(l, fam_vo)
             pass_on(l, fam_q)
-        arrive(rows_step)
+        arrive(first_step)
+        arrive(rest_step)
         return mem_key, small_key
 
     forward(0)
-    row_step = forward(1)
+    forward(1)
     for l in range(LAYERS):
         r.small[l] = jnp.zeros((16, D), F32)
     mem_key1, small_key1 = backward(1)

time: 188 us -> 183 us (0.973)
  Pallas kernels: 187 us -> 182 us
    pallas_call x1, Pallas kernels: 184 us -> 179 us  [per_device(): pl.pallas_call(functools.partial(kernel, z, names), out_shape=shapes, in_...]
where the time goes in v6:
time: 183 us
  Pallas kernels  182 us (99%)
    pallas_call x1, Pallas kernels, per_device(): pl.pallas_call(functools.partial(kernel, z, names), out_shape=shapes, in_...  179 us

profile of v6, /device:TPU:0, one launch (start us, length us, event | category | flops | bytes accessed | tf_op | source)
XLA Modules:
  0.0 182.7 jit_solution(8997685727500498517)
XLA Ops:
  0.6 178.6 %two_layers.1 = (bf16[1,256,768]{2,1,0:T(8,128)(2,1)}, f32[1,2,768]{2,1,0:T(2,128)}, f32[1,2,768]{2,1,0:T(2,128)}, f32[1,3,192,192]{3,2,1,0:T(8,128)}, f32[1,2,1...) custom-call(bf16[2,256,768]{2,1,0:T(8,128)(2,1)} %refs_0_.1, ...), custom_call_target="tpu_custom_call" | custom-call | tf_op jit(solution)/shard_map/two_layers/pallas_call | solution.py:1245
  179.3 3.3 %hand_out.1 = (bf16[1,256,768]{2,1,0:T(8,128)(2,1)}, f32[1,2,768]{2,1,0:T(2,128)}, f32[1,2,768]{2,1,0:T(2,128)}, f32[1,3,192,192]{3,2,1,0:T(8,128)}, f32[1,2,192...) custom-call(bf16[1,256,768]{2,1,0:T(8,128)(2,1)} %get-tuple-element., ...), custom_call_target="tpu_custom_call" | custom-call | tf_op jit(solution)/shard_map/hand_out/pallas_call | solution.py:1256

commit v7 on v6

--- a/solution.py
+++ b/solution.py
@@ -734,8 +734,8 @@
         r.small[l, 4:5, :] = jnp.sum(after_grad, axis=0, keepdims=True)
         r.small[l, 5:6, :] = jnp.sum(own_grad, axis=0, keepdims=True)
         add_pair(l, fam_c, pair_c)
+        spread(l, fam_c, False)
         if l == 0:
-            spread(l, fam_c, False)
             pass_on(1, fam_vo)
             pass_on(1, fam_q)
         arrive(shared)
@@ -768,6 +768,7 @@
         pair_vo = hand_over(l, fam_vo)
         for row, i in ((9, 0), (10, 2)):
             r.small[l, row : row + 1, : z.heads_w] = jnp.sum(r.dqkv[i].astype(F32), axis=0, keepdims=True)
+        pass_on(l, fam_p)
         hidden_part, gain_attn, shift_attn = norm_back(r.hidden[l], r.gains[l, 0:1], finish())
         hidden_grad = r.tmp[...] + hidden_part
         r.tmp[...] = hidden_grad
@@ -794,7 +795,6 @@
             row_step = share_rows(r.xfull, 1)
         add_pair(l, fam_qk, pair_qk)
         add_pair(l, fam_vo, pair_vo)
-        pass_on(l, fam_p)
         arrive(value_step)
         value_part = plus(r.x1_src[l, t], r.x1_dst.at[l], T - 1)
         r.x1_mid[l] = value_part.astype(BF16)
@@ -803,7 +803,7 @@
         key_part = plus(r.x2_src[l, t], r.x2_dst.at[l], T - 1)
         r.x2_mid[l] = key_part.astype(BF16)
         key_step = to_segs(lambda _: r.x2_mid.at[l], lambda i: r.x2_far.at[l, i - 1])
-        for family in (fam_c, fam_qk, fam_vo) if l == 1 else (fam_qk, fam_vo):
+        for family in (fam_qk, fam_vo):
             spread(l, family, False)
         query_grad = feature_map_back(r.qmem[l].astype(F32), dot_nn(dots_grad, r.phik[l])).astype(BF16)
         for u in range(T):
@@ -821,6 +821,8 @@
         first_step = to_parts(lambda _: target.at[first], lambda i: target.at[first])
         if l == 1:
             spread_shard(0, 0)
+        if l == 1:
+            pass_on(l, fam_c)
         arrive(value_step)
         direct = plus(value_part, r.x1_far.at[l], S - 1)
         arrive(key_step)

time: 183 us -> 181 us (0.989)
  no operation moved by 1% of the time
where the time goes in v7:
time: 181 us
  Pallas kernels  181 us (100%)
    pallas_call x1, Pallas kernels, per_device(): pl.pallas_call(functools.partial(kernel, z, names), out_shape=shapes, in_...  177 us

profile of v7, /device:TPU:0, one launch (start us, length us, event | category | flops | bytes accessed | tf_op | source)
XLA Modules:
  0.0 181.3 jit_solution(17396110790885992457)
XLA Ops:
  0.6 177.2 %two_layers.1 = (bf16[1,256,768]{2,1,0:T(8,128)(2,1)}, f32[1,2,768]{2,1,0:T(2,128)}, f32[1,2,768]{2,1,0:T(2,128)}, f32[1,3,192,192]{3,2,1,0:T(8,128)}, f32[1,2,1...) custom-call(bf16[2,256,768]{2,1,0:T(8,128)(2,1)} %refs_0_.1, ...), custom_call_target="tpu_custom_call" | custom-call | tf_op jit(solution)/shard_map/two_layers/pallas_call | solution.py:1247
  177.8 3.3 %hand_out.1 = (bf16[1,256,768]{2,1,0:T(8,128)(2,1)}, f32[1,2,768]{2,1,0:T(2,128)}, f32[1,2,768]{2,1,0:T(2,128)}, f32[1,3,192,192]{3,2,1,0:T(8,128)}, f32[1,2,192...) custom-call(bf16[1,256,768]{2,1,0:T(8,128)(2,1)} %get-tuple-element., ...), custom_call_target="tpu_custom_call" | custom-call | tf_op jit(solution)/shard_map/hand_out/pallas_call | solution.py:1258

commit v8 on v7

--- a/solution.py
+++ b/solution.py
@@ -141,8 +141,8 @@
         probs=fl(2, z.heads, R, R), mixed=bf(2, R, z.heads_w), after=fl(2, C, D), normed_mlp=bf(2, R, D),
         slope=fl(2, R, z.units), act=bf(2, R, z.units), rs_src=bf(7, R, D), rs_own=fl(R, D), q_src=bf(R, z.keys_w), q_parts=bf(T, C, z.keys_w), k_parts=bf(T, M, z.keys_w), rs_dst=bf(7, T - 1, C, D),
         low2=bf(2, R, D), dpre=bf(R, z.units), dqkv=bf(3, R, z.heads_w),
-        x1_src=bf(2, T, M, z.val_w), x1_dst=bf(2, T - 1, M, z.val_w), x1_mid=bf(2, M, z.val_w), x1_far=bf(2, max(S - 1, 1), M, z.val_w),
-        x2_src=bf(2, T, M, z.keys_w), x2_dst=bf(2, T - 1, M, z.keys_w), x2_mid=bf(2, M, z.keys_w), x2_far=bf(2, max(S - 1, 1), M, z.keys_w), x4_src=bf(2, T, M, z.keys_w), x4_dst=bf(2, T - 1, M, z.keys_w), ksolve=fl(M, z.keys), dk_direct=fl(M, z.keys_w),
+        x1_src=bf(2, T, M - MEM, z.val_w), x1_dst=bf(2, T - 1, M - MEM, z.val_w), x1_mid=bf(2, M - MEM, z.val_w), x1_far=bf(2, max(S - 1, 1), M - MEM, z.val_w),
+        x2_src=bf(2, T, M - MEM, z.keys_w), x2_dst=bf(2, T - 1, M - MEM, z.keys_w), x2_mid=bf(2, M - MEM, z.keys_w), x2_far=bf(2, max(S - 1, 1), M - MEM, z.keys_w), x4_src=bf(2, T, M, z.keys_w), x4_dst=bf(2, T - 1, M, z.keys_w), ksolve=fl(M, z.keys), dk_direct=fl(M, z.keys_w),
         dq_src=bf(2, T, C, z.keys_w), dq_all=bf(2, R, z.keys_w), dv=bf(M, z.val_w), vgrad=fl(M, z.val_w),
         x3_src=bf(2, MEM, D), x3_dst=bf(2, T - 1, MEM, D), final=bf(R, D), tmp=fl(C, D),
         grad_p=bf(2, S, z.cut_pad, z.units), grad_c=bf(2, S, z.cut_pad, z.units), grad_qk=bf(2, S, z.cut_pad, 2 * z.heads_w),
@@ -783,13 +783,13 @@
         dots_high, dots_low = split(r.qdots[l])
         for u in range(T):
             grad = dot_tn(dots_high, highs[u]) + dot_tn(dots_high, lows[u]) + dot_tn(dots_low, highs[u])
-            r.x1_src[l, u] = grad.astype(BF16)
+            r.x1_src[l, u] = grad[: M - MEM].astype(BF16)
         value_step = to_parts(lambda peer: r.x1_src.at[l, peer], lambda i: r.x1_dst.at[l, i - 1])
         dots_grad = sum(dot_nt(highs[u], r.uall[l, u]) + dot_nt(lows[u], r.uall[l, u]) for u in range(T)) + den_grad
         dots_grad = (dots_grad * row_mask).astype(BF16)
         key_direct = feature_map_back(r.keyb[l].astype(F32), dot_tn(dots_grad, r.phiq[l]))
         for u in range(T):
-            r.x2_src[l, u] = key_direct[:, u * z.keys_w : (u + 1) * z.keys_w].astype(BF16)
+            r.x2_src[l, u] = key_direct[: M - MEM, u * z.keys_w : (u + 1) * z.keys_w].astype(BF16)
         key_step = to_parts(lambda peer: r.x2_src.at[l, peer], lambda i: r.x2_dst.at[l, i - 1])
         if l == 1:
             row_step = share_rows(r.xfull, 1)
@@ -824,7 +824,7 @@
         if l == 1:
             pass_on(l, fam_c)
         arrive(value_step)
-        direct = plus(value_part, r.x1_far.at[l], S - 1)
+        direct = jnp.concatenate([plus(value_part, r.x1_far.at[l], S - 1), jnp.zeros((MEM, z.val_w), F32)], axis=0)
         arrive(key_step)
         small_key = small_parts(l, small_key)
         key_dots = r.kdots[l]
@@ -843,7 +843,8 @@
         key_solve = feature_map_back(r.keyb[l].astype(F32), dot_nn(both, r.phik[l]))
         r.ksolve[...] = key_solve
         r.dv[...] = value_grad.astype(BF16)
-        r.dk_direct[...] = plus(key_part, r.x2_far.at[l], S - 1)
+        r.dk_direct[: M - MEM, :] = plus(key_part, r.x2_far.at[l], S - 1)
+        r.dk_direct[M - MEM :, :] = jnp.zeros((MEM, z.keys_w), F32)
         tail = dot_nn(r.dv[seg_rows, :], r.w_value[l])
         tail = tail + dot_nn(r.dk_direct[seg_rows, :].astype(BF16), r.w_keys[l, 1, shard_rows(t), :])
         tail = tail + dot_nn(r.ksolve[seg_rows, :].astype(BF16), r.w_keys[l, 1])

time: 181 us -> 180 us (level)
  Pallas kernels: 181 us -> 179 us
    pallas_call x1, Pallas kernels: 177 us -> 175 us  [per_device(): pl.pallas_call(functools.partial(kernel, z, names), out_shape=shapes, in_...]
where the time goes in v8:
time: 180 us; the launch traced here: 179 us
  Pallas kernels  179 us (99%)
    pallas_call x1, Pallas kernels, per_device(): pl.pallas_call(functools.partial(kernel, z, names), out_shape=shapes, in_...  175 us

profile of v8, /device:TPU:0, one launch (start us, length us, event | category | flops | bytes accessed | tf_op | source)
XLA Modules:
  0.0 179.4 jit_solution(11217072421350536311)
XLA Ops:
  0.6 175.3 %two_layers.1 = (bf16[1,256,768]{2,1,0:T(8,128)(2,1)}, f32[1,2,768]{2,1,0:T(2,128)}, f32[1,2,768]{2,1,0:T(2,128)}, f32[1,3,192,192]{3,2,1,0:T(8,128)}, f32[1,2,1...) custom-call(bf16[2,256,768]{2,1,0:T(8,128)(2,1)} %refs_0_.1, ...), custom_call_target="tpu_custom_call" | custom-call | tf_op jit(solution)/shard_map/two_layers/pallas_call | solution.py:1248
  175.9 3.3 %hand_out.1 = (bf16[1,256,768]{2,1,0:T(8,128)(2,1)}, f32[1,2,768]{2,1,0:T(2,128)}, f32[1,2,768]{2,1,0:T(2,128)}, f32[1,3,192,192]{3,2,1,0:T(8,128)}, f32[1,2,192...) custom-call(bf16[1,256,768]{2,1,0:T(8,128)(2,1)} %get-tuple-element., ...), custom_call_target="tpu_custom_call" | custom-call | tf_op jit(solution)/shard_map/hand_out/pallas_call | solution.py:1259
